TPU v7x, 32 devices: a whole 2x2x4 slice. The times are simulated.
32 devices in a mesh: dp: 16 (over z, x, core), expert: 2 (over y).
Axes of the slice: x: 2, y: 2, z: 4, core: 2. Of those that a mesh axis runs over, the one named last changes fastest.
Arguments:
- grad_out: bfloat16 [4096, 2560], P(('dp', 'expert')), may hold values from -6 to 6
- saved_input: bfloat16 [4096, 2560], P(('dp', 'expert')), may hold values from -6 to 6
- expert_ids: int32 [4096, 2], P(('dp', 'expert')), may hold values from 0 to 3, all different within a row; in each aligned block of 128 rows (0 to 127, 128 to 255, ...) at most 128 rows name the same one
- gate_weights: float32 [4096, 2], P(('dp', 'expert')), may hold values from 0.2 to 1
- up_weight: bfloat16 [4, 2560, 512], P('expert', 'dp'), may hold values from -0.125 to 0.125
- down_weight: bfloat16 [4, 512, 2560], P('expert', 'dp'), may hold values from -0.25 to 0.25
- engram_gate: float32 [4096, 4], P(('dp', 'expert')), may hold values from 0.1 to 1
- memory_owner: int32 [4096, 4], P(('dp', 'expert')), may hold values from 0 to 15, all different within a row; in each aligned block of 128 rows (0 to 127, 128 to 255, ...) at most 64 rows name the same one
- memory_slot: int32 [4096, 4], P(('dp', 'expert')), may hold values from 0 to 127
Outputs:
- grad_input: bfloat16 [4096, 2560], P(('dp', 'expert'))
- table_grad: float32 [4, 2048, 1280], P(None, ('dp', 'expert'))
Inputs may be any that keep to these rules, and one draw needn't show every extreme that they name: `expert_ids`: each row names 2 different experts; among the rows of one device (aligned blocks of 128 rows) no expert is named more than 128 times, a bound that some block reaches. `memory_owner`: each row names 4 different owners; among the rows of one device (aligned blocks of 128 rows) no owner is named more than 64 times, a bound that some block reaches.
All inputs are finite; a program needn't handle non-finite values.
Results may differ from a plain program's by a relative error of at most 0.014.
Values may be sent and summed in bfloat16 or wider, within the bound.
No kernel may reach another device: no remote copies, remote signals or barrier semaphores. Data moves between devices by JAX's collectives and lax.ppermute only.
A program may use at most 128 MiB of HBM per device.

v0:
```python
import jax
import jax.numpy as jnp
from jax import lax
from jax.sharding import PartitionSpec as P

TOP = 2
HEADS = 2
SHARD = 128


def silu_slope(pre):
    sig = jax.nn.sigmoid(pre)
    return sig * (1.0 + pre * (1.0 - sig))


def slot_places(targets, groups, capacity):
    flat = targets.reshape(-1)
    onehot = (flat[:, None] == jnp.arange(groups, dtype=jnp.int32)[None, :]).astype(jnp.int32)
    before = jnp.cumsum(onehot, axis=0) - onehot
    place = jnp.sum(before * onehot, axis=1)
    return flat * capacity + place


def memory_path(grad_out, engram_gate, memory_owner, memory_slot):
    tok_rows = grad_out.shape[0]
    lookups = engram_gate.shape[1]
    width = grad_out.shape[1] // 2
    groups = lax.axis_size("dp")
    capacity = 2 * tok_rows * lookups // groups
    halves = grad_out.reshape(tok_rows, 2, width)
    rows = (engram_gate[:, :, None] * jnp.repeat(halves, HEADS, axis=1).astype(jnp.float32)).astype(
        jnp.bfloat16
    )
    places = slot_places(memory_owner, groups, capacity)
    keys = (jnp.arange(lookups, dtype=jnp.int32)[None, :] * SHARD + memory_slot).reshape(-1)
    send_rows = (
        jnp.zeros((groups * capacity, width), jnp.bfloat16).at[places].set(rows.reshape(-1, width))
    )
    send_keys = jnp.zeros((groups * capacity,), jnp.int32).at[places].set(keys)
    got_rows, got_keys = (
        lax.all_to_all(
            send_rows.reshape(groups, capacity, width),
            "dp",
            split_axis=0,
            concat_axis=0,
            tiled=True,
        ),
        lax.all_to_all(
            send_keys.reshape(groups, capacity), "dp", split_axis=0, concat_axis=0, tiled=True
        ),
    )
    dense = (
        jnp.zeros((lookups * SHARD, width), jnp.float32)
        .at[got_keys.reshape(-1)]
        .add(got_rows.reshape(-1, width).astype(jnp.float32))
    )
    return lax.psum_scatter(
        dense.reshape(lookups, SHARD, width).astype(jnp.bfloat16),
        "expert",
        scatter_dimension=1,
        tiled=True,
    ).astype(jnp.float32)


def per_device(
    grad_out,
    saved_input,
    expert_ids,
    gate_weights,
    up_weight,
    down_weight,
    engram_gate,
    memory_owner,
    memory_slot,
):
    tok_rows, width = grad_out.shape
    local_experts = up_weight.shape[0]
    groups = lax.axis_size("expert")
    experts = local_experts * groups
    capacity = 2 * tok_rows * TOP // experts
    places = slot_places(expert_ids, experts, capacity)
    send_grad = (
        jnp.zeros((experts * capacity, width), jnp.bfloat16)
        .at[places]
        .set(jnp.repeat(grad_out, TOP, axis=0))
    )
    send_input = (
        jnp.zeros((experts * capacity, width), jnp.bfloat16)
        .at[places]
        .set(jnp.repeat(saved_input, TOP, axis=0))
    )
    shape = (groups, local_experts, capacity, width)
    got_grad, got_input = (
        lax.all_to_all(send_grad.reshape(shape), "expert", split_axis=0, concat_axis=0, tiled=True),
        lax.all_to_all(
            send_input.reshape(shape), "expert", split_axis=0, concat_axis=0, tiled=True
        ),
    )
    pre = jnp.einsum(
        "secd,edh->sech",
        got_input,
        lax.all_gather(up_weight, "dp", axis=1, tiled=True),
        preferred_element_type=jnp.float32,
    )
    back = jnp.einsum(
        "secd,ehd->sech",
        got_grad,
        lax.all_gather(down_weight, "dp", axis=1, tiled=True),
        preferred_element_type=jnp.float32,
    )
    slope = (back * silu_slope(pre)).astype(jnp.bfloat16)
    expert_grad = jnp.einsum(
        "sech,edh->secd",
        slope,
        lax.all_gather(up_weight, "dp", axis=1, tiled=True),
        preferred_element_type=jnp.float32,
    ).astype(jnp.bfloat16)
    returned = lax.all_to_all(expert_grad, "expert", split_axis=0, concat_axis=0, tiled=True)
    picked = returned.reshape(experts * capacity, width)[places]
    weighted = gate_weights.reshape(-1, 1) * picked.astype(jnp.float32)
    grad_input = jnp.sum(weighted.reshape(tok_rows, TOP, width), axis=1).astype(jnp.bfloat16)
    table_part = memory_path(grad_out, engram_gate, memory_owner, memory_slot)
    return (grad_input, table_part)


def solution(mesh):
    return jax.shard_map(
        per_device,
        mesh=mesh,
        in_specs=(
            P(("dp", "expert"), None),
            P(("dp", "expert"), None),
            P(("dp", "expert"), None),
            P(("dp", "expert"), None),
            P("expert", "dp", None),
            P("expert", "dp", None),
            P(("dp", "expert"), None),
            P(("dp", "expert"), None),
            P(("dp", "expert"), None),
        ),
        out_specs=(P(("dp", "expert"), None), P(None, ("dp", "expert"), None)),
        check_vma=False,
    )
```

profile of v0, /device:TPU:10, one launch (start us, length us, event | category | flops | bytes accessed | tf_op | source)
XLA Modules:
  0.0 270.1 jit_solution(3934675372716309784)
XLA Ops:
  8.0 0.7 all-gather.5.cloned.1.call-update
  8.8 0.7 all-gather.3.cloned.1.call-update
  9.5 0.8 copy.67
  10.5 1.2 reduce-window.16
  11.7 0.2 slice_reduce_fusion
  11.9 0.7 broadcast_multiply_fusion
  12.6 0.1 copy.66
  12.8 0.8 broadcast_add_fusion
  13.6 0.1 copy.70
  13.9 2.4 scatter_custom_fusion.2
  16.4 0.7 all_to_all.21
  17.1 6.2 %all-to-all-start.3 = ((s32[16,1,64]{2,1,0:T(1,128)}), s32[16,1,64]{2,1,0:T(1,128)S(1)}, u32[]{:S(2)}, u32[]{:S(2)}) async-start(s32[16,1,64]{2,1,0:T(1,128)} %all_to_all.21), calls=%async_computation.3 | async-start | bytes 16384 | tf_op jit(solution)/shard_map/all_to_all | solution.py:48
  23.3 0.8 copy.59
  24.1 0.1 eq.54
  24.2 0.1 eq.50
  24.4 1.2 reduce-window.14
  25.9 0.7 broadcast_multiply_fusion.1
  26.6 0.1 copy.58
  26.7 0.1 mul.78
  27.0 1.8 broadcast_in_dim.11
  28.7 0.5 reshape.217
  29.3 4.3 %scatter_custom_fusion.1 = bf16[512,2560]{1,0:T(8,128)(2,1)} fusion(s32[256]{0:T(256)S(1)} %bitcast.93, bf16[256,2560]{1,0:T(8,128)(2,1)S(1)} %reshape.217, bf16[]{:T(256)} %constant.8.clone.1), kind=kCustom, calls=%fused_computation.27 | custom fusion | bytes 2621442 | tf_op jit(solution)/shard_map/scatter | solution.py:90
  33.6 5.3 %all-to-all-start.1 = ((bf16[2,2,128,2560]{3,2,1,0:T(8,128)(2,1)}), bf16[2,2,128,2560]{3,2,1,0:T(8,128)(2,1)}, u32[]{:S(2)}, u32[]{:S(2)}) async-start(bf16[2,2,128,2560]{3,2,1,0:T(8,128)(2,1)} %bitcast.8), calls=%async_computation.1 | async-start | bytes 5242880 | tf_op jit(solution)/shard_map/all_to_all | solution.py:95
  38.9 0.9 reshape.195
  39.8 2.4 broadcast_in_dim.14
  42.1 3.4 %convert_element_type.75 = f32[512,1280]{1,0:T(8,128)S(1)} reshape(f32[128,2,2,1280]{3,2,1,0:T(2,128)} %broadcast_in_dim.14) | data formatting | bytes 5242880 | tf_op jit(solution)/shard_map/convert_element_type | solution.py:31
  45.8 4.7 %scatter_custom_fusion.3 = bf16[1024,1280]{1,0:T(8,128)(2,1)} fusion(s32[512]{0:T(512)S(1)} %bitcast.100, f32[512,1280]{1,0:T(8,128)S(1)} %convert_element_type.75, f32[512]{0:T(512)S(1)} %mul.89, bf16[]{:T(256)} %constant.8.clone.1), kind=kCustom, calls=%fused_computation.23 | custom fusion | flops 1310720 | bytes 5244930 | tf_op jit(solution)/shard_map/scatter | solution.py:37
  50.4 19.4 %all-to-all-done.1 = bf16[2,2,128,2560]{3,2,1,0:T(8,128)(2,1)} async-done(((bf16[2,2,128,2560]{3,2,1,0:T(8,128)(2,1)}), bf16[2,2,128,2560]{3,2,1,0:T(8,128)(2,1)}, u32[]{:S(2)}, u32[]{:S(2)}) %all-to-all-start.1) | async-done | bytes 2621472 | tf_op jit(solution)/shard_map/all_to_all | solution.py:95
  69.8 6.0 %all-to-all-start.4 = ((bf16[16,64,1280]{2,1,0:T(8,128)(2,1)}), bf16[16,64,1280]{2,1,0:T(8,128)(2,1)S(1)}, u32[]{:S(2)}, u32[]{:S(2)}) async-start(bf16[16,64,1280]{2,1,0:T(8,128)(2,1)} %bitcast.90), calls=%async_computation.4 | async-start | bytes 5242880 | tf_op jit(solution)/shard_map/all_to_all | solution.py:41
  75.9 1.7 broadcast_in_dim.10
  77.6 4.1 %reshape.209 = bf16[256,2560]{1,0:T(8,128)(2,1)} reshape(bf16[128,2,2560]{2,1,0:T(2,128)(2,1)} %broadcast_in_dim.10) | data formatting | bytes 2621440 | tf_op jit(solution)/shard_map/reshape | solution.py:85
  81.7 5.1 %scatter_custom_fusion = bf16[512,2560]{1,0:T(8,128)(2,1)} fusion(s32[256]{0:T(256)S(1)} %bitcast.94, bf16[256,2560]{1,0:T(8,128)(2,1)} %reshape.209, bf16[]{:T(256)} %constant.8.clone.1), kind=kCustom, calls=%fused_computation.29 | custom fusion | bytes 2621952 | tf_op jit(solution)/shard_map/scatter | solution.py:85
  86.7 79.2 %all-to-all-done.4 = bf16[16,64,1280]{2,1,0:T(8,128)(2,1)S(1)} async-done(((bf16[16,64,1280]{2,1,0:T(8,128)(2,1)}), bf16[16,64,1280]{2,1,0:T(8,128)(2,1)S(1)}, u32[]{:S(2)}, u32[]{:S(2)}) %all-to-all-start.4) | async-done | bytes 2621472 | tf_op jit(solution)/shard_map/all_to_all | solution.py:41
  165.9 5.2 %all-to-all-start = ((bf16[2,2,128,2560]{3,2,1,0:T(8,128)(2,1)}), bf16[2,2,128,2560]{3,2,1,0:T(8,128)(2,1)}, u32[]{:S(2)}, u32[]{:S(2)}) async-start(bf16[2,2,128,2560]{3,2,1,0:T(8,128)(2,1)} %bitcast.4), calls=%async_computation | async-start | bytes 5242880 | tf_op jit(solution)/shard_map/all_to_all | solution.py:94
  171.2 0.5 broadcast.165
  171.7 0.7 reduce.5
  172.5 11.7 %scatter_custom_fusion.4 = f32[512,1280]{1,0:T(8,128)} fusion(s32[1024]{0:T(1024)S(1)} %bitcast.97, bf16[1024,1280]{1,0:T(8,128)(2,1)S(1)} %bitcast.89, f32[]{:T(128)} %constant.13.clone.1), kind=kCustom, calls=%fused_computation.6 | custom fusion | flops 2621440 | bytes 5242884 | tf_op jit(solution)/shard_map/scatter-add | solution.py:55
  184.2 2.9 %convert_element_type.79 = bf16[512,1280]{1,0:T(8,128)(2,1)} convert(f32[512,1280]{1,0:T(8,128)} %scatter_custom_fusion.4) | non-fusion elementwise | flops 655360 | bytes 3932160 | tf_op jit(solution)/shard_map/convert_element_type | solution.py:58
  187.2 5.8 %fusion.21 = f32[2,2,128,512]{3,2,0,1:T(8,128)} fusion(bf16[2,2560,512]{2,1,0:T(8,128)(2,1)} %all-gather.5.cloned.1.call-done, bf16[2,2,128,2560]{3,2,1,0:T(8,128)(2,1)} %all-to-all-done.1), kind=kOutput, calls=%fused_computation.21 | convolution fusion | flops 1342177280 | bytes 8912896 | tf_op jit(solution)/shard_map/secd,edh->sech/dot_general | solution.py:99
  193.0 16.7 %all-to-all-done = bf16[2,2,128,2560]{3,2,1,0:T(8,128)(2,1)} async-done(((bf16[2,2,128,2560]{3,2,1,0:T(8,128)(2,1)}), bf16[2,2,128,2560]{3,2,1,0:T(8,128)(2,1)}, u32[]{:S(2)}, u32[]{:S(2)}) %all-to-all-start) | async-done | bytes 2621472 | tf_op jit(solution)/shard_map/all_to_all | solution.py:94
  209.6 8.1 %fusion.11 = bf16[2,2,128,2560]{3,2,0,1:T(8,128)(2,1)S(1)} fusion(bf16[2,2560,512]{2,1,0:T(8,128)(2,1)} %all-gather.5.cloned.1.call-done, bf16[2,512,2560]{2,1,0:T(8,128)(2,1)} %all-gather.3.cloned.1.call-done, bf16[2,2,128,2560]{3,2,1,0:T(8,128)(2,1)} %all-to-all-done, f32[2,2,128,512]{3,2,0,1:T(8,128)} %fusion.21), kind=kOutput, calls=%fused_computation.15 | convolution fusion | flops 2688024576 | bytes 16777216 | tf_op jit(solution)/shard_map/sech,edh->secd/dot_general | solution.py:112
  217.8 1.7 copy.65
  219.5 4.2 %all-to-all-start.2 = ((bf16[2,2,128,2560]{3,2,1,0:T(8,128)(2,1)}), bf16[2,2,128,2560]{3,2,1,0:T(8,128)(2,1)S(1)}, u32[]{:S(2)}, u32[]{:S(2)}) async-start(bf16[2,2,128,2560]{3,2,1,0:T(8,128)(2,1)} %copy.65), calls=%async_computation.2 | async-start | bytes 5242880 | tf_op jit(solution)/shard_map/all_to_all | solution.py:118
  223.9 2.3 convert_element_type.81
  226.1 26.4 %all-to-all-done.2 = bf16[2,2,128,2560]{3,2,1,0:T(8,128)(2,1)S(1)} async-done(((bf16[2,2,128,2560]{3,2,1,0:T(8,128)(2,1)}), bf16[2,2,128,2560]{3,2,1,0:T(8,128)(2,1)S(1)}, u32[]{:S(2)}, u32[]{:S(2)}) %all-to-all-start.2) | async-done | bytes 2621472 | tf_op jit(solution)/shard_map/all_to_all | solution.py:118
  252.5 2.5 gather_fusion
  255.0 3.1 %reshape.194 = f32[128,2,2560]{2,1,0:T(2,128)S(1)} reshape(bf16[256,2560]{1,0:T(8,128)(2,1)} %gather_fusion) | data formatting | bytes 3932160 | tf_op jit(solution)/shard_map/convert_element_type | solution.py:120
  258.1 4.5 %multiply_reduce_fusion = bf16[128,2560]{1,0:T(8,128)(2,1)} fusion(f32[128,2,2560]{2,1,0:T(2,128)S(1)} %reshape.194, f32[128,2]{1,0:T(8,128)S(1)} %copy.57), kind=kLoop, calls=%fused_computation.19 | loop fusion | flops 983040 | bytes 3277824 | tf_op jit(solution)/shard_map/reduce_sum | solution.py:121
  (39 shorter events, 1.6 us)
Async XLA Ops:
  8.0 179.2 %all-gather.5.cloned.1.call-start = ((), (), s32[]{:S(2)}) async-start(), calls=%async_computation.7 | async-start | bytes 5570560 | tf_op jit(solution)/shard_map/all_gather | solution.py:115
  8.7 200.9 %all-gather.3.cloned.1.call-start = ((), (), s32[]{:S(2)}) async-start(), calls=%async_computation.6 | async-start | bytes 5570560 | tf_op jit(solution)/shard_map/all_gather | solution.py:108
  17.1 16.5 %all-to-all-start.3 = ((s32[16,1,64]{2,1,0:T(1,128)}), s32[16,1,64]{2,1,0:T(1,128)S(1)}, u32[]{:S(2)}, u32[]{:S(2)}) async-start(s32[16,1,64]{2,1,0:T(1,128)} %all_to_all.21), calls=%async_computation.3 | async-start | bytes 16384 | tf_op jit(solution)/shard_map/all_to_all | solution.py:48
  33.6 5.3 %copy-start = (bf16[128,2560]{1,0:T(8,128)(2,1)S(1)}, bf16[128,2560]{1,0:T(8,128)(2,1)}, u32[]{:S(2)}) copy-start(bf16[128,2560]{1,0:T(8,128)(2,1)} %param.9) | copy-start | bytes 1966084
  33.6 36.3 %all-to-all-start.1 = ((bf16[2,2,128,2560]{3,2,1,0:T(8,128)(2,1)}), bf16[2,2,128,2560]{3,2,1,0:T(8,128)(2,1)}, u32[]{:S(2)}, u32[]{:S(2)}) async-start(bf16[2,2,128,2560]{3,2,1,0:T(8,128)(2,1)} %bitcast.8), calls=%async_computation.1 | async-start | bytes 5242880 | tf_op jit(solution)/shard_map/all_to_all | solution.py:95
  42.1 3.4 %copy-start.1 = (f32[128,4]{0,1:T(4,128)S(1)}, f32[128,4]{0,1:T(4,128)}, u32[]{:S(2)}) copy-start(f32[128,4]{0,1:T(4,128)} %param.15) | copy-start | bytes 6148
  69.8 96.1 %all-to-all-start.4 = ((bf16[16,64,1280]{2,1,0:T(8,128)(2,1)}), bf16[16,64,1280]{2,1,0:T(8,128)(2,1)S(1)}, u32[]{:S(2)}, u32[]{:S(2)}) async-start(bf16[16,64,1280]{2,1,0:T(8,128)(2,1)} %bitcast.90), calls=%async_computation.4 | async-start | bytes 5242880 | tf_op jit(solution)/shard_map/all_to_all | solution.py:41
  165.9 43.7 %all-to-all-start = ((bf16[2,2,128,2560]{3,2,1,0:T(8,128)(2,1)}), bf16[2,2,128,2560]{3,2,1,0:T(8,128)(2,1)}, u32[]{:S(2)}, u32[]{:S(2)}) async-start(bf16[2,2,128,2560]{3,2,1,0:T(8,128)(2,1)} %bitcast.4), calls=%async_computation | async-start | bytes 5242880 | tf_op jit(solution)/shard_map/all_to_all | solution.py:94
  171.2 52.7 %reduce-scatter.2.cloned.1.call-start = ((), (), s32[]{:S(2)}) async-start(), calls=%async_computation.8 | async-start | bytes 1966080 | tf_op jit(solution)/shard_map/reduce_scatter | solution.py:57
  219.5 4.3 %copy-start.2 = (f32[128,2]{0,1:T(2,128)S(1)}, f32[128,2]{0,1:T(2,128)}, u32[]{:S(2)}) copy-start(f32[128,2]{0,1:T(2,128)} %param.12) | copy-start | bytes 3076
  219.5 33.1 %all-to-all-start.2 = ((bf16[2,2,128,2560]{3,2,1,0:T(8,128)(2,1)}), bf16[2,2,128,2560]{3,2,1,0:T(8,128)(2,1)S(1)}, u32[]{:S(2)}, u32[]{:S(2)}) async-start(bf16[2,2,128,2560]{3,2,1,0:T(8,128)(2,1)} %copy.65), calls=%async_computation.2 | async-start | bytes 5242880 | tf_op jit(solution)/shard_map/all_to_all | solution.py:118
Sparse Core Ops, SparseCore 0:
  11.1 56.3 all-gather.4
  69.8 87.8 all-gather.2
Sparse Core Ops, SparseCore 1:
  187.3 30.2 reduce-scatter.1
where the time goes:
time: 271 us; the launch traced here: 270 us
  waiting for transfers between devices  143 us (53%)
  local copies, waits for them, and re-layouts  38.6 us (14%)
  other arithmetic  31.6 us (12%)
  starting transfers between devices  27.2 us (10%)
  between operations  15.7 us (6%)
  matrix products  13.9 us (5%)
    all_to_all x1, waiting for transfers between devices, memory_path(): lax.all_to_all(send_rows.reshape(groups, capacity, width), 'dp', split_ax...  79.2 us
    all_to_all x1, waiting for transfers between devices, per_device(): lax.all_to_all(expert_grad, 'expert', split_axis=0, concat_axis=0, tiled=...  26.4 us
    all_to_all x1, waiting for transfers between devices, per_device(): lax.all_to_all(send_input.reshape(shape), 'expert', split_axis=0, concat_...  19.4 us
    all_to_all x1, waiting for transfers between devices, per_device(): lax.all_to_all(send_grad.reshape(shape), 'expert', split_axis=0, concat_a...  16.7 us
    scatter-add x1, other arithmetic, memory_path(): dense = jnp.zeros((lookups * SHARD, width), jnp.float32).at[got_keys.resh...  11.7 us
    dot_general x1, matrix products, per_device(): jnp.einsum('sech,edh->secd', slope, lax.all_gather(up_weight, 'dp', axis=...  8.14 us
    all_to_all x1, starting transfers between devices, memory_path(): lax.all_to_all(send_keys.reshape(groups, capacity), 'dp', split_axis=0, c...  6.24 us
    all_to_all x1, starting transfers between devices, memory_path(): lax.all_to_all(send_rows.reshape(groups, capacity, width), 'dp', split_ax...  6.03 us
  transfers between devices with their start and end apart: 8, of which 4 were waited for; matrix products, arithmetic and copies ran while one was open for 27% of the time, Pallas kernels for 0%

commit v1 on v0

v1 whole, which is shorter than its diff:
```python
import functools

import jax
import jax.numpy as jnp
from jax import lax
from jax.experimental import pallas as pl
from jax.experimental.pallas import tpu as pltpu
from jax.sharding import PartitionSpec as P

ORDERS = 2
SHARD = 128
LANES = 128


def silu_slope(pre):
    sig = jax.nn.sigmoid(pre)
    return sig * (1.0 + pre * (1.0 - sig))


def swap(value, bit):
    size = lax.axis_size("dp")
    return lax.ppermute(value, "dp", [(i, i ^ bit) for i in range(size)])


def over_expert(value, step):
    size = lax.axis_size("expert")
    return lax.ppermute(value, "expert", [(i, (i + step) % size) for i in range(size)])


def over_even(value):
    size = lax.axis_size("dp")
    pairs = []
    for i in range(size):
        z = i // 4
        to = i if z in (0, size // 4 - 1) else (i + 4 if z % 2 else i - 4)
        pairs.append((i, to))
    return lax.ppermute(value, "dp", pairs)


def pick(by_plane, plane):
    value = by_plane[-1]
    for z in range(len(by_plane) - 2, -1, -1):
        if by_plane[z] is not by_plane[z + 1]:
            value = jnp.where(plane <= z, by_plane[z], value)
    return value


def arrivals(planes):
    orders = []
    for z in range(planes):
        order = []
        for step in range(1, planes):
            for kind in (0, 1):
                offset = step if (z + kind) % 2 == 0 else -step
                if 0 <= z + offset < planes:
                    order.append((step, kind, offset))
        orders.append(order)
    return orders


def prepare_kernel(up_ref, down_ref, grad_ref, *refs):
    ids_ref, weights_ref, gate_ref, owner_ref, slot_ref, packed_ref, rows_ref, meta_ref = refs
    blocks, rows, cols = packed_ref.shape[1] // 2, packed_ref.shape[2], packed_ref.shape[3]
    for e in range(packed_ref.shape[0]):
        for b in range(blocks):
            packed_ref[e, b] = up_ref[e, b * rows : (b + 1) * rows, :]
            packed_ref[e, blocks + b] = down_ref[e, :, b * cols : (b + 1) * cols]
    tok, width = grad_ref.shape
    rows_ref[:, pl.ds(0, width)] = grad_ref[...]
    weights = weights_ref[...]
    high = weights.astype(jnp.bfloat16).astype(jnp.float32)
    meta_ref[...] = jnp.zeros_like(meta_ref)
    at = 0
    for value in (
        owner_ref[...].astype(jnp.float32),
        slot_ref[...].astype(jnp.float32),
        gate_ref[...],
        ids_ref[...].astype(jnp.float32),
        high,
        weights - high,
    ):
        meta_ref[pl.ds(at, value.shape[0]), :] = value
        at += value.shape[0]
    rows_ref[:, pl.ds(width, LANES)] = meta_ref[...].T.astype(jnp.bfloat16)


def prepare(up, down, grad_out, expert_ids, gate_weights, engram_gate, owner, slot):
    experts, _, hid = up.shape
    rows, width = down.shape[1:]
    tok = grad_out.shape[0]
    return pl.pallas_call(
        prepare_kernel,
        out_shape=(
            jax.ShapeDtypeStruct((experts, 2 * (width // hid), rows, hid), up.dtype),
            jax.ShapeDtypeStruct((tok, width + LANES), grad_out.dtype),
        ),
        scratch_shapes=[pltpu.VMEM((LANES, tok), jnp.float32)],
    )(up, down, grad_out, expert_ids.T, gate_weights.T, engram_gate.T, owner.T, slot.T)


def table_kernel(lookups, planes, place_ref, *refs):
    blocks = refs[: -planes - 2]
    outs, tokens, sem = refs[-planes - 2 : -2], refs[-2], refs[-1]
    tok, total = blocks[0].shape
    width = total - LANES
    half = width // ORDERS
    heads = lookups // ORDERS
    part = outs[0].shape[0] // lookups
    copies = []
    for b, block in enumerate(blocks):
        copy = pltpu.make_async_copy(block, tokens.at[pl.ds(b * tok, tok)], sem.at[b])
        copy.start()
        copies.append(copy)
    for copy in copies:
        copy.wait()
    count = tok * len(blocks)
    metas = [
        tokens[pl.ds(b * tok, tok), pl.ds(width, LANES)].astype(jnp.float32).T
        for b in range(len(blocks))
    ]
    meta = jnp.concatenate([m[: 3 * lookups] for m in metas], axis=1)
    key = meta[:lookups] * SHARD + meta[lookups : 2 * lookups]
    gate = meta[2 * lookups :]
    me, expert = place_ref[0], place_ref[1]
    plane = me // 4
    row = lax.broadcasted_iota(jnp.int32, (part, count), 0)
    for o in range(ORDERS):
        hits = []
        for offset in range(planes):
            to = lax.rem(jnp.where(plane % 2 == 0, plane + offset, plane + planes - offset), planes)
            to = to * 4 + me % 4
            rows = (row + (to * SHARD + expert * part)).astype(jnp.float32)
            for j in range(o * heads, (o + 1) * heads):
                hit = jnp.where(rows == key[j : j + 1], gate[j : j + 1], 0.0)
                hits.append(hit.astype(jnp.bfloat16))
        sums = jnp.dot(
            jnp.concatenate(hits, axis=0),
            tokens[:, pl.ds(o * half, half)],
            preferred_element_type=jnp.float32,
        )
        size = heads * part
        for offset in range(planes):
            outs[offset][pl.ds(o * size, size), :] = sums[
                offset * size : (offset + 1) * size
            ].astype(outs[offset].dtype)


def table_sums(blocks, place, lookups, part):
    tok, total = blocks[0].shape
    half = (total - LANES) // ORDERS
    planes = lax.axis_size("dp") // 4
    rows = lookups * part
    return pl.pallas_call(
        functools.partial(table_kernel, lookups, planes),
        out_shape=tuple(
            jax.ShapeDtypeStruct((rows, half), jnp.bfloat16 if offset else jnp.float32)
            for offset in range(planes)
        ),
        in_specs=[pl.BlockSpec(memory_space=pltpu.SMEM)]
        + [pl.BlockSpec(memory_space=pl.ANY)] * len(blocks),
        scratch_shapes=[
            pltpu.VMEM((tok * len(blocks), total), jnp.bfloat16),
            pltpu.SemaphoreType.DMA((len(blocks),)),
        ],
        compiler_params=pltpu.CompilerParams(vmem_limit_bytes=56 << 20),
        cost_estimate=pl.CostEstimate(
            flops=2 * planes * rows * tok * len(blocks) * half,
            bytes_accessed=2 * tok * len(blocks) * total + 2 * planes * rows * half,
            transcendentals=0,
        ),
    )(place, *blocks)


def ffn_kernel(where, groups, planes, lookups, top, *refs):
    place_ref, tokens, refs = refs[0], refs[1 : 1 + 2 * groups], refs[1 + 2 * groups :]
    pieces, refs = refs[: len(where)], refs[len(where) :]
    own_ref, rest_ref, grad, inp, up, down, token_sem, piece_sem = refs
    tok, width = own_ref.shape
    experts, blocks, size, rows, hid = down.shape
    me, expert = place_ref[0], place_ref[1]
    plane = me // 4

    token_copies = []
    for g in range(groups):
        for source, target, sem in ((tokens[g], grad, 0), (tokens[groups + g], inp, 1)):
            copy = pltpu.make_async_copy(
                source, target.at[pl.ds(g * tok, tok)], token_sem.at[sem, g]
            )
            copy.start()
            token_copies.append(copy)
    ups, downs = [], []
    for number, (offsets, flip) in enumerate(where):
        at = jnp.bitwise_xor(me, flip)
        for z, offset in enumerate(offsets):
            if offset:
                at = at + jnp.where(plane == z, 4 * offset, 0)
        copy = pltpu.make_async_copy(
            pieces[number].at[:, pl.ds(0, blocks)],
            up.at[:, pl.ds(at * blocks, blocks)],
            piece_sem.at[0, number],
        )
        copy.start()
        ups.append(copy)
        copy = pltpu.make_async_copy(
            pieces[number].at[:, pl.ds(blocks, blocks)],
            down.at[:, :, at],
            piece_sem.at[1, number],
        )
        copy.start()
        downs.append(copy)
    for copy in token_copies + ups + downs:
        copy.wait()

    def up_block(e, b):
        return up[e, b * size : (b + 1) * size].reshape(size * rows, hid)

    chunk = 2 * tok if groups % 2 == 0 else tok
    for start in range(0, groups * tok, chunk):
        span = pl.ds(start, chunk)
        meta = grad[span, pl.ds(width, LANES)].astype(jnp.float32)
        at = 3 * lookups
        slopes = []
        for e in range(experts):
            pre = jnp.zeros((chunk, hid), jnp.float32)
            back = jnp.zeros((chunk, hid), jnp.float32)
            for b in range(blocks):
                cols = pl.ds(b * hid, hid)
                pre += jnp.dot(inp[span, cols], up_block(e, b), preferred_element_type=jnp.float32)
                back += lax.dot_general(
                    grad[span, cols],
                    down[e, b].reshape(size * rows, hid),
                    (((1,), (1,)), ((), ())),
                    preferred_element_type=jnp.float32,
                )
            weight = jnp.zeros((chunk, 1), jnp.float32)
            number = (expert * experts + e).astype(jnp.float32)
            for k in range(top):
                value = meta[:, at + top + k : at + top + k + 1]
                value += meta[:, at + 2 * top + k : at + 2 * top + k + 1]
                weight += jnp.where(meta[:, at + k : at + k + 1] == number, value, 0.0)
            slopes.append((back * silu_slope(pre) * weight).astype(jnp.bfloat16))
        for b in range(blocks):
            cols = pl.ds(b * hid, hid)
            total = jnp.zeros((chunk, hid), jnp.float32)
            for e in range(experts):
                total += lax.dot_general(
                    slopes[e],
                    up_block(e, b),
                    (((1,), (1,)), ((), ())),
                    preferred_element_type=jnp.float32,
                )
            if start == 0:
                own_ref[:, cols] = total[:tok]
                if chunk > tok:
                    rest_ref[pl.ds(0, chunk - tok), cols] = total[tok:].astype(jnp.bfloat16)
            else:
                rest_ref[pl.ds(start - tok, chunk), cols] = total.astype(jnp.bfloat16)


def expert_layers(grads, inputs, pieces, place, lookups, top):
    groups = len(grads)
    tok, width = inputs[0].shape
    experts, blocks2, rows, hid = pieces[0][0].shape
    blocks = blocks2 // 2
    dp = lax.axis_size("dp")
    where = tuple((tuple(offsets), flip) for _, offsets, flip in pieces)
    rest_rows = max(groups - 1, 1) * tok
    return pl.pallas_call(
        functools.partial(ffn_kernel, where, groups, dp // 4, lookups, top),
        out_shape=(
            jax.ShapeDtypeStruct((tok, width), jnp.float32),
            jax.ShapeDtypeStruct((rest_rows, width), jnp.bfloat16),
        ),
        in_specs=[pl.BlockSpec(memory_space=pltpu.SMEM)]
        + [pl.BlockSpec(memory_space=pl.ANY)] * (2 * groups + len(pieces)),
        out_specs=(
            pl.BlockSpec(memory_space=pltpu.VMEM),
            pl.BlockSpec(memory_space=pltpu.VMEM),
        ),
        scratch_shapes=[
            pltpu.VMEM((groups * tok, width + LANES), jnp.bfloat16),
            pltpu.VMEM((groups * tok, width), jnp.bfloat16),
            pltpu.VMEM((experts, dp * blocks, rows, hid), jnp.bfloat16),
            pltpu.VMEM((experts, blocks, dp, rows, hid), jnp.bfloat16),
            pltpu.SemaphoreType.DMA((2, groups)),
            pltpu.SemaphoreType.DMA((2, len(pieces))),
        ],
        compiler_params=pltpu.CompilerParams(vmem_limit_bytes=56 << 20),
        cost_estimate=pl.CostEstimate(
            flops=6 * groups * tok * width * hid * experts,
            bytes_accessed=4 * experts * width * hid + 12 * groups * tok * width,
            transcendentals=groups * tok * hid * experts,
        ),
    )(place, *grads, *inputs, *[piece[0] for piece in pieces])


def per_device(
    grad_out,
    saved_input,
    expert_ids,
    gate_weights,
    up_weight,
    down_weight,
    engram_gate,
    memory_owner,
    memory_slot,
):
    tok, width = grad_out.shape
    lookups, top = engram_gate.shape[1], expert_ids.shape[1]
    groups = lax.axis_size("expert")
    planes = lax.axis_size("dp") // 4
    part = SHARD // groups
    me = lax.axis_index("dp")
    plane = me // 4
    place = jnp.stack([me, lax.axis_index("expert")]).astype(jnp.int32)
    others = range(1, groups)
    fence = lax.optimization_barrier

    packed, rows = prepare(
        up_weight,
        down_weight,
        grad_out,
        expert_ids,
        gate_weights,
        engram_gate,
        memory_owner,
        memory_slot,
    )
    orders = arrivals(planes)
    came = {}
    zero = (0,) * planes
    pieces = [(packed, zero, 0)]
    blocks = [rows]
    grads = [rows]

    def along(step, line):
        even = over_even(line[0]) if step < planes - 1 else None
        return swap(line[1], 4), even

    def arrival(number):
        by_plane = [came[order[number][0]][order[number][1]] for order in orders]
        return pick(by_plane, plane), tuple(order[number][2] for order in orders)

    inner = jnp.logical_and(plane > 0, plane < planes - 1)

    def plus(share, came_in, even):
        came_in = came_in.astype(jnp.float32)
        if even:
            came_in = jnp.where(inner, came_in, 0.0)
        return share.astype(jnp.float32) + came_in

    def reduce(step, sums):
        odd, even = partials[planes - step], partials[step]
        if step > 1 and sums[1] is not None:
            odd = plus(odd, sums[1], True).astype(jnp.bfloat16)
        even = over_even(plus(even, sums[0], False).astype(jnp.bfloat16)) if step > 1 else None
        return swap(odd, 4), even

    def together(near, line, over_y, over_x, *rest):
        near, line, over_y, over_x, rest = fence((near, line[::-1], over_y, over_x, rest))
        return near, line[::-1], over_y, over_x, rest

    near = swap(rows, 1)
    line = along(1, (packed, packed))
    got = [over_expert(rows, step) for step in others]
    rows_x = swap(rows, 2)
    near, line, got, rows_x, (late,) = together(near, line, got, rows_x, packed)
    came[1] = line
    grads += got
    blocks += [near, rows_x] + got

    near = swap(rows_x, 1)
    line = along(2, line) if planes > 2 else line
    far = [over_expert(rows_x, step) for step in others]
    own_x = swap(late, 2)
    value, where = arrival(0)
    near, line, far, passed, (value, later) = together(near, line, far, own_x, value, saved_input)
    came[min(2, planes - 1)] = line
    blocks += [near] + far
    pieces += [(passed, zero, 2)]
    waiting = [(packed, zero, 1), (passed, zero, 3)]

    sums, inputs = (), []
    for number in range(1, planes):
        pieces += [(value, where, 0)]
        moved, waiting = waiting, [(value, where, 1)]
        next_value = next_at = ()
        if number + 1 < planes:
            next_value, next_at = arrival(number)
        if number == 1:
            near = [swap(block, 1) for block in got + far]
            partials = table_sums(blocks + near, place, lookups, part)
            moved, waiting = [], moved + waiting
            inputs = [over_expert(later, step) for step in others]
        elif number + 1 == planes:
            moved, waiting = moved[:2], moved[2:] + waiting
        near = [swap(entry[0], 1) for entry in moved]
        if number + 2 < planes:
            line = along(number + 2, line)
        if number > 1:
            sums = reduce(number - 1, sums)
        near, line, (inputs, sums), passed, (partials, value) = together(
            near, line, (inputs, sums[::-1]), swap(value, 2), partials, next_value
        )
        sums = sums[::-1]
        pieces += [(core, at, flip) for core, (_, at, flip) in zip(near, moved)]
        pieces += [(passed, where, 2)]
        waiting += [(passed, where, 3)]
        came[min(number + 2, planes - 1)] = line
        where = next_at
    inputs = [saved_input] + inputs

    sums = reduce(planes - 1, sums)
    pieces += [(swap(value, 1), at, flip) for value, at, flip in waiting]
    total, rest = expert_layers(grads, inputs, pieces, place, lookups, top)
    total, sums = fence((total, sums))
    for back in others:
        value = rest[(back - 1) * tok : back * tok]
        total = total + over_expert(value, groups - back).astype(jnp.float32)
    table = partials[0]
    for came_in, even in zip(sums, (False, True)):
        if came_in is not None:
            table = plus(table, came_in, even)
    return total.astype(jnp.bfloat16), table.reshape(lookups, part, width // ORDERS)


def solution(mesh):
    return jax.shard_map(
        per_device,
        mesh=mesh,
        in_specs=(
            P(("dp", "expert"), None),
            P(("dp", "expert"), None),
            P(("dp", "expert"), None),
            P(("dp", "expert"), None),
            P("expert", "dp", None),
            P("expert", "dp", None),
            P(("dp", "expert"), None),
            P(("dp", "expert"), None),
            P(("dp", "expert"), None),
        ),
        out_specs=(P(("dp", "expert"), None), P(None, ("dp", "expert"), None)),
        check_vma=False,
    )
```

time: 271 us -> 148 us (0.55)
  waiting for transfers between devices: 143 us -> 88.7 us
  local copies, waits for them, and re-layouts: 38.6 us -> 1.65 us
  other arithmetic: 31.6 us -> 6.45 us
  Pallas kernels: 0 us -> 21.8 us
  between operations: 15.7 us -> 1.01 us
  matrix products: 13.9 us -> 0 us
    all_to_all x5 -> x0, waiting for transfers between devices: 142 us -> none  [the longest x1 79.2 us: memory_path(): lax.all_to_all(send_rows.reshape(groups, capacity, width), 'dp', split_ax...]
    ppermute x0 -> x31, waiting for transfers between devices: none -> 88.7 us  [the longest x23 47.8 us: swap(): return lax.ppermute(value, 'dp', [(i, i ^ bit) for i in range(size)])]
    all_to_all x5 -> x0, starting transfers between devices: 27.1 us -> none  [the longest x1 6.24 us: memory_path(): lax.all_to_all(send_keys.reshape(groups, capacity), 'dp', split_axis=0, c...]
    ppermute x0 -> x31, starting transfers between devices: none -> 25.7 us  [the longest x4 14.2 us: over_even(): return lax.ppermute(value, 'dp', pairs)]
    pallas_call x0 -> x3, Pallas kernels: none -> 21.8 us  [the longest x1 11.3 us: expert_layers(): pl.pallas_call(functools.partial(ffn_kernel, where, groups, dp // 4, look...]
    dot_general x2 -> x0, matrix products: 13.9 us -> none  [the longest x1 8.14 us: per_device(): jnp.einsum('sech,edh->secd', slope, lax.all_gather(up_weight, 'dp', axis=...]
    scatter x3 -> x0, local copies, waits for them, and re-layouts: 11.8 us -> none  [the longest x1 5.06 us: per_device(): send_grad = jnp.zeros((experts * capacity, width), jnp.bfloat16).at[place...]
    scatter-add x1 -> x0, other arithmetic: 11.7 us -> none  [memory_path(): dense = jnp.zeros((lookups * SHARD, width), jnp.float32).at[got_keys.resh...]
  transfers between devices with their start and end apart: 8 -> 31, of which waited for: 4 -> 15; matrix products, arithmetic and copies ran while one was open for 27% -> 4% of each run, Pallas kernels for 0% -> 13%
where the time goes in v1:
time: 148 us; the launch traced here: 145 us
  waiting for transfers between devices  88.7 us (60%)
  starting transfers between devices  25.7 us (17%)
  Pallas kernels  21.8 us (15%)
  other arithmetic  6.45 us (4%)
  local copies, waits for them, and re-layouts  1.65 us (1%)
    ppermute x23, waiting for transfers between devices, swap(): return lax.ppermute(value, 'dp', [(i, i ^ bit) for i in range(size)])  47.8 us
    ppermute x4, waiting for transfers between devices, over_even(): return lax.ppermute(value, 'dp', pairs)  22.7 us
    ppermute x4, waiting for transfers between devices, over_expert(): lax.ppermute(value, 'expert', [(i, (i + step) % size) for i in range(size)])  18.3 us
    ppermute x4, starting transfers between devices, over_even(): return lax.ppermute(value, 'dp', pairs)  14.2 us
    pallas_call x1, Pallas kernels, expert_layers(): pl.pallas_call(functools.partial(ffn_kernel, where, groups, dp // 4, look...  11.3 us
    pallas_call x1, Pallas kernels, table_sums(): pl.pallas_call(functools.partial(table_kernel, lookups, planes), out_shap...  7.98 us
    ppermute x23, starting transfers between devices, swap(): return lax.ppermute(value, 'dp', [(i, i ^ bit) for i in range(size)])  7.35 us
    ppermute x4, starting transfers between devices, over_expert(): lax.ppermute(value, 'expert', [(i, (i + step) % size) for i in range(size)])  4.18 us
  transfers between devices with their start and end apart: 31, of which 15 were waited for; matrix products, arithmetic and copies ran while one was open for 4% of the time, Pallas kernels for 13%

profile of v1, /device:TPU:10, one launch (start us, length us, event | category | flops | bytes accessed | tf_op | source)
XLA Modules:
  0.0 145.4 jit_solution(17042197327496309153)
XLA Ops:
  0.6 2.5 %shard_map.104 = (bf16[2,10,32,512]{3,2,1,0:T(8,128)(2,1)}, bf16[128,2688]{1,0:T(8,128)(2,1)}) custom-call(bf16[2,160,512]{2,1,0:T(8,128)(2,1)} %up_ref.1, bf16[2,32,2560]{2,1,0:T(8,128)(2,1)} %down_ref.1, bf16[128,2560]{1,0:T(8,128)(2,1)} %grad_ref.1, s32[2,128]{1,0:T(2,128)} %bitcast.12, f32[2,128]{1,0:T(2,128)} %bitcast.13, f32[4,128]{1,0:T(4,128)} %bitcast.9, ...), custom_call_target="tpu_custom_call" | custom-call | tf_op jit(solution)/shard_map/pallas_call | solution.py:91
  3.1 0.5 collective-permute-start.4
  3.6 1.5 %collective-permute-start.3 = (bf16[128,2688]{1,0:T(8,128)(2,1)}, bf16[128,2688]{1,0:T(8,128)(2,1)S(1)}, u32[]{:S(2)}, u32[]{:S(2)}) collective-permute-start(bf16[128,2688]{1,0:T(8,128)(2,1)} %get-tuple-element.55.refs_0_.refs_1_), channel_id=1, source_target_pairs={{0,1},{1,0},{2,3},{3,2},{4,5},{5,4},{6,7},{7,6},{8,9},{9,8},{10,11... | collective-permute-start | bytes 2064392 | tf_op jit(solution)/shard_map/ppermute | solution.py:27
  5.2 0.4 collective-permute-start.2
  5.6 4.6 %collective-permute-start.1 = (bf16[2,10,32,512]{3,2,1,0:T(8,128)(2,1)}, bf16[2,10,32,512]{3,2,1,0:T(8,128)(2,1)S(1)}, u32[]{:S(2)}, u32[]{:S(2)}) collective-permute-start(bf16[2,10,32,512]{3,2,1,0:T(8,128)(2,1)} %get-tuple-element.61.refs_5_), channel_id=1, source_target_pairs={{0,0},{2,2},{4,4},{6,6},{8,16},{10,18},{12,20},{14,22},{16,8},{18,... | collective-permute-start | bytes 1966088 | tf_op jit(solution)/shard_map/ppermute | solution.py:37
  10.2 12.4 %collective-permute-done.2.refs_7_ = bf16[2,10,32,512]{3,2,1,0:T(8,128)(2,1)} collective-permute-done((bf16[2,10,32,512]{3,2,1,0:T(8,128)(2,1)}, bf16[2,10,32,512]{3,2,1,0:T(8,128)(2,1)}, u32[]{:S(2)}, u32[]{:S(2)}) %collective-permute-start.2) | collective-permute-done | bytes 655392 | tf_op jit(solution)/shard_map/ppermute | solution.py:22
  22.6 2.9 %collective-permute-done.1 = bf16[2,10,32,512]{3,2,1,0:T(8,128)(2,1)S(1)} collective-permute-done((bf16[2,10,32,512]{3,2,1,0:T(8,128)(2,1)}, bf16[2,10,32,512]{3,2,1,0:T(8,128)(2,1)S(1)}, u32[]{:S(2)}, u32[]{:S(2)}) %collective-permute-start.1) | collective-permute-done | bytes 655392 | tf_op jit(solution)/shard_map/ppermute | solution.py:37
  25.6 1.6 %collective-permute-start.9 = (bf16[2,10,32,512]{3,2,1,0:T(8,128)(2,1)}, bf16[2,10,32,512]{3,2,1,0:T(8,128)(2,1)S(1)}, u32[]{:S(2)}, u32[]{:S(2)}) collective-permute-start(bf16[2,10,32,512]{3,2,1,0:T(8,128)(2,1)} %get-tuple-element.61.refs_5_), channel_id=1, source_target_pairs={{0,4},{2,6},{4,0},{6,2},{8,12},{10,14},{12,8},{14,10},{16,20},{18,... | collective-permute-start | bytes 1966088 | tf_op jit(solution)/shard_map/ppermute | solution.py:22
  27.1 0.5 collective-permute-start.8
  27.6 3.6 %collective-permute-start.6 = (bf16[2,10,32,512]{3,2,1,0:T(8,128)(2,1)}, bf16[2,10,32,512]{3,2,1,0:T(8,128)(2,1)S(1)}, u32[]{:S(2)}, u32[]{:S(2)}) collective-permute-start(bf16[2,10,32,512]{3,2,1,0:T(8,128)(2,1)} %collective-permute-done.2.refs_7_), channel_id=1, source_target_pairs={{0,0},{2,2},{4,4},{6,6},{8,16},{10,18},{12,20},{14,22},{16,8},{18,... | collective-permute-start | bytes 1966088 | tf_op jit(solution)/shard_map/ppermute | solution.py:37
  31.3 0.1 collective-permute-start.7
  31.4 10.9 %collective-permute-done.9.refs_6_ = bf16[2,10,32,512]{3,2,1,0:T(8,128)(2,1)S(1)} collective-permute-done((bf16[2,10,32,512]{3,2,1,0:T(8,128)(2,1)}, bf16[2,10,32,512]{3,2,1,0:T(8,128)(2,1)S(1)}, u32[]{:S(2)}, u32[]{:S(2)}) %collective-permute-start.9) | collective-permute-done | bytes 655392 | tf_op jit(solution)/shard_map/ppermute | solution.py:22
  42.2 4.7 %collective-permute-done.6 = bf16[2,10,32,512]{3,2,1,0:T(8,128)(2,1)S(1)} collective-permute-done((bf16[2,10,32,512]{3,2,1,0:T(8,128)(2,1)}, bf16[2,10,32,512]{3,2,1,0:T(8,128)(2,1)S(1)}, u32[]{:S(2)}, u32[]{:S(2)}) %collective-permute-start.6) | collective-permute-done | bytes 655392 | tf_op jit(solution)/shard_map/ppermute | solution.py:37
  46.9 1.3 collective-permute-done.7
  48.2 0.1 collective-permute-start.14
  48.3 1.6 %collective-permute-start.11 = (bf16[128,2560]{1,0:T(8,128)(2,1)}, bf16[128,2560]{1,0:T(8,128)(2,1)}, u32[]{:S(2)}, u32[]{:S(2)}) collective-permute-start(bf16[128,2560]{1,0:T(8,128)(2,1)} %refs_3_.1), channel_id=1, source_target_pairs={{0,1},{1,0},{2,3},{3,2},{4,5},{5,4},{6,7},{7,6},{8,9},{9,8},{10,11... | collective-permute-start | bytes 1966088 | tf_op jit(solution)/shard_map/ppermute | solution.py:27
  49.9 0.3 collective-permute-start.10
  50.2 0.5 collective-permute-start.12
  50.8 0.7 copy-done.10
  51.6 0.6 pad_add_fusion.place_ref.refs_0_
  52.3 8.0 %shard_map.105 = (f32[256,1280]{1,0:T(8,128)}, bf16[256,1280]{1,0:T(8,128)(2,1)}, bf16[256,1280]{1,0:T(8,128)(2,1)}, bf16[256,1280]{1,0:T(8,128)(2,1)}) custom-call(s32[2]{0:T(128)} %pad_add_fusion.place_ref.refs_0_, bf16[128,2688]{1,0:T(8,128)(2,1)} %get-tuple-element.55.refs_0_.refs_1_, bf16[128,2688]{1,0:T(8,128)(2,1)} %copy-done.8, ...), custom_call_target="tpu_custom_call" | custom-call | flops 2684354560 | bytes 8126464 | tf_op jit(solution)/shard_map/pallas_call | solution.py:153
  60.3 5.5 %collective-permute-done.11.refs_4_ = bf16[128,2560]{1,0:T(8,128)(2,1)} collective-permute-done((bf16[128,2560]{1,0:T(8,128)(2,1)}, bf16[128,2560]{1,0:T(8,128)(2,1)}, u32[]{:S(2)}, u32[]{:S(2)}) %collective-permute-start.11) | collective-permute-done | bytes 655392 | tf_op jit(solution)/shard_map/ppermute | solution.py:27
  65.8 0.9 collective-permute-done.10
  66.7 0.3 collective-permute-done.12.refs_8_
  67.0 1.7 %collective-permute-start.20 = (bf16[256,1280]{1,0:T(8,128)(2,1)}, bf16[256,1280]{1,0:T(8,128)(2,1)S(1)}, u32[]{:S(2)}, u32[]{:S(2)}) collective-permute-start(bf16[256,1280]{1,0:T(8,128)(2,1)} %get-tuple-element.101), channel_id=1, source_target_pairs={{0,8},{2,10},{4,12},{6,14},{8,0},{10,2},{12,4},{14,6},{16,24},{18,... | collective-permute-start | bytes 1966088 | tf_op jit(solution)/shard_map/ppermute | solution.py:22
  68.8 0.5 collective-permute-start.21
  69.4 0.1 collective-permute-start.15
  69.5 14.8 %collective-permute-done.20 = bf16[256,1280]{1,0:T(8,128)(2,1)S(1)} collective-permute-done((bf16[256,1280]{1,0:T(8,128)(2,1)}, bf16[256,1280]{1,0:T(8,128)(2,1)S(1)}, u32[]{:S(2)}, u32[]{:S(2)}) %collective-permute-start.20) | collective-permute-done | bytes 655392 | tf_op jit(solution)/shard_map/ppermute | solution.py:22
  84.4 1.4 collective-permute-done.21.refs_14_
  85.7 0.4 collective-permute-start.24
  86.1 2.1 %add_convert_fusion.3 = bf16[256,1280]{1,0:T(8,128)(2,1)} fusion(bf16[256,1280]{1,0:T(8,128)(2,1)S(1)} %collective-permute-done.20, bf16[256,1280]{1,0:T(8,128)(2,1)} %get-tuple-element.84), kind=kLoop, calls=%fused_computation.4 | loop fusion | flops 1310720 | bytes 1966080 | tf_op jit(solution)/shard_map/convert_element_type | solution.py:356
  88.2 2.4 %collective-permute-start.23 = (bf16[256,1280]{1,0:T(8,128)(2,1)}, bf16[256,1280]{1,0:T(8,128)(2,1)S(1)}, u32[]{:S(2)}, u32[]{:S(2)}) collective-permute-start(bf16[256,1280]{1,0:T(8,128)(2,1)} %add_convert_fusion.3), channel_id=1, source_target_pairs={{0,0},{2,2},{4,4},{6,6},{8,16},{10,18},{12,20},{14,22},{16,8},{18,... | collective-permute-start | bytes 1966088 | tf_op jit(solution)/shard_map/ppermute | solution.py:37
  90.7 0.1 collective-permute-start.22
  90.8 0.6 collective-permute-start.25
  91.4 0.2 collective-permute-start.26
  91.5 15.1 %collective-permute-done.23 = bf16[256,1280]{1,0:T(8,128)(2,1)S(1)} collective-permute-done((bf16[256,1280]{1,0:T(8,128)(2,1)}, bf16[256,1280]{1,0:T(8,128)(2,1)S(1)}, u32[]{:S(2)}, u32[]{:S(2)}) %collective-permute-start.23) | collective-permute-done | bytes 655392 | tf_op jit(solution)/shard_map/ppermute | solution.py:37
  106.6 1.4 collective-permute-done.25.refs_18_
  108.0 1.2 add_convert_fusion.1
  109.3 3.5 %collective-permute-start.29 = (bf16[256,1280]{1,0:T(8,128)(2,1)S(1)}, bf16[256,1280]{1,0:T(8,128)(2,1)S(1)}, u32[]{:S(2)}, u32[]{:S(2)}) collective-permute-start(bf16[256,1280]{1,0:T(8,128)(2,1)S(1)} %add_convert_fusion.1), channel_id=1, source_target_pairs={{0,0},{2,2},{4,4},{6,6},{8,16},{10,18},{12,20},{14,22},{16,8},{18,... | collective-permute-start | bytes 1966088 | tf_op jit(solution)/shard_map/ppermute | solution.py:37
  112.9 0.2 add_convert_fusion.2
  113.2 2.0 %collective-permute-done.27.refs_20_ = bf16[2,10,32,512]{3,2,1,0:T(8,128)(2,1)S(1)} collective-permute-done((bf16[2,10,32,512]{3,2,1,0:T(8,128)(2,1)}, bf16[2,10,32,512]{3,2,1,0:T(8,128)(2,1)S(1)}, u32[]{:S(2)}, u32[]{:S(2)}) %collective-permute-start.27) | collective-permute-done | bytes 655392 | tf_op jit(solution)/shard_map/ppermute | solution.py:22
  115.2 0.8 copy-done.17
  116.0 11.3 %shard_map.106 = (f32[128,2560]{1,0:T(8,128)}, bf16[128,2560]{1,0:T(8,128)(2,1)}) custom-call(s32[2]{0:T(128)} %pad_add_fusion.place_ref.refs_0_, bf16[128,2688]{1,0:T(8,128)(2,1)} %get-tuple-element.55.refs_0_.refs_1_, bf16[128,2688]{1,0:T(8,128)(2,1)} %copy-done.6, bf16[128,2560]{1,0:T(8,128)(2,1)} %refs_3_.1, ...), custom_call_target="tpu_custom_call" | custom-call | flops 4026531840 | bytes 18350080 | tf_op jit(solution)/shard_map/pallas_call | solution.py:268
  127.4 0.6 collective-permute-start.30
  127.9 2.4 %collective-permute-done.28 = bf16[256,1280]{1,0:T(8,128)(2,1)S(1)} collective-permute-done((bf16[256,1280]{1,0:T(8,128)(2,1)S(1)}, bf16[256,1280]{1,0:T(8,128)(2,1)S(1)}, u32[]{:S(2)}, u32[]{:S(2)}) %collective-permute-start.28) | collective-permute-done | bytes 655392 | tf_op jit(solution)/shard_map/ppermute | solution.py:22
  130.3 1.3 select_add_fusion
  131.6 12.8 %collective-permute-done.30 = bf16[128,2560]{1,0:T(8,128)(2,1)S(1)} collective-permute-done((bf16[128,2560]{1,0:T(8,128)(2,1)}, bf16[128,2560]{1,0:T(8,128)(2,1)S(1)}, u32[]{:S(2)}, u32[]{:S(2)}) %collective-permute-start.30) | collective-permute-done | bytes 655392 | tf_op jit(solution)/shard_map/ppermute | solution.py:27
  144.4 0.9 add_convert_fusion
  (61 shorter events, 0.5 us)
Async XLA Ops:
  3.1 22.4 %collective-permute-start.4 = (bf16[128,2688]{1,0:T(8,128)(2,1)}, bf16[128,2688]{1,0:T(8,128)(2,1)S(1)}, u32[]{:S(2)}, u32[]{:S(2)}) collective-permute-start(bf16[128,2688]{1,0:T(8,128)(2,1)} %get-tuple-element.55.refs_0_.refs_1_), channel_id=1, source_target_pairs={{0,4},{2,6},{4,0},{6,2},{8,12},{10,14},{12,8},{14,10},{16,20},{18,... | collective-permute-start | bytes 2064392 | tf_op jit(solution)/shard_map/ppermute | solution.py:22
  3.6 21.9 %collective-permute-start.3 = (bf16[128,2688]{1,0:T(8,128)(2,1)}, bf16[128,2688]{1,0:T(8,128)(2,1)S(1)}, u32[]{:S(2)}, u32[]{:S(2)}) collective-permute-start(bf16[128,2688]{1,0:T(8,128)(2,1)} %get-tuple-element.55.refs_0_.refs_1_), channel_id=1, source_target_pairs={{0,1},{1,0},{2,3},{3,2},{4,5},{5,4},{6,7},{7,6},{8,9},{9,8},{10,11... | collective-permute-start | bytes 2064392 | tf_op jit(solution)/shard_map/ppermute | solution.py:27
  5.1 20.4 %collective-permute-start = (bf16[128,2688]{1,0:T(8,128)(2,1)}, bf16[128,2688]{1,0:T(8,128)(2,1)S(1)}, u32[]{:S(2)}, u32[]{:S(2)}) collective-permute-start(bf16[128,2688]{1,0:T(8,128)(2,1)} %get-tuple-element.55.refs_0_.refs_1_), channel_id=1, source_target_pairs={{0,2},{2,0},{4,6},{6,4},{8,10},{10,8},{12,14},{14,12},{16,18},{18,... | collective-permute-start | bytes 2064392 | tf_op jit(solution)/shard_map/ppermute | solution.py:22
  5.2 17.5 %collective-permute-start.2 = (bf16[2,10,32,512]{3,2,1,0:T(8,128)(2,1)}, bf16[2,10,32,512]{3,2,1,0:T(8,128)(2,1)}, u32[]{:S(2)}, u32[]{:S(2)}) collective-permute-start(bf16[2,10,32,512]{3,2,1,0:T(8,128)(2,1)} %get-tuple-element.61.refs_5_), channel_id=1, source_target_pairs={{0,8},{2,10},{4,12},{6,14},{8,0},{10,2},{12,4},{14,6},{16,24},{18,... | collective-permute-start | bytes 1966088 | tf_op jit(solution)/shard_map/ppermute | solution.py:22
  5.6 19.9 %collective-permute-start.1 = (bf16[2,10,32,512]{3,2,1,0:T(8,128)(2,1)}, bf16[2,10,32,512]{3,2,1,0:T(8,128)(2,1)S(1)}, u32[]{:S(2)}, u32[]{:S(2)}) collective-permute-start(bf16[2,10,32,512]{3,2,1,0:T(8,128)(2,1)} %get-tuple-element.61.refs_5_), channel_id=1, source_target_pairs={{0,0},{2,2},{4,4},{6,6},{8,16},{10,18},{12,20},{14,22},{16,8},{18,... | collective-permute-start | bytes 1966088 | tf_op jit(solution)/shard_map/ppermute | solution.py:37
  25.5 25.2 %copy-start.7 = (bf16[128,2688]{1,0:T(8,128)(2,1)}, bf16[128,2688]{1,0:T(8,128)(2,1)S(1)}, u32[]{:S(2)}) copy-start(bf16[128,2688]{1,0:T(8,128)(2,1)S(1)} %collective-permute-done.4.refs_2_) | copy-start | bytes 2064388
  25.5 22.8 %copy-start.6 = (bf16[128,2688]{1,0:T(8,128)(2,1)}, bf16[128,2688]{1,0:T(8,128)(2,1)S(1)}, u32[]{:S(2)}) copy-start(bf16[128,2688]{1,0:T(8,128)(2,1)S(1)} %collective-permute-done.3.refs_3_.refs_2_) | copy-start | bytes 2064388
  25.6 25.2 %copy-start.8 = (bf16[128,2688]{1,0:T(8,128)(2,1)}, bf16[128,2688]{1,0:T(8,128)(2,1)S(1)}, u32[]{:S(2)}) copy-start(bf16[128,2688]{1,0:T(8,128)(2,1)S(1)} %collective-permute-done.refs_1_) | copy-start | bytes 2064388
  25.6 16.6 %collective-permute-start.9 = (bf16[2,10,32,512]{3,2,1,0:T(8,128)(2,1)}, bf16[2,10,32,512]{3,2,1,0:T(8,128)(2,1)S(1)}, u32[]{:S(2)}, u32[]{:S(2)}) collective-permute-start(bf16[2,10,32,512]{3,2,1,0:T(8,128)(2,1)} %get-tuple-element.61.refs_5_), channel_id=1, source_target_pairs={{0,4},{2,6},{4,0},{6,2},{8,12},{10,14},{12,8},{14,10},{16,20},{18,... | collective-permute-start | bytes 1966088 | tf_op jit(solution)/shard_map/ppermute | solution.py:22
  27.1 21.1 %collective-permute-start.8 = (bf16[128,2688]{1,0:T(8,128)(2,1)S(1)}, bf16[128,2688]{1,0:T(8,128)(2,1)}, u32[]{:S(2)}, u32[]{:S(2)}) collective-permute-start(bf16[128,2688]{1,0:T(8,128)(2,1)S(1)} %collective-permute-done.4.refs_2_), channel_id=1, source_target_pairs={{0,1},{1,0},{2,3},{3,2},{4,5},{5,4},{6,7},{7,6},{8,9},{9,8},{10,11... | collective-permute-start | bytes 2064392 | tf_op jit(solution)/shard_map/ppermute | solution.py:27
  27.6 20.6 %collective-permute-start.5 = (bf16[128,2688]{1,0:T(8,128)(2,1)S(1)}, bf16[128,2688]{1,0:T(8,128)(2,1)S(1)}, u32[]{:S(2)}, u32[]{:S(2)}) collective-permute-start(bf16[128,2688]{1,0:T(8,128)(2,1)S(1)} %collective-permute-done.4.refs_2_), channel_id=1, source_target_pairs={{0,2},{2,0},{4,6},{6,4},{8,10},{10,8},{12,14},{14,12},{16,18},{18,... | collective-permute-start | bytes 2064392 | tf_op jit(solution)/shard_map/ppermute | solution.py:22
  27.6 19.2 %collective-permute-start.6 = (bf16[2,10,32,512]{3,2,1,0:T(8,128)(2,1)}, bf16[2,10,32,512]{3,2,1,0:T(8,128)(2,1)S(1)}, u32[]{:S(2)}, u32[]{:S(2)}) collective-permute-start(bf16[2,10,32,512]{3,2,1,0:T(8,128)(2,1)} %collective-permute-done.2.refs_7_), channel_id=1, source_target_pairs={{0,0},{2,2},{4,4},{6,6},{8,16},{10,18},{12,20},{14,22},{16,8},{18,... | collective-permute-start | bytes 1966088 | tf_op jit(solution)/shard_map/ppermute | solution.py:37
  31.3 16.9 %collective-permute-start.7 = (bf16[2,10,32,512]{3,2,1,0:T(8,128)(2,1)S(1)}, bf16[2,10,32,512]{3,2,1,0:T(8,128)(2,1)S(1)}, u32[]{:S(2)}, u32[]{:S(2)}) collective-permute-start(bf16[2,10,32,512]{3,2,1,0:T(8,128)(2,1)S(1)} %collective-permute-done.1), channel_id=1, source_target_pairs={{0,8},{2,10},{4,12},{6,14},{8,0},{10,2},{12,4},{14,6},{16,24},{18,... | collective-permute-start | bytes 1966088 | tf_op jit(solution)/shard_map/ppermute | solution.py:22
  42.2 6.1 %copy-start.11 = (bf16[2,10,32,512]{3,2,1,0:T(8,128)(2,1)}, bf16[2,10,32,512]{3,2,1,0:T(8,128)(2,1)S(1)}, u32[]{:S(2)}) copy-start(bf16[2,10,32,512]{3,2,1,0:T(8,128)(2,1)S(1)} %collective-permute-done.9.refs_6_) | copy-start | bytes 1966084
  42.2 8.5 %collective-permute-start.13 = (bf16[128,2688]{1,0:T(8,128)(2,1)S(1)}, bf16[128,2688]{1,0:T(8,128)(2,1)S(1)}, u32[]{:S(2)}, u32[]{:S(2)}) collective-permute-start(bf16[128,2688]{1,0:T(8,128)(2,1)S(1)} %collective-permute-done.3.refs_3_.refs_2_), channel_id=1, source_target_pairs={{0,2},{2,0},{4,6},{6,4},{8,10},{10,8},{12,14},{14,12},{16,18},{18,... | collective-permute-start | bytes 2064392 | tf_op jit(solution)/shard_map/ppermute | solution.py:22
  48.2 2.6 %copy-start.9 = (bf16[128,2688]{1,0:T(8,128)(2,1)}, bf16[128,2688]{1,0:T(8,128)(2,1)S(1)}, u32[]{:S(2)}) copy-start(bf16[128,2688]{1,0:T(8,128)(2,1)S(1)} %collective-permute-done.5.refs_4_) | copy-start | bytes 2064388
  48.2 4.0 %collective-permute-start.14 = (bf16[128,2688]{1,0:T(8,128)(2,1)}, bf16[128,2688]{1,0:T(8,128)(2,1)}, u32[]{:S(2)}, u32[]{:S(2)}) collective-permute-start(bf16[128,2688]{1,0:T(8,128)(2,1)} %collective-permute-done.8.refs_5_), channel_id=1, source_target_pairs={{0,2},{2,0},{4,6},{6,4},{8,10},{10,8},{12,14},{14,12},{16,18},{18,... | collective-permute-start | bytes 2064392 | tf_op jit(solution)/shard_map/ppermute | solution.py:22
  48.3 17.4 %collective-permute-start.11 = (bf16[128,2560]{1,0:T(8,128)(2,1)}, bf16[128,2560]{1,0:T(8,128)(2,1)}, u32[]{:S(2)}, u32[]{:S(2)}) collective-permute-start(bf16[128,2560]{1,0:T(8,128)(2,1)} %refs_3_.1), channel_id=1, source_target_pairs={{0,1},{1,0},{2,3},{3,2},{4,5},{5,4},{6,7},{7,6},{8,9},{9,8},{10,11... | collective-permute-start | bytes 1966088 | tf_op jit(solution)/shard_map/ppermute | solution.py:27
  49.9 16.8 %collective-permute-start.10 = (bf16[2,10,32,512]{3,2,1,0:T(8,128)(2,1)S(1)}, bf16[2,10,32,512]{3,2,1,0:T(8,128)(2,1)S(1)}, u32[]{:S(2)}, u32[]{:S(2)}) collective-permute-start(bf16[2,10,32,512]{3,2,1,0:T(8,128)(2,1)S(1)} %collective-permute-done.6), channel_id=1, source_target_pairs={{0,8},{2,10},{4,12},{6,14},{8,0},{10,2},{12,4},{14,6},{16,24},{18,... | collective-permute-start | bytes 1966088 | tf_op jit(solution)/shard_map/ppermute | solution.py:22
  50.2 16.8 %collective-permute-start.12 = (bf16[2,10,32,512]{3,2,1,0:T(8,128)(2,1)}, bf16[2,10,32,512]{3,2,1,0:T(8,128)(2,1)}, u32[]{:S(2)}, u32[]{:S(2)}) collective-permute-start(bf16[2,10,32,512]{3,2,1,0:T(8,128)(2,1)} %collective-permute-done.2.refs_7_), channel_id=1, source_target_pairs={{0,4},{2,6},{4,0},{6,2},{8,12},{10,14},{12,8},{14,10},{16,20},{18,... | collective-permute-start | bytes 1966088 | tf_op jit(solution)/shard_map/ppermute | solution.py:22
  50.7 0.8 copy-start.10
  50.7 18.0 %collective-permute-start.16 = (bf16[2,10,32,512]{3,2,1,0:T(8,128)(2,1)}, bf16[2,10,32,512]{3,2,1,0:T(8,128)(2,1)}, u32[]{:S(2)}, u32[]{:S(2)}) collective-permute-start(bf16[2,10,32,512]{3,2,1,0:T(8,128)(2,1)} %get-tuple-element.61.refs_5_), channel_id=1, source_target_pairs={{0,2},{2,0},{4,6},{6,4},{8,10},{10,8},{12,14},{14,12},{16,18},{18,... | collective-permute-start | bytes 1966088 | tf_op jit(solution)/shard_map/ppermute | solution.py:22
  52.2 17.2 %copy-start.2 = (bf16[2,10,32,512]{3,2,1,0:T(8,128)(2,1)}, bf16[2,10,32,512]{3,2,1,0:T(8,128)(2,1)S(1)}, u32[]{:S(2)}) copy-start(bf16[2,10,32,512]{3,2,1,0:T(8,128)(2,1)S(1)} %select_select_fusion.1.refs_9_) | copy-start | bytes 1966084
  52.2 13.6 %copy-start.12 = (bf16[2,10,32,512]{3,2,1,0:T(8,128)(2,1)S(1)}, bf16[2,10,32,512]{3,2,1,0:T(8,128)(2,1)}, u32[]{:S(2)}) copy-start(bf16[2,10,32,512]{3,2,1,0:T(8,128)(2,1)} %copy-done.11) | copy-start | bytes 1966084
  52.2 17.3 %collective-permute-start.18 = (bf16[2,10,32,512]{3,2,1,0:T(8,128)(2,1)}, bf16[2,10,32,512]{3,2,1,0:T(8,128)(2,1)S(1)}, u32[]{:S(2)}, u32[]{:S(2)}) collective-permute-start(bf16[2,10,32,512]{3,2,1,0:T(8,128)(2,1)} %collective-permute-done.2.refs_7_), channel_id=1, source_target_pairs={{0,2},{2,0},{4,6},{6,4},{8,10},{10,8},{12,14},{14,12},{16,18},{18,... | collective-permute-start | bytes 1966088 | tf_op jit(solution)/shard_map/ppermute | solution.py:22
  65.8 3.6 %collective-permute-start.17 = (bf16[2,10,32,512]{3,2,1,0:T(8,128)(2,1)S(1)}, bf16[2,10,32,512]{3,2,1,0:T(8,128)(2,1)S(1)}, u32[]{:S(2)}, u32[]{:S(2)}) collective-permute-start(bf16[2,10,32,512]{3,2,1,0:T(8,128)(2,1)S(1)} %copy-done.12), channel_id=1, source_target_pairs={{0,2},{2,0},{4,6},{6,4},{8,10},{10,8},{12,14},{14,12},{16,18},{18,... | collective-permute-start | bytes 1966088 | tf_op jit(solution)/shard_map/ppermute | solution.py:22
  67.0 2.5 %collective-permute-start.19 = (bf16[2,10,32,512]{3,2,1,0:T(8,128)(2,1)}, bf16[2,10,32,512]{3,2,1,0:T(8,128)(2,1)S(1)}, u32[]{:S(2)}, u32[]{:S(2)}) collective-permute-start(bf16[2,10,32,512]{3,2,1,0:T(8,128)(2,1)} %collective-permute-done.12.refs_8_), channel_id=1, source_target_pairs={{0,2},{2,0},{4,6},{6,4},{8,10},{10,8},{12,14},{14,12},{16,18},{18,... | collective-permute-start | bytes 1966088 | tf_op jit(solution)/shard_map/ppermute | solution.py:22
  67.0 17.4 %collective-permute-start.20 = (bf16[256,1280]{1,0:T(8,128)(2,1)}, bf16[256,1280]{1,0:T(8,128)(2,1)S(1)}, u32[]{:S(2)}, u32[]{:S(2)}) collective-permute-start(bf16[256,1280]{1,0:T(8,128)(2,1)} %get-tuple-element.101), channel_id=1, source_target_pairs={{0,8},{2,10},{4,12},{6,14},{8,0},{10,2},{12,4},{14,6},{16,24},{18,... | collective-permute-start | bytes 1966088 | tf_op jit(solution)/shard_map/ppermute | solution.py:22
  68.8 17.0 %collective-permute-start.21 = (bf16[2,10,32,512]{3,2,1,0:T(8,128)(2,1)S(1)}, bf16[2,10,32,512]{3,2,1,0:T(8,128)(2,1)}, u32[]{:S(2)}, u32[]{:S(2)}) collective-permute-start(bf16[2,10,32,512]{3,2,1,0:T(8,128)(2,1)S(1)} %select_select_fusion.1.refs_9_), channel_id=1, source_target_pairs={{0,4},{2,6},{4,0},{6,2},{8,12},{10,14},{12,8},{14,10},{16,20},{18,... | collective-permute-start | bytes 1966088 | tf_op jit(solution)/shard_map/ppermute | solution.py:22
  69.4 39.9 %copy-start.3 = (bf16[2,10,32,512]{3,2,1,0:T(8,128)(2,1)}, bf16[2,10,32,512]{3,2,1,0:T(8,128)(2,1)S(1)}, u32[]{:S(2)}) copy-start(bf16[2,10,32,512]{3,2,1,0:T(8,128)(2,1)S(1)} %select_select_fusion.refs_15_) | copy-start | bytes 1966084
  69.4 38.7 %copy-start.5 = (bf16[256,1280]{1,0:T(8,128)(2,1)S(1)}, bf16[256,1280]{1,0:T(8,128)(2,1)}, u32[]{:S(2)}) copy-start(bf16[256,1280]{1,0:T(8,128)(2,1)} %get-tuple-element.101) | copy-start | bytes 1966084
  69.4 21.4 %copy-start.14 = (bf16[2,10,32,512]{3,2,1,0:T(8,128)(2,1)}, bf16[2,10,32,512]{3,2,1,0:T(8,128)(2,1)S(1)}, u32[]{:S(2)}) copy-start(bf16[2,10,32,512]{3,2,1,0:T(8,128)(2,1)S(1)} %collective-permute-done.17.refs_11_) | copy-start | bytes 1966084
  69.4 22.0 %collective-permute-start.15 = (bf16[2,10,32,512]{3,2,1,0:T(8,128)(2,1)S(1)}, bf16[2,10,32,512]{3,2,1,0:T(8,128)(2,1)}, u32[]{:S(2)}, u32[]{:S(2)}) collective-permute-start(bf16[2,10,32,512]{3,2,1,0:T(8,128)(2,1)S(1)} %select_select_fusion.1.refs_9_), channel_id=1, source_target_pairs={{0,2},{2,0},{4,6},{6,4},{8,10},{10,8},{12,14},{14,12},{16,18},{18,... | collective-permute-start | bytes 1966088 | tf_op jit(solution)/shard_map/ppermute | solution.py:22
  69.5 21.2 %copy-start.13 = (bf16[2,10,32,512]{3,2,1,0:T(8,128)(2,1)}, bf16[2,10,32,512]{3,2,1,0:T(8,128)(2,1)S(1)}, u32[]{:S(2)}) copy-start(bf16[2,10,32,512]{3,2,1,0:T(8,128)(2,1)S(1)} %collective-permute-done.18.refs_12_) | copy-start | bytes 1966084
  69.5 21.3 %copy-start.15 = (bf16[2,10,32,512]{3,2,1,0:T(8,128)(2,1)}, bf16[2,10,32,512]{3,2,1,0:T(8,128)(2,1)S(1)}, u32[]{:S(2)}) copy-start(bf16[2,10,32,512]{3,2,1,0:T(8,128)(2,1)S(1)} %collective-permute-done.19.refs_13_) | copy-start | bytes 1966084
  85.7 20.9 %collective-permute-start.24 = (bf16[256,1280]{1,0:T(8,128)(2,1)}, bf16[256,1280]{1,0:T(8,128)(2,1)}, u32[]{:S(2)}, u32[]{:S(2)}) collective-permute-start(bf16[256,1280]{1,0:T(8,128)(2,1)} %get-tuple-element.84), channel_id=1, source_target_pairs={{0,8},{2,10},{4,12},{6,14},{8,0},{10,2},{12,4},{14,6},{16,24},{18,... | collective-permute-start | bytes 1966088 | tf_op jit(solution)/shard_map/ppermute | solution.py:22
  88.2 24.7 %copy-start.4 = (bf16[256,1280]{1,0:T(8,128)(2,1)S(1)}, bf16[256,1280]{1,0:T(8,128)(2,1)}, u32[]{:S(2)}) copy-start(bf16[256,1280]{1,0:T(8,128)(2,1)} %get-tuple-element.99) | copy-start | bytes 1966084
  88.2 18.4 %collective-permute-start.23 = (bf16[256,1280]{1,0:T(8,128)(2,1)}, bf16[256,1280]{1,0:T(8,128)(2,1)S(1)}, u32[]{:S(2)}, u32[]{:S(2)}) collective-permute-start(bf16[256,1280]{1,0:T(8,128)(2,1)} %add_convert_fusion.3), channel_id=1, source_target_pairs={{0,0},{2,2},{4,4},{6,6},{8,16},{10,18},{12,20},{14,22},{16,8},{18,... | collective-permute-start | bytes 1966088 | tf_op jit(solution)/shard_map/ppermute | solution.py:37
  90.7 16.0 %collective-permute-start.22 = (bf16[2,10,32,512]{3,2,1,0:T(8,128)(2,1)}, bf16[2,10,32,512]{3,2,1,0:T(8,128)(2,1)}, u32[]{:S(2)}, u32[]{:S(2)}) collective-permute-start(bf16[2,10,32,512]{3,2,1,0:T(8,128)(2,1)} %collective-permute-done.21.refs_14_), channel_id=1, source_target_pairs={{0,2},{2,0},{4,6},{6,4},{8,10},{10,8},{12,14},{14,12},{16,18},{18,... | collective-permute-start | bytes 1966088 | tf_op jit(solution)/shard_map/ppermute | solution.py:22
  90.8 17.2 %collective-permute-start.25 = (bf16[2,10,32,512]{3,2,1,0:T(8,128)(2,1)S(1)}, bf16[2,10,32,512]{3,2,1,0:T(8,128)(2,1)}, u32[]{:S(2)}, u32[]{:S(2)}) collective-permute-start(bf16[2,10,32,512]{3,2,1,0:T(8,128)(2,1)S(1)} %select_select_fusion.refs_15_), channel_id=1, source_target_pairs={{0,4},{2,6},{4,0},{6,2},{8,12},{10,14},{12,8},{14,10},{16,20},{18,... | collective-permute-start | bytes 1966088 | tf_op jit(solution)/shard_map/ppermute | solution.py:22
  91.4 21.8 %collective-permute-start.26 = (bf16[2,10,32,512]{3,2,1,0:T(8,128)(2,1)S(1)}, bf16[2,10,32,512]{3,2,1,0:T(8,128)(2,1)S(1)}, u32[]{:S(2)}, u32[]{:S(2)}) collective-permute-start(bf16[2,10,32,512]{3,2,1,0:T(8,128)(2,1)S(1)} %select_select_fusion.refs_15_), channel_id=1, source_target_pairs={{0,2},{2,0},{4,6},{6,4},{8,10},{10,8},{12,14},{14,12},{16,18},{18,... | collective-permute-start | bytes 1966088 | tf_op jit(solution)/shard_map/ppermute | solution.py:22
  109.3 18.7 %collective-permute-start.29 = (bf16[256,1280]{1,0:T(8,128)(2,1)S(1)}, bf16[256,1280]{1,0:T(8,128)(2,1)S(1)}, u32[]{:S(2)}, u32[]{:S(2)}) collective-permute-start(bf16[256,1280]{1,0:T(8,128)(2,1)S(1)} %add_convert_fusion.1), channel_id=1, source_target_pairs={{0,0},{2,2},{4,4},{6,6},{8,16},{10,18},{12,20},{14,22},{16,8},{18,... | collective-permute-start | bytes 1966088 | tf_op jit(solution)/shard_map/ppermute | solution.py:37
  112.8 2.4 %collective-permute-start.27 = (bf16[2,10,32,512]{3,2,1,0:T(8,128)(2,1)}, bf16[2,10,32,512]{3,2,1,0:T(8,128)(2,1)S(1)}, u32[]{:S(2)}, u32[]{:S(2)}) collective-permute-start(bf16[2,10,32,512]{3,2,1,0:T(8,128)(2,1)} %collective-permute-done.25.refs_18_), channel_id=1, source_target_pairs={{0,2},{2,0},{4,6},{6,4},{8,10},{10,8},{12,14},{14,12},{16,18},{18,... | collective-permute-start | bytes 1966088 | tf_op jit(solution)/shard_map/ppermute | solution.py:22
  113.1 17.2 %copy-start = (f32[256,1280]{1,0:T(8,128)S(1)}, f32[256,1280]{1,0:T(8,128)}, u32[]{:S(2)}) copy-start(f32[256,1280]{1,0:T(8,128)} %get-tuple-element.105) | copy-start | bytes 3932164
  113.1 17.2 %collective-permute-start.28 = (bf16[256,1280]{1,0:T(8,128)(2,1)S(1)}, bf16[256,1280]{1,0:T(8,128)(2,1)S(1)}, u32[]{:S(2)}, u32[]{:S(2)}) collective-permute-start(bf16[256,1280]{1,0:T(8,128)(2,1)S(1)} %add_convert_fusion.2), channel_id=1, source_target_pairs={{0,8},{2,10},{4,12},{6,14},{8,0},{10,2},{12,4},{14,6},{16,24},{18,... | collective-permute-start | bytes 1966088 | tf_op jit(solution)/shard_map/ppermute | solution.py:22
  113.2 2.0 %copy-start.16 = (bf16[2,10,32,512]{3,2,1,0:T(8,128)(2,1)}, bf16[2,10,32,512]{3,2,1,0:T(8,128)(2,1)S(1)}, u32[]{:S(2)}) copy-start(bf16[2,10,32,512]{3,2,1,0:T(8,128)(2,1)S(1)} %collective-permute-done.26.refs_19_) | copy-start | bytes 1966084
  127.4 17.1 %collective-permute-start.30 = (bf16[128,2560]{1,0:T(8,128)(2,1)}, bf16[128,2560]{1,0:T(8,128)(2,1)S(1)}, u32[]{:S(2)}, u32[]{:S(2)}) collective-permute-start(bf16[128,2560]{1,0:T(8,128)(2,1)} %get-tuple-element.104), channel_id=1, source_target_pairs={{0,1},{1,0},{2,3},{3,2},{4,5},{5,4},{6,7},{7,6},{8,9},{9,8},{10,11... | collective-permute-start | bytes 1966088 | tf_op jit(solution)/shard_map/ppermute | solution.py:27
  130.3 14.1 %copy-start.1 = (f32[128,2560]{1,0:T(8,128)S(1)}, f32[128,2560]{1,0:T(8,128)}, u32[]{:S(2)}) copy-start(f32[128,2560]{1,0:T(8,128)} %get-tuple-element.103) | copy-start | bytes 3932164
  (1 other events, 0.8 us)

commit v2 on v1

v2 whole, which is shorter than its diff:
```python
import functools
import math

import jax
import jax.numpy as jnp
from jax import lax
from jax.experimental import pallas as pl
from jax.experimental.pallas import tpu as pltpu
from jax.sharding import PartitionSpec as P

ORDERS = 2
SHARD = 128
LANES = 128


def silu_slope(pre):
    sig = jax.nn.sigmoid(pre)
    return sig * (1.0 + pre * (1.0 - sig))


def swap(value, bit):
    size = lax.axis_size("dp")
    return lax.ppermute(value, "dp", [(i, i ^ bit) for i in range(size)])


def over_expert(value, step):
    size = lax.axis_size("expert")
    return lax.ppermute(value, "expert", [(i, (i + step) % size) for i in range(size)])


def over_even(value):
    planes = lax.axis_size("dp") // 4
    pairs = []
    for z in range(1, planes - 1, 2):
        for i in range(z * 4, z * 4 + 4):
            pairs += [(i, i + 4), (i + 4, i)]
    return lax.ppermute(value, "dp", pairs)


def pick(by_plane, plane):
    value = by_plane[-1]
    for z in range(len(by_plane) - 2, -1, -1):
        if by_plane[z] is not by_plane[z + 1]:
            value = jnp.where(plane <= z, by_plane[z], value)
    return value


def arrivals(planes):
    orders = []
    for z in range(planes):
        order = []
        for step in range(1, planes):
            for kind in (0, 1):
                offset = step if (z + kind) % 2 == 0 else -step
                if 0 <= z + offset < planes:
                    order.append((step, kind, offset))
        orders.append(order)
    return orders


def prepare_kernel(up_ref, down_ref, grad_ref, *refs):
    ids_ref, weights_ref, gate_ref, owner_ref, slot_ref, packed_ref, rows_ref, meta_ref = refs
    blocks, rows, cols = packed_ref.shape[1] // 2, packed_ref.shape[2], packed_ref.shape[3]
    for e in range(packed_ref.shape[0]):
        for b in range(blocks):
            packed_ref[e, b] = up_ref[e, b * rows : (b + 1) * rows, :]
            packed_ref[e, blocks + b] = down_ref[e, :, b * cols : (b + 1) * cols]
    tok, width = grad_ref.shape
    rows_ref[:, pl.ds(0, width)] = grad_ref[...]
    weights = weights_ref[...]
    high = weights.astype(jnp.bfloat16).astype(jnp.float32)
    meta_ref[...] = jnp.zeros_like(meta_ref)
    at = 0
    for value in (
        owner_ref[...].astype(jnp.float32),
        slot_ref[...].astype(jnp.float32),
        gate_ref[...],
        ids_ref[...].astype(jnp.float32),
        high,
        weights - high,
    ):
        meta_ref[pl.ds(at, value.shape[0]), :] = value
        at += value.shape[0]
    rows_ref[:, pl.ds(width, LANES)] = meta_ref[...].T.astype(jnp.bfloat16)


def prepare(up, down, grad_out, expert_ids, gate_weights, engram_gate, owner, slot):
    experts, _, hid = up.shape
    rows, width = down.shape[1:]
    tok = grad_out.shape[0]
    return pl.pallas_call(
        prepare_kernel,
        out_shape=(
            jax.ShapeDtypeStruct((experts, 2 * (width // hid), rows, hid), up.dtype),
            jax.ShapeDtypeStruct((tok, width + LANES), grad_out.dtype),
        ),
        scratch_shapes=[pltpu.VMEM((LANES, tok), jnp.float32)],
    )(up, down, grad_out, expert_ids.T, gate_weights.T, engram_gate.T, owner.T, slot.T)


def unstacked(refs):
    dims = min(ref.ndim for ref in refs)
    blocks = []
    for ref in refs:
        blocks += [ref] if ref.ndim == dims else [ref.at[i] for i in range(ref.shape[0])]
    return blocks


def folded(rows, width, shape):
    _, count, deep, wide = shape
    return (
        shape[0] == ORDERS
        and width % (wide // 2) == 0
        and rows % (2 * deep) == 0
        and (width // (wide // 2)) * (rows // (2 * deep)) == count
    )


def folds(rows, width, shape):
    _, _, deep, wide = shape
    for b in range(width // (wide // 2)):
        for h in range(rows // (2 * deep)):
            for u in range(2):
                yield (
                    b * (rows // (2 * deep)) + h,
                    u * (wide // 2),
                    (2 * h + u) * deep,
                    b * (wide // 2),
                )


def table_kernel(lookups, part, planes, offsets, place_ref, *refs):
    count = len(offsets)
    blocks = unstacked(refs[: -count - 2])
    outs, tokens, sem = refs[-count - 2 : -2], refs[-2], refs[-1]
    width = tokens.shape[1] - LANES
    half = width // ORDERS
    heads = lookups // ORDERS
    copies, at = [], 0
    for b, block in enumerate(blocks):
        copies.append(
            pltpu.make_async_copy(block, tokens.at[pl.ds(at, block.shape[0])], sem.at[b])
        )
        at += block.shape[0]
    for copy in copies:
        copy.start()
    for copy in copies:
        copy.wait()
    metas = [
        tokens[pl.ds(first, LANES), pl.ds(width, LANES)].astype(jnp.float32).T
        for first in range(0, at, LANES)
    ]
    meta = jnp.concatenate([m[: 3 * lookups] for m in metas], axis=1)
    key = meta[:lookups] * SHARD + meta[lookups : 2 * lookups]
    gate = meta[2 * lookups :]
    me, expert = place_ref[0], place_ref[1]
    plane = me // 4
    row = lax.broadcasted_iota(jnp.int32, (part, at), 0)
    size = heads * part
    for o in range(ORDERS):
        hits = []
        for offset in offsets:
            to = lax.rem(jnp.where(plane % 2 == 0, plane + offset, plane + planes - offset), planes)
            to = to * 4 + me % 4
            rows = (row + (to * SHARD + expert * part)).astype(jnp.float32)
            for j in range(o * heads, (o + 1) * heads):
                hit = jnp.where(rows == key[j : j + 1], gate[j : j + 1], 0.0)
                hits.append(hit.astype(jnp.bfloat16))
        sums = jnp.dot(
            jnp.concatenate(hits, axis=0),
            tokens[:, pl.ds(o * half, half)],
            preferred_element_type=jnp.float32,
        )
        for number, out in enumerate(outs):
            value = sums[number * size : (number + 1) * size].astype(out.dtype)
            if len(out.shape) == 2:
                out[pl.ds(o * size, size), :] = value
                continue
            deep, wide = out.shape[2], out.shape[3] // 2
            for block, lane, at, column in folds(size, half, out.shape):
                out[o, block, :, pl.ds(lane, wide)] = value[at : at + deep, column : column + wide]


def table_sums(blocks, place, lookups, part, offsets, shape):
    total = blocks[0].shape[1]
    planes = lax.axis_size("dp") // 4
    rows, half = lookups * part, (total - LANES) // ORDERS
    count = sum(block.shape[0] for block in blocks)
    return pl.pallas_call(
        functools.partial(table_kernel, lookups, part, planes, tuple(offsets)),
        out_shape=tuple(
            jax.ShapeDtypeStruct(shape, jnp.bfloat16 if offset else jnp.float32)
            for offset in offsets
        ),
        in_specs=[pl.BlockSpec(memory_space=pltpu.SMEM)]
        + [pl.BlockSpec(memory_space=pl.ANY)] * len(blocks),
        scratch_shapes=[
            pltpu.VMEM((count, total), jnp.bfloat16),
            pltpu.SemaphoreType.DMA((len(blocks),)),
        ],
        compiler_params=pltpu.CompilerParams(vmem_limit_bytes=56 << 20),
        cost_estimate=pl.CostEstimate(
            flops=2 * len(offsets) * rows * count * half,
            bytes_accessed=2 * count * total + 2 * len(offsets) * rows * half,
            transcendentals=0,
        ),
    )(place, *blocks)


def table_total_kernel(*refs):
    values, out = refs[:-1], refs[-1]
    if len(values[0].shape) == 2:
        out[...] = sum(value[...].astype(jnp.float32) for value in values)
        return
    size, width = out.shape[0] // ORDERS, out.shape[1]
    deep, wide = values[0].shape[2], values[0].shape[3] // 2
    for o in range(ORDERS):
        for block, lane, at, column in folds(size, width, values[0].shape):
            out[pl.ds(o * size + at, deep), pl.ds(column, wide)] = sum(
                value[o, block, :, pl.ds(lane, wide)].astype(jnp.float32) for value in values
            )


def table_total(values, rows, width):
    return pl.pallas_call(
        table_total_kernel,
        out_shape=jax.ShapeDtypeStruct((rows, width), jnp.float32),
        compiler_params=pltpu.CompilerParams(vmem_limit_bytes=32 << 20),
    )(*values)


def located(where, place_ref, planes):
    offsets, flip = where
    me = place_ref[0]
    at = jnp.bitwise_xor(me, flip)
    for z, offset in enumerate(offsets):
        if offset:
            at = at + jnp.where(me // 4 == z, 4 * offset, 0)
    return at


def token_copies(tokens, targets, sem):
    groups = len(tokens) // 2
    tok = tokens[0].shape[0]
    copies = []
    for number, token in enumerate(tokens):
        target, g = targets[number // groups], number % groups
        copies.append(
            pltpu.make_async_copy(
                token, target.at[pl.ds(g * tok, tok)], sem.at[number // groups, g]
            )
        )
    return copies


def row_chunk(groups, tok):
    return 2 * tok if groups % 2 == 0 else tok


def hidden_kernel(where, last, groups, planes, *refs):
    place_ref, tokens, refs = refs[0], refs[1 : 1 + 2 * groups], refs[1 + 2 * groups :]
    pieces, refs = unstacked(refs[:-9]), refs[-9:]
    turned_ref, pre_ref, back_ref, grad, inp, up, down, token_sem, piece_sem = refs
    experts, blocks, size, rows, hid = down.shape
    copies = token_copies(tokens, (grad, inp), token_sem)
    for number, piece in enumerate(pieces):
        at = located(where[number], place_ref, planes)
        copies.append(
            pltpu.make_async_copy(
                piece.at[:, pl.ds(0, blocks)],
                up.at[:, pl.ds(at * blocks, blocks)],
                piece_sem.at[0, number],
            )
        )
        copies.append(
            pltpu.make_async_copy(
                piece.at[:, pl.ds(blocks, blocks)], down.at[:, :, at], piece_sem.at[1, number]
            )
        )
    for copy in copies:
        copy.start()
    for copy in copies:
        copy.wait()
    pair = located(last, place_ref, planes) // 2
    up[:, pl.ds(pair * 2 * blocks, 2 * blocks)] = jnp.zeros(
        (experts, 2 * blocks, rows, hid), up.dtype
    )
    tok = tokens[0].shape[0]
    chunk = row_chunk(groups, tok)
    for e in range(experts):
        for b in range(blocks):
            block = up[e, b * size : (b + 1) * size].reshape(size * rows, hid)
            turned_ref[e, :, pl.ds(b * hid, hid)] = block.T
    for start in range(0, groups * tok, chunk):
        span = pl.ds(start, chunk)
        for e in range(experts):
            pre = jnp.zeros((chunk, hid), jnp.float32)
            back = jnp.zeros((chunk, hid), jnp.float32)
            for b in range(blocks):
                cols = pl.ds(b * hid, hid)
                pre += jnp.dot(
                    inp[span, cols],
                    up[e, b * size : (b + 1) * size].reshape(size * rows, hid),
                    preferred_element_type=jnp.float32,
                )
                back += lax.dot_general(
                    grad[span, cols],
                    down[e, b].reshape(size * rows, hid),
                    (((1,), (1,)), ((), ())),
                    preferred_element_type=jnp.float32,
                )
            pre_ref[span, pl.ds(e * hid, hid)] = pre
            back_ref[span, pl.ds(e * hid, hid)] = back


def slab_of(blocks, rows):
    held = 2 * blocks * rows
    return held, -(-(LANES - math.gcd(held, LANES) + held) // LANES) * LANES


def result_kernel(last, groups, planes, lookups, top, *refs):
    place_ref, tokens, refs = refs[0], refs[1 : 1 + 2 * groups], refs[1 + 2 * groups :]
    turned_ref, first_ref, second_ref, pre_ref, back_ref, own_ref, rest_ref, *refs = refs
    grad, part, up, down, turned, pre_part, back_part, token_sem, piece_sem, turned_sem = refs
    tok, width = own_ref.shape
    experts, blocks, per, rows, hid = down.shape
    expert = place_ref[1]
    pair = located(last, place_ref, planes) // 2
    held, slab = slab_of(blocks, rows)
    base = pl.multiple_of(pair * held // LANES * LANES, LANES)
    skip = lax.rem(pair * held, LANES)

    up[...] = jnp.zeros_like(up)
    copies = token_copies(
        list(tokens[:groups]) + [token.at[:, pl.ds(base, slab)] for token in tokens[groups:]],
        (grad, part),
        token_sem,
    )
    for number, piece in enumerate((first_ref, second_ref)):
        at = located((last[0], last[1] + number), place_ref, planes)
        copies.append(
            pltpu.make_async_copy(
                piece.at[:, pl.ds(0, blocks)],
                up.at[:, pl.ds(skip // rows + lax.rem(at, 2) * blocks, blocks)],
                piece_sem.at[0, number],
            )
        )
        copies.append(
            pltpu.make_async_copy(
                piece.at[:, pl.ds(blocks, blocks)],
                down.at[:, :, lax.rem(at, per)],
                piece_sem.at[1, number],
            )
        )
    copies.append(pltpu.make_async_copy(pre_ref, pre_part, piece_sem.at[0, 2]))
    copies.append(pltpu.make_async_copy(back_ref, back_part, piece_sem.at[1, 2]))
    turns = [
        pltpu.make_async_copy(
            turned_ref.at[:, :, pl.ds(b * hid, hid)],
            turned.at[:, :, pl.ds(b * hid, hid)],
            turned_sem.at[b],
        )
        for b in range(blocks)
    ]
    for copy in copies + turns:
        copy.start()
    for copy in copies:
        copy.wait()

    hid_slab = pl.multiple_of(pair * 2 // per * LANES, LANES)
    hid_skip = lax.rem(pair * 2, per) * rows
    chunk = row_chunk(groups, tok)
    at = 3 * lookups
    lane = lax.broadcasted_iota(jnp.int32, (chunk, slab), 1)
    lane = jnp.logical_and(lane >= skip, lane < skip + held)
    hid_lane = lax.broadcasted_iota(jnp.int32, (chunk, LANES), 1)
    hid_lane = jnp.logical_and(hid_lane >= hid_skip, hid_lane < hid_skip + 2 * rows)
    for start in range(0, groups * tok, chunk):
        span = pl.ds(start, chunk)
        meta = grad[span, pl.ds(width, LANES)].astype(jnp.float32)
        mine = jnp.where(lane, part[span, :].astype(jnp.float32), 0.0).astype(jnp.bfloat16)
        slopes = []
        for e in range(experts):
            units = pl.ds(e * hid, hid)
            pre = pre_part[span, units] + jnp.dot(
                mine, up[e].reshape(slab, hid), preferred_element_type=jnp.float32
            )
            late = jnp.zeros((chunk, LANES), jnp.float32)
            for b in range(blocks):
                late += lax.dot_general(
                    grad[span, pl.ds(b * hid, hid)],
                    down[e, b].reshape(LANES, hid),
                    (((1,), (1,)), ((), ())),
                    preferred_element_type=jnp.float32,
                )
            lanes = pl.ds(pl.multiple_of(e * hid + hid_slab, LANES), LANES)
            back_part[span, lanes] = jnp.where(hid_lane, late, back_part[span, lanes])
            weight = jnp.zeros((chunk, 1), jnp.float32)
            number = (expert * experts + e).astype(jnp.float32)
            for k in range(top):
                value = meta[:, at + top + k : at + top + k + 1]
                value += meta[:, at + 2 * top + k : at + 2 * top + k + 1]
                weight += jnp.where(meta[:, at + k : at + k + 1] == number, value, 0.0)
            slope = back_part[span, units] * silu_slope(pre) * weight
            slopes.append(slope.astype(jnp.bfloat16))
        for b in range(blocks):
            cols = pl.ds(b * hid, hid)
            if start == 0:
                turns[b].wait()
            total = jnp.zeros((chunk, hid), jnp.float32)
            for e in range(experts):
                total += jnp.dot(
                    slopes[e], turned[e, :, cols], preferred_element_type=jnp.float32
                )
            if start == 0:
                own_ref[:, cols] = total[:tok]
                if chunk > tok:
                    rest_ref[pl.ds(0, chunk - tok), cols] = total[tok:].astype(jnp.bfloat16)
            else:
                rest_ref[pl.ds(start - tok, chunk), cols] = total.astype(jnp.bfloat16)
        late = jnp.zeros((chunk, slab), jnp.float32)
        for e in range(experts):
            late += lax.dot_general(
                slopes[e],
                up[e].reshape(slab, hid),
                (((1,), (1,)), ((), ())),
                preferred_element_type=jnp.float32,
            )
        cols = pl.ds(base, slab)
        if start == 0:
            own_ref[:, cols] += late[:tok]
            late, span = late[tok:], pl.ds(0, chunk - tok)
        else:
            span = pl.ds(start - tok, chunk)
        if start or chunk > tok:
            known = rest_ref[span, cols].astype(jnp.float32)
            rest_ref[span, cols] = (known + late).astype(jnp.bfloat16)


def hidden_layers(grads, inputs, pieces, last, place):
    groups = len(grads)
    tok, width = inputs[0].shape
    experts, blocks2, rows, hid = pieces[0][0].shape[-4:]
    blocks = blocks2 // 2
    dp = lax.axis_size("dp")
    where = tuple(entry for _, entries in pieces for entry in entries)
    any_space, vmem = pl.BlockSpec(memory_space=pl.ANY), pl.BlockSpec(memory_space=pltpu.VMEM)
    return pl.pallas_call(
        functools.partial(hidden_kernel, where, last, groups, dp // 4),
        out_shape=(
            jax.ShapeDtypeStruct((experts, hid, width), jnp.bfloat16),
            jax.ShapeDtypeStruct((groups * tok, experts * hid), jnp.float32),
            jax.ShapeDtypeStruct((groups * tok, experts * hid), jnp.float32),
        ),
        in_specs=[pl.BlockSpec(memory_space=pltpu.SMEM)]
        + [any_space] * (2 * groups + len(pieces)),
        out_specs=(vmem, vmem, vmem),
        scratch_shapes=[
            pltpu.VMEM((groups * tok, width + LANES), jnp.bfloat16),
            pltpu.VMEM((groups * tok, width), jnp.bfloat16),
            pltpu.VMEM((experts, dp * blocks, rows, hid), jnp.bfloat16),
            pltpu.VMEM((experts, blocks, dp, rows, hid), jnp.bfloat16),
            pltpu.SemaphoreType.DMA((2, groups)),
            pltpu.SemaphoreType.DMA((2, len(where))),
        ],
        compiler_params=pltpu.CompilerParams(vmem_limit_bytes=56 << 20),
        cost_estimate=pl.CostEstimate(
            flops=4 * groups * tok * width * hid * experts,
            bytes_accessed=6 * experts * width * hid + 8 * groups * tok * width,
            transcendentals=0,
        ),
    )(place, *grads, *inputs, *[piece[0] for piece in pieces])


def expert_results(grads, inputs, hidden, first, second, last, place, lookups, top):
    groups = len(grads)
    tok, width = inputs[0].shape
    experts, blocks2, rows, hid = first.shape
    blocks = blocks2 // 2
    dp = lax.axis_size("dp")
    turned, pre, back = hidden
    rest_rows = max(groups - 1, 1) * tok
    slab = slab_of(blocks, rows)[1]
    any_space, vmem = pl.BlockSpec(memory_space=pl.ANY), pl.BlockSpec(memory_space=pltpu.VMEM)
    return pl.pallas_call(
        functools.partial(result_kernel, last, groups, dp // 4, lookups, top),
        out_shape=(
            jax.ShapeDtypeStruct((tok, width), jnp.float32),
            jax.ShapeDtypeStruct((rest_rows, width), jnp.bfloat16),
        ),
        in_specs=[pl.BlockSpec(memory_space=pltpu.SMEM)] + [any_space] * (2 * groups + 5),
        out_specs=(vmem, vmem),
        scratch_shapes=[
            pltpu.VMEM((groups * tok, width + LANES), jnp.bfloat16),
            pltpu.VMEM((groups * tok, slab), jnp.bfloat16),
            pltpu.VMEM((experts, slab // rows, rows, hid), jnp.bfloat16),
            pltpu.VMEM((experts, blocks, LANES // rows, rows, hid), jnp.bfloat16),
            pltpu.VMEM(turned.shape, jnp.bfloat16),
            pltpu.VMEM(pre.shape, jnp.float32),
            pltpu.VMEM(back.shape, jnp.float32),
            pltpu.SemaphoreType.DMA((2, groups)),
            pltpu.SemaphoreType.DMA((2, 3)),
            pltpu.SemaphoreType.DMA((blocks,)),
        ],
        compiler_params=pltpu.CompilerParams(vmem_limit_bytes=60 << 20),
        cost_estimate=pl.CostEstimate(
            flops=2 * groups * tok * width * hid * experts,
            bytes_accessed=2 * experts * width * hid + 12 * groups * tok * width,
            transcendentals=groups * tok * hid * experts,
        ),
    )(place, *grads, *inputs, turned, first, second, pre, back)


def per_device(
    grad_out,
    saved_input,
    expert_ids,
    gate_weights,
    up_weight,
    down_weight,
    engram_gate,
    memory_owner,
    memory_slot,
):
    tok, width = grad_out.shape
    lookups, top = engram_gate.shape[1], expert_ids.shape[1]
    groups = lax.axis_size("expert")
    planes = lax.axis_size("dp") // 4
    part = SHARD // groups
    me = lax.axis_index("dp")
    plane = me // 4
    place = jnp.stack([me, lax.axis_index("expert")]).astype(jnp.int32)
    others = range(1, groups)
    fence = lax.optimization_barrier

    packed, rows = prepare(
        up_weight,
        down_weight,
        grad_out,
        expert_ids,
        gate_weights,
        engram_gate,
        memory_owner,
        memory_slot,
    )
    orders = arrivals(planes)
    came = {}
    zero = (0,) * planes

    def along(step, line):
        even = over_even(line[0]) if step < planes - 1 else None
        return swap(line[1], 4), even

    def arrival(number):
        by_plane = [came[order[number][0]][order[number][1]] for order in orders]
        offsets = tuple(order[number][2] for order in orders)
        return pick(by_plane, plane), offsets

    def plus(share, came_in):
        return (share.astype(jnp.float32) + came_in.astype(jnp.float32)).astype(jnp.bfloat16)

    def reduce(step, sums):
        odd, even = partials[planes - step], partials[step]
        if step > 1 and sums[1] is not None:
            odd = plus(odd, sums[1])
        even = over_even(plus(even, sums[0])) if step > 1 else None
        return swap(odd, 4), even

    half = width // ORDERS
    fits = planes > 3 and folded(lookups // ORDERS * part, half, packed.shape)
    shape = packed.shape if fits else (lookups * part, half)


    rows_x = swap(rows, 2)
    got = [over_expert(rows, step) for step in others]
    came[1] = along(1, (packed, packed))
    late, rows_x = fence((packed, rows_x))
    rows_x, got, near = fence((rows_x, got, swap(rows, 1)))
    grads = [rows] + got
    far = [over_expert(rows_x, step) for step in others]
    near = [near, swap(rows_x, 1)]
    if planes > 2:
        came[2] = along(2, came[1])
        got, far, near, came[2] = fence((got, far, near, came[2]))
    blocks = [rows, rows_x, *near, *got, *far]
    for block in got + far:
        blocks += [swap(block[: tok // 2], 1), swap(block[tok // 2 :], 1)]
    partials = table_sums(blocks, place, lookups, part, range(planes), shape)
    for step in range(3, planes - 1 if fits else planes):
        came[step] = along(step, came[step - 1])
    if fits:
        ends = jnp.logical_or(plane == 0, plane == planes - 1)
        met = swap(jnp.where(ends, partials[planes - 1], came[planes - 2][1]), 4)
        came[planes - 1] = (met, None)

    value, where = arrival(0)
    pair = jnp.stack([late, value])
    pair_x = swap(pair, 2)
    later, far = fence((saved_input, far))
    inputs = [over_expert(later, step) for step in others]

    pieces = [(pair, ((zero, 0), (where, 0)))]
    passed, passed_at = pair_x, ((zero, 2), (where, 2))
    todo, near, near_at = pieces[:1], [], []
    sums = ()

    def across(entries):
        return [
            (swap(array, 1), tuple((offsets, flip + 1) for offsets, flip in at))
            for array, at in entries
        ]

    for number in range(2, planes):
        value, where = arrival(number - 1)
        if number == 2:
            partials, value, passed = fence((partials, value, passed))
        else:
            value, passed, inputs = fence((value, passed, inputs))
        pieces += [(passed, passed_at)] + list(zip(near, near_at))
        todo += [(passed, passed_at)]
        moved = across(todo)
        near, near_at = [array for array, _ in moved], [at for _, at in moved]
        passed, passed_at = swap(value, 2), ((where, 2),)
        pieces += [(value, ((where, 0),))]
        todo = [(value, ((where, 0),))]
        if number + 1 == planes:
            moved = across(todo)
            near, near_at = near + [moved[0][0]], near_at + [moved[0][1]]
            todo = []
    pieces += list(zip(near, near_at)) + across(todo)
    inputs = [saved_input] + inputs
    last = (passed_at[0][0], 2)
    hidden = hidden_layers(grads, inputs, pieces, last, place)

    if fits:
        sums = met, None
    for step in range(2 if fits else 1, planes - 1):
        sums = reduce(step, sums)
    sums, hidden, passed = fence((sums, hidden, passed))
    total, rest = expert_results(
        grads, inputs, hidden, passed, swap(passed, 1), last, place, lookups, top
    )
    total, sums = fence((total, sums))
    if planes > 1:
        sums = reduce(planes - 1, sums)
    for back in others:
        value = rest[(back - 1) * tok : back * tok]
        total = total + over_expert(value, groups - back).astype(jnp.float32)
    sums = [partials[0]] + [came_in for came_in in sums[::-1] if came_in is not None]
    table = table_total(sums, lookups * part, half)
    return total.astype(jnp.bfloat16), table.reshape(lookups, part, width // ORDERS)


def solution(mesh):
    return jax.shard_map(
        per_device,
        mesh=mesh,
        in_specs=(
            P(("dp", "expert"), None),
            P(("dp", "expert"), None),
            P(("dp", "expert"), None),
            P(("dp", "expert"), None),
            P("expert", "dp", None),
            P("expert", "dp", None),
            P(("dp", "expert"), None),
            P(("dp", "expert"), None),
            P(("dp", "expert"), None),
        ),
        out_specs=(P(("dp", "expert"), None), P(None, ("dp", "expert"), None)),
        check_vma=False,
    )
```

time: 148 us -> 134 us (0.905)
  waiting for transfers between devices: 88.7 us -> 62.5 us
  Pallas kernels: 21.8 us -> 33.4 us
  local copies, waits for them, and re-layouts: 1.65 us -> 5.45 us
    ppermute x4, waiting for transfers between devices: 22.7 us -> 9.53 us  [over_even(): return lax.ppermute(value, 'dp', pairs)]
    pallas_call x2 -> x4, Pallas kernels: 19.3 us -> 30.9 us  [the longest x1 11.1 us: hidden_layers(): pl.pallas_call(functools.partial(hidden_kernel, where, last, groups, dp /...]
    ppermute x23 -> x21, waiting for transfers between devices: 47.8 us -> 41.1 us  [swap(): return lax.ppermute(value, 'dp', [(i, i ^ bit) for i in range(size)])]
    ppermute x4, waiting for transfers between devices: 18.3 us -> 11.9 us  [over_expert(): lax.ppermute(value, 'expert', [(i, (i + step) % size) for i in range(size)])]
    ppermute x4, starting transfers between devices: 14.2 us -> 11.7 us  [over_even(): return lax.ppermute(value, 'dp', pairs)]
    slice x0 -> x2, local copies, waits for them, and re-layouts: none -> 1.91 us  [per_device(): blocks += [swap(block[:tok // 2], 1), swap(block[tok // 2:], 1)]]
    unnamed x36 -> x60, local copies, waits for them, and re-layouts: 1.65 us -> 3.54 us
    ppermute x23 -> x21, starting transfers between devices: 7.35 us -> 7.75 us  [swap(): return lax.ppermute(value, 'dp', [(i, i ^ bit) for i in range(size)])]
  transfers between devices with their start and end apart: 31 -> 29, of which waited for: 15 -> 18; matrix products, arithmetic and copies ran while one was open for 4% -> 6% of each run, Pallas kernels for 13% -> 14%
where the time goes in v2:
time: 134 us; the launch traced here: 132 us
  waiting for transfers between devices  62.5 us (47%)
  Pallas kernels  33.4 us (25%)
  starting transfers between devices  24.5 us (18%)
  other arithmetic  5.63 us (4%)
  local copies, waits for them, and re-layouts  5.45 us (4%)
    ppermute x21, waiting for transfers between devices, swap(): return lax.ppermute(value, 'dp', [(i, i ^ bit) for i in range(size)])  41.1 us
    ppermute x4, waiting for transfers between devices, over_expert(): lax.ppermute(value, 'expert', [(i, (i + step) % size) for i in range(size)])  11.9 us
    ppermute x4, starting transfers between devices, over_even(): return lax.ppermute(value, 'dp', pairs)  11.7 us
    pallas_call x1, Pallas kernels, hidden_layers(): pl.pallas_call(functools.partial(hidden_kernel, where, last, groups, dp /...  11.1 us
    pallas_call x1, Pallas kernels, expert_results(): pl.pallas_call(functools.partial(result_kernel, last, groups, dp // 4, lo...  10.9 us
    ppermute x4, waiting for transfers between devices, over_even(): return lax.ppermute(value, 'dp', pairs)  9.53 us
    pallas_call x1, Pallas kernels, table_sums(): pl.pallas_call(functools.partial(table_kernel, lookups, part, planes, tup...  7.77 us
    ppermute x21, starting transfers between devices, swap(): return lax.ppermute(value, 'dp', [(i, i ^ bit) for i in range(size)])  7.75 us
  transfers between devices with their start and end apart: 29, of which 18 were waited for; matrix products, arithmetic and copies ran while one was open for 6% of the time, Pallas kernels for 14%

profile of v2, /device:TPU:10, one launch (start us, length us, event | category | flops | bytes accessed | tf_op | source)
XLA Modules:
  0.0 132.5 jit_solution(15528321148403870068)
XLA Ops:
  0.6 2.5 %shard_map.104 = (bf16[2,10,32,512]{3,2,1,0:T(8,128)(2,1)}, bf16[128,2688]{1,0:T(8,128)(2,1)}) custom-call(bf16[2,160,512]{2,1,0:T(8,128)(2,1)} %up_ref.1, bf16[2,32,2560]{2,1,0:T(8,128)(2,1)} %down_ref.1, bf16[128,2560]{1,0:T(8,128)(2,1)} %grad_ref.1, s32[2,128]{1,0:T(2,128)} %bitcast.16, f32[2,128]{1,0:T(2,128)} %bitcast.17, f32[4,128]{1,0:T(4,128)} %bitcast.13, ...), custom_call_target="tpu_custom_call" | custom-call | tf_op jit(solution)/shard_map/pallas_call | solution.py:91
  3.1 0.5 collective-permute-start
  3.6 1.5 %collective-permute-start.1 = (bf16[128,2688]{1,0:T(8,128)(2,1)}, bf16[128,2688]{1,0:T(8,128)(2,1)S(1)}, u32[]{:S(2)}, u32[]{:S(2)}) collective-permute-start(bf16[128,2688]{1,0:T(8,128)(2,1)} %get-tuple-element.43.refs_0_.refs_1_), channel_id=1, source_target_pairs={{0,1},{1,0},{2,3},{3,2},{4,5},{5,4},{6,7},{7,6},{8,9},{9,8},{10,11... | collective-permute-start | bytes 2064392 | tf_op jit(solution)/shard_map/ppermute | solution.py:28
  5.1 3.5 %collective-permute-start.5 = (bf16[2,10,32,512]{3,2,1,0:T(8,128)(2,1)}, bf16[2,10,32,512]{3,2,1,0:T(8,128)(2,1)S(1)}, u32[]{:S(2)}, u32[]{:S(2)}) collective-permute-start(bf16[2,10,32,512]{3,2,1,0:T(8,128)(2,1)} %get-tuple-element.59), channel_id=1, source_target_pairs={{8,16},{16,8},{10,18},{18,10},{12,20},{20,12},{14,22},{22,14},{9,1... | collective-permute-start | bytes 1966088 | tf_op jit(solution)/shard_map/ppermute | solution.py:37
  8.7 11.8 %collective-permute-done.refs_1_ = bf16[128,2688]{1,0:T(8,128)(2,1)S(1)} collective-permute-done((bf16[128,2688]{1,0:T(8,128)(2,1)}, bf16[128,2688]{1,0:T(8,128)(2,1)S(1)}, u32[]{:S(2)}, u32[]{:S(2)}) %collective-permute-start) | collective-permute-done | bytes 688160 | tf_op jit(solution)/shard_map/ppermute | solution.py:23
  20.5 0.3 collective-permute-done.1.refs_4_.refs_2_
  20.7 1.6 %collective-permute-start.3 = (bf16[128,2688]{1,0:T(8,128)(2,1)S(1)}, bf16[128,2688]{1,0:T(8,128)(2,1)S(1)}, u32[]{:S(2)}, u32[]{:S(2)}) collective-permute-start(bf16[128,2688]{1,0:T(8,128)(2,1)S(1)} %collective-permute-done.refs_1_), channel_id=1, source_target_pairs={{0,1},{1,0},{2,3},{3,2},{4,5},{5,4},{6,7},{7,6},{8,9},{9,8},{10,11... | collective-permute-start | bytes 2064392 | tf_op jit(solution)/shard_map/ppermute | solution.py:28
  22.3 2.1 %collective-permute-done.5 = bf16[2,10,32,512]{3,2,1,0:T(8,128)(2,1)S(1)} collective-permute-done((bf16[2,10,32,512]{3,2,1,0:T(8,128)(2,1)}, bf16[2,10,32,512]{3,2,1,0:T(8,128)(2,1)S(1)}, u32[]{:S(2)}, u32[]{:S(2)}) %collective-permute-start.5) | collective-permute-done | bytes 655392 | tf_op jit(solution)/shard_map/ppermute | solution.py:37
  24.4 1.4 %collective-permute-done.7 = bf16[2,10,32,512]{3,2,1,0:T(8,128)(2,1)S(1)} collective-permute-done((bf16[2,10,32,512]{3,2,1,0:T(8,128)(2,1)}, bf16[2,10,32,512]{3,2,1,0:T(8,128)(2,1)S(1)}, u32[]{:S(2)}, u32[]{:S(2)}) %collective-permute-start.7) | collective-permute-done | bytes 655392 | tf_op jit(solution)/shard_map/ppermute | solution.py:23
  25.8 2.3 %collective-permute-start.8 = (bf16[2,10,32,512]{3,2,1,0:T(8,128)(2,1)S(1)}, bf16[2,10,32,512]{3,2,1,0:T(8,128)(2,1)S(1)}, u32[]{:S(2)}, u32[]{:S(2)}) collective-permute-start(bf16[2,10,32,512]{3,2,1,0:T(8,128)(2,1)S(1)} %collective-permute-done.7), channel_id=1, source_target_pairs={{8,16},{16,8},{10,18},{18,10},{12,20},{20,12},{14,22},{22,14},{9,1... | collective-permute-start | bytes 1966088 | tf_op jit(solution)/shard_map/ppermute | solution.py:37
  28.1 1.2 pad_maximum_fusion.refs_5_
  29.4 1.6 %collective-permute-start.14 = (bf16[2,2,10,32,512]{4,3,2,1,0:T(8,128)(2,1)S(1)}, bf16[2,2,10,32,512]{4,3,2,1,0:T(8,128)(2,1)}, u32[]{:S(2)}, u32[]{:S(2)}) collective-permute-start(bf16[2,2,10,32,512]{4,3,2,1,0:T(8,128)(2,1)S(1)} %pad_maximum_fusion.refs_5_), channel_id=1, source_target_pairs={{0,4},{2,6},{4,0},{6,2},{8,12},{10,14},{12,8},{14,10},{16,20},{18,... | collective-permute-start | bytes 3932168 | tf_op jit(solution)/shard_map/ppermute | solution.py:23
  30.9 9.8 %collective-permute-done.6 = bf16[2,10,32,512]{3,2,1,0:T(8,128)(2,1)S(1)} collective-permute-done((bf16[2,10,32,512]{3,2,1,0:T(8,128)(2,1)S(1)}, bf16[2,10,32,512]{3,2,1,0:T(8,128)(2,1)S(1)}, u32[]{:S(2)}, u32[]{:S(2)}) %collective-permute-start.6) | collective-permute-done | bytes 655392 | tf_op jit(solution)/shard_map/ppermute | solution.py:23
  40.8 2.9 %collective-permute-done.8 = bf16[2,10,32,512]{3,2,1,0:T(8,128)(2,1)S(1)} collective-permute-done((bf16[2,10,32,512]{3,2,1,0:T(8,128)(2,1)S(1)}, bf16[2,10,32,512]{3,2,1,0:T(8,128)(2,1)S(1)}, u32[]{:S(2)}, u32[]{:S(2)}) %collective-permute-start.8) | collective-permute-done | bytes 655392 | tf_op jit(solution)/shard_map/ppermute | solution.py:37
  43.7 1.0 fusion
  44.7 0.5 collective-permute-start.12
  45.2 0.9 fusion.1
  46.2 0.5 collective-permute-start.9
  46.7 0.6 pad_add_fusion.place_ref.refs_0_
  47.5 0.5 collective-permute-start.16
  48.1 0.6 collective-permute-done.9.refs_6_
  48.8 7.8 %shard_map.105 = (f32[2,10,32,512]{3,2,1,0:T(8,128)}, bf16[2,10,32,512]{3,2,1,0:T(8,128)(2,1)}, bf16[2,10,32,512]{3,2,1,0:T(8,128)(2,1)}, bf16[2,10,32,512]{3,2,1,0:T(8,128)(2,1)}) custom-call(s32[2]{0:T(128)} %pad_add_fusion.place_ref.refs_0_, bf16[128,2688]{1,0:T(8,128)(2,1)} %get-tuple-element.43.refs_0_.refs_1_, bf16[128,2688]{1,0:T(8,128)(2,1)} %copy-done.26, ...), custom_call_target="tpu_custom_call" | custom-call | flops 2684354560 | bytes 8126464 | tf_op jit(solution)/shard_map/pallas_call | solution.py:189
  56.8 0.9 copy-done.18
  57.9 1.5 %collective-permute-done.14.refs_6_ = bf16[2,2,10,32,512]{4,3,2,1,0:T(8,128)(2,1)} collective-permute-done((bf16[2,2,10,32,512]{4,3,2,1,0:T(8,128)(2,1)S(1)}, bf16[2,2,10,32,512]{4,3,2,1,0:T(8,128)(2,1)}, u32[]{:S(2)}, u32[]{:S(2)}) %collective-permute-start.14) | collective-permute-done | bytes 1310752 | tf_op jit(solution)/shard_map/ppermute | solution.py:23
  59.5 1.5 %collective-permute-start.15 = (bf16[2,10,32,512]{3,2,1,0:T(8,128)(2,1)S(1)}, bf16[2,10,32,512]{3,2,1,0:T(8,128)(2,1)S(1)}, u32[]{:S(2)}, u32[]{:S(2)}) collective-permute-start(bf16[2,10,32,512]{3,2,1,0:T(8,128)(2,1)S(1)} %select_select_fusion.refs_7_), channel_id=1, source_target_pairs={{0,4},{2,6},{4,0},{6,2},{8,12},{10,14},{12,8},{14,10},{16,20},{18,... | collective-permute-start | bytes 1966088 | tf_op jit(solution)/shard_map/ppermute | solution.py:23
  61.0 12.6 %collective-permute-done.13 = bf16[2,10,32,512]{3,2,1,0:T(8,128)(2,1)S(1)} collective-permute-done((bf16[2,10,32,512]{3,2,1,0:T(8,128)(2,1)S(1)}, bf16[2,10,32,512]{3,2,1,0:T(8,128)(2,1)S(1)}, u32[]{:S(2)}, u32[]{:S(2)}) %collective-permute-start.13) | collective-permute-done | bytes 655392 | tf_op jit(solution)/shard_map/ppermute | solution.py:23
  73.6 1.2 collective-permute-done.15.refs_8_
  74.8 0.5 collective-permute-start.23
  75.3 2.2 %add_convert_fusion.3 = bf16[2,10,32,512]{3,2,1,0:T(8,128)(2,1)} fusion(bf16[2,10,32,512]{3,2,1,0:T(8,128)(2,1)S(1)} %collective-permute-done.13, bf16[2,10,32,512]{3,2,1,0:T(8,128)(2,1)} %get-tuple-element.63), kind=kLoop, calls=%fused_computation.4 | loop fusion | flops 1310720 | bytes 1966080 | tf_op jit(solution)/shard_map/convert_element_type | solution.py:560
  77.5 0.7 collective-permute-start.17
  78.2 2.4 %collective-permute-start.18 = (bf16[2,10,32,512]{3,2,1,0:T(8,128)(2,1)}, bf16[2,10,32,512]{3,2,1,0:T(8,128)(2,1)S(1)}, u32[]{:S(2)}, u32[]{:S(2)}) collective-permute-start(bf16[2,10,32,512]{3,2,1,0:T(8,128)(2,1)} %add_convert_fusion.3), channel_id=1, source_target_pairs={{8,16},{16,8},{10,18},{18,10},{12,20},{20,12},{14,22},{22,14},{9,1... | collective-permute-start | bytes 1966088 | tf_op jit(solution)/shard_map/ppermute | solution.py:37
  80.7 1.6 %collective-permute-start.24 = (bf16[2,10,32,512]{3,2,1,0:T(8,128)(2,1)S(1)}, bf16[2,10,32,512]{3,2,1,0:T(8,128)(2,1)S(1)}, u32[]{:S(2)}, u32[]{:S(2)}) collective-permute-start(bf16[2,10,32,512]{3,2,1,0:T(8,128)(2,1)S(1)} %select_select_fusion.1.refs_11_), channel_id=1, source_target_pairs={{0,4},{2,6},{4,0},{6,2},{8,12},{10,14},{12,8},{14,10},{16,20},{18,... | collective-permute-start | bytes 1966088 | tf_op jit(solution)/shard_map/ppermute | solution.py:23
  82.3 0.8 copy-done.15
  83.1 11.1 %shard_map.106 = (bf16[2,512,2560]{2,1,0:T(8,128)(2,1)}, f32[256,1024]{1,0:T(8,128)}, f32[256,1024]{1,0:T(8,128)}) custom-call(s32[2]{0:T(128)} %pad_add_fusion.place_ref.refs_0_, bf16[128,2688]{1,0:T(8,128)(2,1)} %get-tuple-element.43.refs_0_.refs_1_, bf16[128,2688]{1,0:T(8,128)(2,1)} %copy-done.1, bf16[128,2560]{1,0:T(8,128)(2,1)} %refs_3_.3, ...), custom_call_target="tpu_custom_call" | custom-call | flops 2684354560 | bytes 20971520 | tf_op jit(solution)/shard_map/pallas_call | solution.py:448
  94.2 0.2 collective-permute-done.17
  94.4 2.2 %collective-permute-done.18 = bf16[2,10,32,512]{3,2,1,0:T(8,128)(2,1)S(1)} collective-permute-done((bf16[2,10,32,512]{3,2,1,0:T(8,128)(2,1)}, bf16[2,10,32,512]{3,2,1,0:T(8,128)(2,1)S(1)}, u32[]{:S(2)}, u32[]{:S(2)}) %collective-permute-start.18) | collective-permute-done | bytes 655392 | tf_op jit(solution)/shard_map/ppermute | solution.py:37
  96.7 0.3 collective-permute-done.24.refs_6_
  97.0 0.6 copy-done.24
  97.5 1.5 %collective-permute-done.25.refs_7_ = bf16[2,10,32,512]{3,2,1,0:T(8,128)(2,1)S(1)} collective-permute-done((bf16[2,10,32,512]{3,2,1,0:T(8,128)(2,1)S(1)}, bf16[2,10,32,512]{3,2,1,0:T(8,128)(2,1)S(1)}, u32[]{:S(2)}, u32[]{:S(2)}) %collective-permute-start.25) | collective-permute-done | bytes 655392 | tf_op jit(solution)/shard_map/ppermute | solution.py:23
  99.0 0.8 copy-done.16
  99.9 10.9 %shard_map.107 = (f32[128,2560]{1,0:T(8,128)}, bf16[128,2560]{1,0:T(8,128)(2,1)}) custom-call(s32[2]{0:T(128)} %pad_add_fusion.place_ref.refs_0_, bf16[128,2688]{1,0:T(8,128)(2,1)} %get-tuple-element.43.refs_0_.refs_1_, bf16[128,2688]{1,0:T(8,128)(2,1)} %copy-done.1, bf16[128,2560]{1,0:T(8,128)(2,1)} %refs_3_.3, bf16[128,2560]{1,0:T(8,128)(2,1)} %copy-done.4, ...), custom_call_target="tpu_custom_call" | custom-call | flops 1342177280 | bytes 13107200 | tf_op jit(solution)/shard_map/pallas_call | solution.py:485
  110.8 1.4 %collective-permute-start.26 = (bf16[128,2560]{1,0:T(8,128)(2,1)}, bf16[128,2560]{1,0:T(8,128)(2,1)S(1)}, u32[]{:S(2)}, u32[]{:S(2)}) collective-permute-start(bf16[128,2560]{1,0:T(8,128)(2,1)} %get-tuple-element.78), channel_id=1, source_target_pairs={{0,1},{1,0},{2,3},{3,2},{4,5},{5,4},{6,7},{7,6},{8,9},{9,8},{10,11... | collective-permute-start | bytes 1966088 | tf_op jit(solution)/shard_map/ppermute | solution.py:28
  112.2 0.2 add_convert_fusion
  112.7 3.5 %collective-permute-start.27 = (bf16[2,10,32,512]{3,2,1,0:T(8,128)(2,1)S(1)}, bf16[2,10,32,512]{3,2,1,0:T(8,128)(2,1)S(1)}, u32[]{:S(2)}, u32[]{:S(2)}) collective-permute-start(bf16[2,10,32,512]{3,2,1,0:T(8,128)(2,1)S(1)} %add_convert_fusion.1), channel_id=1, source_target_pairs={{8,16},{16,8},{10,18},{18,10},{12,20},{20,12},{14,22},{22,14},{9,1... | collective-permute-start | bytes 1966088 | tf_op jit(solution)/shard_map/ppermute | solution.py:37
  116.2 11.6 %collective-permute-done.26 = bf16[128,2560]{1,0:T(8,128)(2,1)S(1)} collective-permute-done((bf16[128,2560]{1,0:T(8,128)(2,1)}, bf16[128,2560]{1,0:T(8,128)(2,1)S(1)}, u32[]{:S(2)}, u32[]{:S(2)}) %collective-permute-start.26) | collective-permute-done | bytes 655392 | tf_op jit(solution)/shard_map/ppermute | solution.py:28
  127.8 1.0 add_convert_fusion.2
  129.0 2.3 %collective-permute-done.27.refs_1_ = bf16[2,10,32,512]{3,2,1,0:T(8,128)(2,1)S(1)} collective-permute-done((bf16[2,10,32,512]{3,2,1,0:T(8,128)(2,1)S(1)}, bf16[2,10,32,512]{3,2,1,0:T(8,128)(2,1)S(1)}, u32[]{:S(2)}, u32[]{:S(2)}) %collective-permute-start.27) | collective-permute-done | bytes 655392 | tf_op jit(solution)/shard_map/ppermute | solution.py:37
  131.3 1.2 shard_map.108
  (86 shorter events, 1.5 us)
Async XLA Ops:
  3.1 17.4 %collective-permute-start = (bf16[128,2688]{1,0:T(8,128)(2,1)}, bf16[128,2688]{1,0:T(8,128)(2,1)S(1)}, u32[]{:S(2)}, u32[]{:S(2)}) collective-permute-start(bf16[128,2688]{1,0:T(8,128)(2,1)} %get-tuple-element.43.refs_0_.refs_1_), channel_id=1, source_target_pairs={{0,4},{2,6},{4,0},{6,2},{8,12},{10,14},{12,8},{14,10},{16,20},{18,... | collective-permute-start | bytes 2064392 | tf_op jit(solution)/shard_map/ppermute | solution.py:23
  3.6 17.1 %collective-permute-start.1 = (bf16[128,2688]{1,0:T(8,128)(2,1)}, bf16[128,2688]{1,0:T(8,128)(2,1)S(1)}, u32[]{:S(2)}, u32[]{:S(2)}) collective-permute-start(bf16[128,2688]{1,0:T(8,128)(2,1)} %get-tuple-element.43.refs_0_.refs_1_), channel_id=1, source_target_pairs={{0,1},{1,0},{2,3},{3,2},{4,5},{5,4},{6,7},{7,6},{8,9},{9,8},{10,11... | collective-permute-start | bytes 2064392 | tf_op jit(solution)/shard_map/ppermute | solution.py:28
  5.1 15.6 %collective-permute-start.2 = (bf16[128,2688]{1,0:T(8,128)(2,1)}, bf16[128,2688]{1,0:T(8,128)(2,1)S(1)}, u32[]{:S(2)}, u32[]{:S(2)}) collective-permute-start(bf16[128,2688]{1,0:T(8,128)(2,1)} %get-tuple-element.43.refs_0_.refs_1_), channel_id=1, source_target_pairs={{0,2},{2,0},{4,6},{6,4},{8,10},{10,8},{12,14},{14,12},{16,18},{18,... | collective-permute-start | bytes 2064392 | tf_op jit(solution)/shard_map/ppermute | solution.py:23
  5.1 19.2 %collective-permute-start.5 = (bf16[2,10,32,512]{3,2,1,0:T(8,128)(2,1)}, bf16[2,10,32,512]{3,2,1,0:T(8,128)(2,1)S(1)}, u32[]{:S(2)}, u32[]{:S(2)}) collective-permute-start(bf16[2,10,32,512]{3,2,1,0:T(8,128)(2,1)} %get-tuple-element.59), channel_id=1, source_target_pairs={{8,16},{16,8},{10,18},{18,10},{12,20},{20,12},{14,22},{22,14},{9,1... | collective-permute-start | bytes 1966088 | tf_op jit(solution)/shard_map/ppermute | solution.py:37
  8.6 17.1 %collective-permute-start.7 = (bf16[2,10,32,512]{3,2,1,0:T(8,128)(2,1)}, bf16[2,10,32,512]{3,2,1,0:T(8,128)(2,1)S(1)}, u32[]{:S(2)}, u32[]{:S(2)}) collective-permute-start(bf16[2,10,32,512]{3,2,1,0:T(8,128)(2,1)} %get-tuple-element.59), channel_id=1, source_target_pairs={{0,8},{2,10},{4,12},{6,14},{8,0},{10,2},{12,4},{14,6},{16,24},{18,... | collective-permute-start | bytes 1966088 | tf_op jit(solution)/shard_map/ppermute | solution.py:23
  20.5 8.9 %copy-start.26 = (bf16[128,2688]{1,0:T(8,128)(2,1)}, bf16[128,2688]{1,0:T(8,128)(2,1)S(1)}, u32[]{:S(2)}) copy-start(bf16[128,2688]{1,0:T(8,128)(2,1)S(1)} %collective-permute-done.refs_1_) | copy-start | bytes 2064388
  20.7 24.5 %copy-start.1 = (bf16[128,2688]{1,0:T(8,128)(2,1)}, bf16[128,2688]{1,0:T(8,128)(2,1)S(1)}, u32[]{:S(2)}) copy-start(bf16[128,2688]{1,0:T(8,128)(2,1)S(1)} %collective-permute-done.1.refs_4_.refs_2_) | copy-start | bytes 2064388
  20.7 7.4 %copy-start.27 = (bf16[128,2688]{1,0:T(8,128)(2,1)}, bf16[128,2688]{1,0:T(8,128)(2,1)S(1)}, u32[]{:S(2)}) copy-start(bf16[128,2688]{1,0:T(8,128)(2,1)S(1)} %collective-permute-done.2.refs_2_) | copy-start | bytes 2064388
  20.7 23.0 %collective-permute-start.3 = (bf16[128,2688]{1,0:T(8,128)(2,1)S(1)}, bf16[128,2688]{1,0:T(8,128)(2,1)S(1)}, u32[]{:S(2)}, u32[]{:S(2)}) collective-permute-start(bf16[128,2688]{1,0:T(8,128)(2,1)S(1)} %collective-permute-done.refs_1_), channel_id=1, source_target_pairs={{0,1},{1,0},{2,3},{3,2},{4,5},{5,4},{6,7},{7,6},{8,9},{9,8},{10,11... | collective-permute-start | bytes 2064392 | tf_op jit(solution)/shard_map/ppermute | solution.py:28
  22.3 21.4 %collective-permute-start.4 = (bf16[128,2688]{1,0:T(8,128)(2,1)S(1)}, bf16[128,2688]{1,0:T(8,128)(2,1)S(1)}, u32[]{:S(2)}, u32[]{:S(2)}) collective-permute-start(bf16[128,2688]{1,0:T(8,128)(2,1)S(1)} %collective-permute-done.refs_1_), channel_id=1, source_target_pairs={{0,2},{2,0},{4,6},{6,4},{8,10},{10,8},{12,14},{14,12},{16,18},{18,... | collective-permute-start | bytes 2064392 | tf_op jit(solution)/shard_map/ppermute | solution.py:23
  24.4 5.0 %copy-start.17 = (bf16[2,10,32,512]{3,2,1,0:T(8,128)(2,1)}, bf16[2,10,32,512]{3,2,1,0:T(8,128)(2,1)S(1)}, u32[]{:S(2)}) copy-start(bf16[2,10,32,512]{3,2,1,0:T(8,128)(2,1)S(1)} %collective-permute-done.5) | copy-start | bytes 1966084
  24.4 16.4 %collective-permute-start.6 = (bf16[2,10,32,512]{3,2,1,0:T(8,128)(2,1)S(1)}, bf16[2,10,32,512]{3,2,1,0:T(8,128)(2,1)S(1)}, u32[]{:S(2)}, u32[]{:S(2)}) collective-permute-start(bf16[2,10,32,512]{3,2,1,0:T(8,128)(2,1)S(1)} %collective-permute-done.5), channel_id=1, source_target_pairs={{0,8},{2,10},{4,12},{6,14},{8,0},{10,2},{12,4},{14,6},{16,24},{18,... | collective-permute-start | bytes 1966088 | tf_op jit(solution)/shard_map/ppermute | solution.py:23
  25.8 17.9 %collective-permute-start.8 = (bf16[2,10,32,512]{3,2,1,0:T(8,128)(2,1)S(1)}, bf16[2,10,32,512]{3,2,1,0:T(8,128)(2,1)S(1)}, u32[]{:S(2)}, u32[]{:S(2)}) collective-permute-start(bf16[2,10,32,512]{3,2,1,0:T(8,128)(2,1)S(1)} %collective-permute-done.7), channel_id=1, source_target_pairs={{8,16},{16,8},{10,18},{18,10},{12,20},{20,12},{14,22},{22,14},{9,1... | collective-permute-start | bytes 1966088 | tf_op jit(solution)/shard_map/ppermute | solution.py:37
  29.4 18.0 %copy-start.2 = (bf16[2,2,10,32,512]{4,3,2,1,0:T(8,128)(2,1)}, bf16[2,2,10,32,512]{4,3,2,1,0:T(8,128)(2,1)S(1)}, u32[]{:S(2)}) copy-start(bf16[2,2,10,32,512]{4,3,2,1,0:T(8,128)(2,1)S(1)} %pad_maximum_fusion.refs_5_) | copy-start | bytes 3932164
  29.4 18.1 %copy-start.3 = (bf16[128,2560]{1,0:T(8,128)(2,1)S(1)}, bf16[128,2560]{1,0:T(8,128)(2,1)}, u32[]{:S(2)}) copy-start(bf16[128,2560]{1,0:T(8,128)(2,1)} %refs_3_.3) | copy-start | bytes 1966084
  29.4 30.1 %collective-permute-start.14 = (bf16[2,2,10,32,512]{4,3,2,1,0:T(8,128)(2,1)S(1)}, bf16[2,2,10,32,512]{4,3,2,1,0:T(8,128)(2,1)}, u32[]{:S(2)}, u32[]{:S(2)}) collective-permute-start(bf16[2,2,10,32,512]{4,3,2,1,0:T(8,128)(2,1)S(1)} %pad_maximum_fusion.refs_5_), channel_id=1, source_target_pairs={{0,4},{2,6},{4,0},{6,2},{8,12},{10,14},{12,8},{14,10},{16,20},{18,... | collective-permute-start | bytes 3932168 | tf_op jit(solution)/shard_map/ppermute | solution.py:23
  40.7 5.4 %copy-start.19 = (bf16[2,10,32,512]{3,2,1,0:T(8,128)(2,1)}, bf16[2,10,32,512]{3,2,1,0:T(8,128)(2,1)S(1)}, u32[]{:S(2)}) copy-start(bf16[2,10,32,512]{3,2,1,0:T(8,128)(2,1)S(1)} %collective-permute-done.6) | copy-start | bytes 1966084
  43.7 2.4 %copy-start.10 = (bf16[128,2688]{1,0:T(8,128)(2,1)}, bf16[128,2688]{1,0:T(8,128)(2,1)S(1)}, u32[]{:S(2)}) copy-start(bf16[128,2688]{1,0:T(8,128)(2,1)S(1)} %collective-permute-done.3.refs_5_) | copy-start | bytes 2064388
  44.7 2.7 %collective-permute-start.11 = (bf16[64,2688]{1,0:T(8,128)(2,1)}, bf16[64,2688]{1,0:T(8,128)(2,1)}, u32[]{:S(2)}, u32[]{:S(2)}) collective-permute-start(bf16[64,2688]{1,0:T(8,128)(2,1)} %get-tuple-element.85), channel_id=1, source_target_pairs={{0,2},{2,0},{4,6},{6,4},{8,10},{10,8},{12,14},{14,12},{16,18},{18,... | collective-permute-start | bytes 1032200 | tf_op jit(solution)/shard_map/ppermute | solution.py:23
  44.7 2.7 %collective-permute-start.12 = (bf16[64,2688]{1,0:T(8,128)(2,1)}, bf16[64,2688]{1,0:T(8,128)(2,1)}, u32[]{:S(2)}, u32[]{:S(2)}) collective-permute-start(bf16[64,2688]{1,0:T(8,128)(2,1)} %get-tuple-element.84), channel_id=1, source_target_pairs={{0,2},{2,0},{4,6},{6,4},{8,10},{10,8},{12,14},{14,12},{16,18},{18,... | collective-permute-start | bytes 1032200 | tf_op jit(solution)/shard_map/ppermute | solution.py:23
  46.1 1.9 %collective-permute-start.10 = (bf16[64,2688]{1,0:T(8,128)(2,1)}, bf16[64,2688]{1,0:T(8,128)(2,1)S(1)}, u32[]{:S(2)}, u32[]{:S(2)}) collective-permute-start(bf16[64,2688]{1,0:T(8,128)(2,1)} %get-tuple-element.86), channel_id=1, source_target_pairs={{0,2},{2,0},{4,6},{6,4},{8,10},{10,8},{12,14},{14,12},{16,18},{18,... | collective-permute-start | bytes 1032200 | tf_op jit(solution)/shard_map/ppermute | solution.py:23
  46.2 2.5 %collective-permute-start.9 = (bf16[64,2688]{1,0:T(8,128)(2,1)}, bf16[64,2688]{1,0:T(8,128)(2,1)}, u32[]{:S(2)}, u32[]{:S(2)}) collective-permute-start(bf16[64,2688]{1,0:T(8,128)(2,1)} %get-tuple-element.87), channel_id=1, source_target_pairs={{0,2},{2,0},{4,6},{6,4},{8,10},{10,8},{12,14},{14,12},{16,18},{18,... | collective-permute-start | bytes 1032200 | tf_op jit(solution)/shard_map/ppermute | solution.py:23
  47.4 30.1 %collective-permute-start.19 = (bf16[2,2,10,32,512]{4,3,2,1,0:T(8,128)(2,1)S(1)}, bf16[2,2,10,32,512]{4,3,2,1,0:T(8,128)(2,1)S(1)}, u32[]{:S(2)}, u32[]{:S(2)}) collective-permute-start(bf16[2,2,10,32,512]{4,3,2,1,0:T(8,128)(2,1)S(1)} %pad_maximum_fusion.refs_5_), channel_id=1, source_target_pairs={{0,2},{2,0},{4,6},{6,4},{8,10},{10,8},{12,14},{14,12},{16,18},{18,... | collective-permute-start | bytes 3932168 | tf_op jit(solution)/shard_map/ppermute | solution.py:23
  47.5 26.2 %collective-permute-start.16 = (bf16[128,2560]{1,0:T(8,128)(2,1)S(1)}, bf16[128,2560]{1,0:T(8,128)(2,1)S(1)}, u32[]{:S(2)}, u32[]{:S(2)}) collective-permute-start(bf16[128,2560]{1,0:T(8,128)(2,1)S(1)} %copy-done.3), channel_id=1, source_target_pairs={{0,1},{1,0},{2,3},{3,2},{4,5},{5,4},{6,7},{7,6},{8,9},{9,8},{10,11... | collective-permute-start | bytes 1966088 | tf_op jit(solution)/shard_map/ppermute | solution.py:28
  56.7 16.8 %collective-permute-start.13 = (bf16[2,10,32,512]{3,2,1,0:T(8,128)(2,1)S(1)}, bf16[2,10,32,512]{3,2,1,0:T(8,128)(2,1)S(1)}, u32[]{:S(2)}, u32[]{:S(2)}) collective-permute-start(bf16[2,10,32,512]{3,2,1,0:T(8,128)(2,1)S(1)} %broadcast_select_fusion), channel_id=1, source_target_pairs={{0,8},{2,10},{4,12},{6,14},{8,0},{10,2},{12,4},{14,6},{16,24},{18,... | collective-permute-start | bytes 1966088 | tf_op jit(solution)/shard_map/ppermute | solution.py:23
  57.9 19.5 %copy-start.5 = (bf16[2,10,32,512]{3,2,1,0:T(8,128)(2,1)}, bf16[2,10,32,512]{3,2,1,0:T(8,128)(2,1)S(1)}, u32[]{:S(2)}) copy-start(bf16[2,10,32,512]{3,2,1,0:T(8,128)(2,1)S(1)} %select_select_fusion.refs_7_) | copy-start | bytes 1966084
  59.5 15.3 %collective-permute-start.15 = (bf16[2,10,32,512]{3,2,1,0:T(8,128)(2,1)S(1)}, bf16[2,10,32,512]{3,2,1,0:T(8,128)(2,1)S(1)}, u32[]{:S(2)}, u32[]{:S(2)}) collective-permute-start(bf16[2,10,32,512]{3,2,1,0:T(8,128)(2,1)S(1)} %select_select_fusion.refs_7_), channel_id=1, source_target_pairs={{0,4},{2,6},{4,0},{6,2},{8,12},{10,14},{12,8},{14,10},{16,20},{18,... | collective-permute-start | bytes 1966088 | tf_op jit(solution)/shard_map/ppermute | solution.py:23
  60.9 17.2 %collective-permute-start.21 = (bf16[2,10,32,512]{3,2,1,0:T(8,128)(2,1)S(1)}, bf16[2,10,32,512]{3,2,1,0:T(8,128)(2,1)S(1)}, u32[]{:S(2)}, u32[]{:S(2)}) collective-permute-start(bf16[2,10,32,512]{3,2,1,0:T(8,128)(2,1)S(1)} %select_select_fusion.refs_7_), channel_id=1, source_target_pairs={{0,2},{2,0},{4,6},{6,4},{8,10},{10,8},{12,14},{14,12},{16,18},{18,... | collective-permute-start | bytes 1966088 | tf_op jit(solution)/shard_map/ppermute | solution.py:23
  73.5 8.7 %collective-permute-start.20 = (bf16[2,2,10,32,512]{4,3,2,1,0:T(8,128)(2,1)}, bf16[2,2,10,32,512]{4,3,2,1,0:T(8,128)(2,1)}, u32[]{:S(2)}, u32[]{:S(2)}) collective-permute-start(bf16[2,2,10,32,512]{4,3,2,1,0:T(8,128)(2,1)} %collective-permute-done.14.refs_6_), channel_id=1, source_target_pairs={{0,2},{2,0},{4,6},{6,4},{8,10},{10,8},{12,14},{14,12},{16,18},{18,... | collective-permute-start | bytes 3932168 | tf_op jit(solution)/shard_map/ppermute | solution.py:23
  73.6 8.6 %copy-start.6 = (bf16[2,10,32,512]{3,2,1,0:T(8,128)(2,1)}, bf16[2,10,32,512]{3,2,1,0:T(8,128)(2,1)S(1)}, u32[]{:S(2)}) copy-start(bf16[2,10,32,512]{3,2,1,0:T(8,128)(2,1)S(1)} %select_select_fusion.1.refs_11_) | copy-start | bytes 1966084
  73.6 8.6 %copy-start.4 = (bf16[128,2560]{1,0:T(8,128)(2,1)}, bf16[128,2560]{1,0:T(8,128)(2,1)S(1)}, u32[]{:S(2)}) copy-start(bf16[128,2560]{1,0:T(8,128)(2,1)S(1)} %collective-permute-done.16.refs_4_) | copy-start | bytes 1966084
  74.8 7.5 %copy-start.11 = (bf16[2,10,32,512]{3,2,1,0:T(8,128)(2,1)}, bf16[2,10,32,512]{3,2,1,0:T(8,128)(2,1)S(1)}, u32[]{:S(2)}) copy-start(bf16[2,10,32,512]{3,2,1,0:T(8,128)(2,1)S(1)} %collective-permute-done.15.refs_8_) | copy-start | bytes 1966084
  74.8 5.8 %collective-permute-start.22 = (bf16[2,10,32,512]{3,2,1,0:T(8,128)(2,1)S(1)}, bf16[2,10,32,512]{3,2,1,0:T(8,128)(2,1)S(1)}, u32[]{:S(2)}, u32[]{:S(2)}) collective-permute-start(bf16[2,10,32,512]{3,2,1,0:T(8,128)(2,1)S(1)} %collective-permute-done.15.refs_8_), channel_id=1, source_target_pairs={{0,2},{2,0},{4,6},{6,4},{8,10},{10,8},{12,14},{14,12},{16,18},{18,... | collective-permute-start | bytes 1966088 | tf_op jit(solution)/shard_map/ppermute | solution.py:23
  74.8 7.4 %collective-permute-start.23 = (bf16[2,10,32,512]{3,2,1,0:T(8,128)(2,1)S(1)}, bf16[2,10,32,512]{3,2,1,0:T(8,128)(2,1)S(1)}, u32[]{:S(2)}, u32[]{:S(2)}) collective-permute-start(bf16[2,10,32,512]{3,2,1,0:T(8,128)(2,1)S(1)} %select_select_fusion.1.refs_11_), channel_id=1, source_target_pairs={{0,2},{2,0},{4,6},{6,4},{8,10},{10,8},{12,14},{14,12},{16,18},{18,... | collective-permute-start | bytes 1966088 | tf_op jit(solution)/shard_map/ppermute | solution.py:23
  77.5 4.8 %copy-start.8 = (bf16[2,2,10,32,512]{4,3,2,1,0:T(8,128)(2,1)}, bf16[2,2,10,32,512]{4,3,2,1,0:T(8,128)(2,1)S(1)}, u32[]{:S(2)}) copy-start(bf16[2,2,10,32,512]{4,3,2,1,0:T(8,128)(2,1)S(1)} %collective-permute-done.19.refs_9_) | copy-start | bytes 3932164
  77.5 16.9 %collective-permute-start.17 = (bf16[2,10,32,512]{3,2,1,0:T(8,128)(2,1)}, bf16[2,10,32,512]{3,2,1,0:T(8,128)(2,1)S(1)}, u32[]{:S(2)}, u32[]{:S(2)}) collective-permute-start(bf16[2,10,32,512]{3,2,1,0:T(8,128)(2,1)} %get-tuple-element.63), channel_id=1, source_target_pairs={{0,8},{2,10},{4,12},{6,14},{8,0},{10,2},{12,4},{14,6},{16,24},{18,... | collective-permute-start | bytes 1966088 | tf_op jit(solution)/shard_map/ppermute | solution.py:23
  78.2 4.0 %copy-start.12 = (bf16[2,10,32,512]{3,2,1,0:T(8,128)(2,1)}, bf16[2,10,32,512]{3,2,1,0:T(8,128)(2,1)S(1)}, u32[]{:S(2)}) copy-start(bf16[2,10,32,512]{3,2,1,0:T(8,128)(2,1)S(1)} %collective-permute-done.21.refs_12_) | copy-start | bytes 1966084
  78.2 18.5 %collective-permute-start.18 = (bf16[2,10,32,512]{3,2,1,0:T(8,128)(2,1)}, bf16[2,10,32,512]{3,2,1,0:T(8,128)(2,1)S(1)}, u32[]{:S(2)}, u32[]{:S(2)}) collective-permute-start(bf16[2,10,32,512]{3,2,1,0:T(8,128)(2,1)} %add_convert_fusion.3), channel_id=1, source_target_pairs={{8,16},{16,8},{10,18},{18,10},{12,20},{20,12},{14,22},{22,14},{9,1... | collective-permute-start | bytes 1966088 | tf_op jit(solution)/shard_map/ppermute | solution.py:37
  80.7 16.3 %collective-permute-start.24 = (bf16[2,10,32,512]{3,2,1,0:T(8,128)(2,1)S(1)}, bf16[2,10,32,512]{3,2,1,0:T(8,128)(2,1)S(1)}, u32[]{:S(2)}, u32[]{:S(2)}) collective-permute-start(bf16[2,10,32,512]{3,2,1,0:T(8,128)(2,1)S(1)} %select_select_fusion.1.refs_11_), channel_id=1, source_target_pairs={{0,4},{2,6},{4,0},{6,2},{8,12},{10,14},{12,8},{14,10},{16,20},{18,... | collective-permute-start | bytes 1966088 | tf_op jit(solution)/shard_map/ppermute | solution.py:23
  94.4 2.5 %copy-start.22 = (bf16[2,10,32,512]{3,2,1,0:T(8,128)(2,1)}, bf16[2,10,32,512]{3,2,1,0:T(8,128)(2,1)S(1)}, u32[]{:S(2)}) copy-start(bf16[2,10,32,512]{3,2,1,0:T(8,128)(2,1)S(1)} %collective-permute-done.17) | copy-start | bytes 1966084
  96.9 15.2 %copy-start.21 = (bf16[2,10,32,512]{3,2,1,0:T(8,128)(2,1)S(1)}, bf16[2,10,32,512]{3,2,1,0:T(8,128)(2,1)}, u32[]{:S(2)}) copy-start(bf16[2,10,32,512]{3,2,1,0:T(8,128)(2,1)} %get-tuple-element.82) | copy-start | bytes 1966084
  96.9 2.1 %collective-permute-start.25 = (bf16[2,10,32,512]{3,2,1,0:T(8,128)(2,1)S(1)}, bf16[2,10,32,512]{3,2,1,0:T(8,128)(2,1)S(1)}, u32[]{:S(2)}, u32[]{:S(2)}) collective-permute-start(bf16[2,10,32,512]{3,2,1,0:T(8,128)(2,1)S(1)} %collective-permute-done.24.refs_6_), channel_id=1, source_target_pairs={{0,2},{2,0},{4,6},{6,4},{8,10},{10,8},{12,14},{14,12},{16,18},{18,... | collective-permute-start | bytes 1966088 | tf_op jit(solution)/shard_map/ppermute | solution.py:23
  99.9 12.3 %copy-start.25 = (bf16[2,10,32,512]{3,2,1,0:T(8,128)(2,1)S(1)}, bf16[2,10,32,512]{3,2,1,0:T(8,128)(2,1)}, u32[]{:S(2)}) copy-start(bf16[2,10,32,512]{3,2,1,0:T(8,128)(2,1)} %copy-done.24) | copy-start | bytes 1966084
  110.8 17.1 %collective-permute-start.26 = (bf16[128,2560]{1,0:T(8,128)(2,1)}, bf16[128,2560]{1,0:T(8,128)(2,1)S(1)}, u32[]{:S(2)}, u32[]{:S(2)}) collective-permute-start(bf16[128,2560]{1,0:T(8,128)(2,1)} %get-tuple-element.78), channel_id=1, source_target_pairs={{0,1},{1,0},{2,3},{3,2},{4,5},{5,4},{6,7},{7,6},{8,9},{9,8},{10,11... | collective-permute-start | bytes 1966088 | tf_op jit(solution)/shard_map/ppermute | solution.py:28
  112.4 15.4 %copy-start.9 = (f32[128,2560]{1,0:T(8,128)S(1)}, f32[128,2560]{1,0:T(8,128)}, u32[]{:S(2)}) copy-start(f32[128,2560]{1,0:T(8,128)} %get-tuple-element.77) | copy-start | bytes 3932164
  112.4 16.6 %collective-permute-start.28 = (bf16[2,10,32,512]{3,2,1,0:T(8,128)(2,1)S(1)}, bf16[2,10,32,512]{3,2,1,0:T(8,128)(2,1)S(1)}, u32[]{:S(2)}, u32[]{:S(2)}) collective-permute-start(bf16[2,10,32,512]{3,2,1,0:T(8,128)(2,1)S(1)} %add_convert_fusion), channel_id=1, source_target_pairs={{0,8},{2,10},{4,12},{6,14},{8,0},{10,2},{12,4},{14,6},{16,24},{18,... | collective-permute-start | bytes 1966088 | tf_op jit(solution)/shard_map/ppermute | solution.py:23
  112.7 18.5 %copy-start = (f32[2,10,32,512]{3,2,1,0:T(8,128)S(1)}, f32[2,10,32,512]{3,2,1,0:T(8,128)}, u32[]{:S(2)}) copy-start(f32[2,10,32,512]{3,2,1,0:T(8,128)} %get-tuple-element.79.refs_0_) | copy-start | bytes 3932164
  112.7 18.5 %collective-permute-start.27 = (bf16[2,10,32,512]{3,2,1,0:T(8,128)(2,1)S(1)}, bf16[2,10,32,512]{3,2,1,0:T(8,128)(2,1)S(1)}, u32[]{:S(2)}, u32[]{:S(2)}) collective-permute-start(bf16[2,10,32,512]{3,2,1,0:T(8,128)(2,1)S(1)} %add_convert_fusion.1), channel_id=1, source_target_pairs={{8,16},{16,8},{10,18},{18,10},{12,20},{20,12},{14,22},{22,14},{9,1... | collective-permute-start | bytes 1966088 | tf_op jit(solution)/shard_map/ppermute | solution.py:37
  (11 other events, 15.3 us)

commit v3 on v2

--- a/solution.py
+++ b/solution.py
@@ -35,6 +35,10 @@
         for i in range(z * 4, z * 4 + 4):
             pairs += [(i, i + 4), (i + 4, i)]
     return lax.ppermute(value, "dp", pairs)
+
+
+def room(*arrays):
+    return sum(math.prod(shape) * size for shape, size in arrays) + (2 << 20)
 
 
 def pick(by_plane, plane):
@@ -198,7 +202,11 @@
             pltpu.VMEM((count, total), jnp.bfloat16),
             pltpu.SemaphoreType.DMA((len(blocks),)),
         ],
-        compiler_params=pltpu.CompilerParams(vmem_limit_bytes=56 << 20),
+        compiler_params=pltpu.CompilerParams(
+            vmem_limit_bytes=room(
+                ((count, total), 2), ((len(offsets) + 1, rows, half), 4), ((len(offsets), rows, count), 2)
+            )
+        ),
         cost_estimate=pl.CostEstimate(
             flops=2 * len(offsets) * rows * count * half,
             bytes_accessed=2 * count * total + 2 * len(offsets) * rows * half,
@@ -225,7 +233,9 @@
     return pl.pallas_call(
         table_total_kernel,
         out_shape=jax.ShapeDtypeStruct((rows, width), jnp.float32),
-        compiler_params=pltpu.CompilerParams(vmem_limit_bytes=32 << 20),
+        compiler_params=pltpu.CompilerParams(
+            vmem_limit_bytes=room(((len(values) + 1, rows, width), 4))
+        ),
     )(*values)
 
 
@@ -318,11 +328,12 @@
     return held, -(-(LANES - math.gcd(held, LANES) + held) // LANES) * LANES
 
 
-def result_kernel(last, groups, planes, lookups, top, *refs):
+def result_kernel(last, begin, groups, planes, lookups, top, *refs):
     place_ref, tokens, refs = refs[0], refs[1 : 1 + 2 * groups], refs[1 + 2 * groups :]
-    turned_ref, first_ref, second_ref, pre_ref, back_ref, own_ref, rest_ref, *refs = refs
+    turned_ref, first_ref, second_ref, pre_ref, back_ref, out_ref, *refs = refs
     grad, part, up, down, turned, pre_part, back_part, token_sem, piece_sem, turned_sem = refs
-    tok, width = own_ref.shape
+    count, width = out_ref.shape
+    tok = count // groups
     experts, blocks, per, rows, hid = down.shape
     expert = place_ref[1]
     pair = located(last, place_ref, planes) // 2
@@ -352,8 +363,9 @@
                 piece_sem.at[1, number],
             )
         )
-    copies.append(pltpu.make_async_copy(pre_ref, pre_part, piece_sem.at[0, 2]))
-    copies.append(pltpu.make_async_copy(back_ref, back_part, piece_sem.at[1, 2]))
+    mine = pl.ds(begin, count)
+    copies.append(pltpu.make_async_copy(pre_ref.at[mine], pre_part, piece_sem.at[0, 2]))
+    copies.append(pltpu.make_async_copy(back_ref.at[mine], back_part, piece_sem.at[1, 2]))
     turns = [
         pltpu.make_async_copy(
             turned_ref.at[:, :, pl.ds(b * hid, hid)],
@@ -412,12 +424,7 @@
                 total += jnp.dot(
                     slopes[e], turned[e, :, cols], preferred_element_type=jnp.float32
                 )
-            if start == 0:
-                own_ref[:, cols] = total[:tok]
-                if chunk > tok:
-                    rest_ref[pl.ds(0, chunk - tok), cols] = total[tok:].astype(jnp.bfloat16)
-            else:
-                rest_ref[pl.ds(start - tok, chunk), cols] = total.astype(jnp.bfloat16)
+            out_ref[span, cols] = total.astype(out_ref.dtype)
         late = jnp.zeros((chunk, slab), jnp.float32)
         for e in range(experts):
             late += lax.dot_general(
@@ -427,14 +434,8 @@
                 preferred_element_type=jnp.float32,
             )
         cols = pl.ds(base, slab)
-        if start == 0:
-            own_ref[:, cols] += late[:tok]
-            late, span = late[tok:], pl.ds(0, chunk - tok)
-        else:
-            span = pl.ds(start - tok, chunk)
-        if start or chunk > tok:
-            known = rest_ref[span, cols].astype(jnp.float32)
-            rest_ref[span, cols] = (known + late).astype(jnp.bfloat16)
+        known = out_ref[span, cols].astype(jnp.float32)
+        out_ref[span, cols] = (known + late).astype(out_ref.dtype)
 
 
 def hidden_layers(grads, inputs, pieces, last, place):
@@ -463,7 +464,13 @@
             pltpu.SemaphoreType.DMA((2, groups)),
             pltpu.SemaphoreType.DMA((2, len(where))),
         ],
-        compiler_params=pltpu.CompilerParams(vmem_limit_bytes=56 << 20),
+        compiler_params=pltpu.CompilerParams(
+            vmem_limit_bytes=room(
+                ((groups * tok, 2 * width + LANES), 2),
+                ((3, experts, hid, width), 2),
+                ((2, groups * tok, experts * hid), 4),
+            )
+        ),
         cost_estimate=pl.CostEstimate(
             flops=4 * groups * tok * width * hid * experts,
             bytes_accessed=6 * experts * width * hid + 8 * groups * tok * width,
@@ -472,37 +479,41 @@
     )(place, *grads, *inputs, *[piece[0] for piece in pieces])
 
 
-def expert_results(grads, inputs, hidden, first, second, last, place, lookups, top):
+def expert_results(grads, inputs, hidden, first, second, last, place, lookups, top, begin, dtype):
     groups = len(grads)
     tok, width = inputs[0].shape
     experts, blocks2, rows, hid = first.shape
     blocks = blocks2 // 2
     dp = lax.axis_size("dp")
     turned, pre, back = hidden
-    rest_rows = max(groups - 1, 1) * tok
     slab = slab_of(blocks, rows)[1]
     any_space, vmem = pl.BlockSpec(memory_space=pl.ANY), pl.BlockSpec(memory_space=pltpu.VMEM)
     return pl.pallas_call(
-        functools.partial(result_kernel, last, groups, dp // 4, lookups, top),
-        out_shape=(
-            jax.ShapeDtypeStruct((tok, width), jnp.float32),
-            jax.ShapeDtypeStruct((rest_rows, width), jnp.bfloat16),
-        ),
+        functools.partial(result_kernel, last, begin, groups, dp // 4, lookups, top),
+        out_shape=jax.ShapeDtypeStruct((groups * tok, width), dtype),
         in_specs=[pl.BlockSpec(memory_space=pltpu.SMEM)] + [any_space] * (2 * groups + 5),
-        out_specs=(vmem, vmem),
+        out_specs=vmem,
         scratch_shapes=[
             pltpu.VMEM((groups * tok, width + LANES), jnp.bfloat16),
             pltpu.VMEM((groups * tok, slab), jnp.bfloat16),
             pltpu.VMEM((experts, slab // rows, rows, hid), jnp.bfloat16),
             pltpu.VMEM((experts, blocks, LANES // rows, rows, hid), jnp.bfloat16),
             pltpu.VMEM(turned.shape, jnp.bfloat16),
-            pltpu.VMEM(pre.shape, jnp.float32),
-            pltpu.VMEM(back.shape, jnp.float32),
+            pltpu.VMEM((groups * tok, pre.shape[1]), jnp.float32),
+            pltpu.VMEM((groups * tok, pre.shape[1]), jnp.float32),
             pltpu.SemaphoreType.DMA((2, groups)),
             pltpu.SemaphoreType.DMA((2, 3)),
             pltpu.SemaphoreType.DMA((blocks,)),
         ],
-        compiler_params=pltpu.CompilerParams(vmem_limit_bytes=60 << 20),
+        compiler_params=pltpu.CompilerParams(
+            vmem_limit_bytes=room(
+                ((groups * tok, width + LANES + slab), 2),
+                ((experts, hid, width + slab), 2),
+                ((experts, LANES, width), 2),
+                ((2, groups * tok, experts * hid), 4),
+                ((groups * tok, width), 4),
+            )
+        ),
         cost_estimate=pl.CostEstimate(
             flops=2 * groups * tok * width * hid * experts,
             bytes_accessed=2 * experts * width * hid + 12 * groups * tok * width,
@@ -581,7 +592,8 @@
     near = [near, swap(rows_x, 1)]
     if planes > 2:
         came[2] = along(2, came[1])
-        got, far, near, came[2] = fence((got, far, near, came[2]))
+        got, far = fence((got, far))
+        near, came[2] = fence((near, came[2]))
     blocks = [rows, rows_x, *near, *got, *far]
     for block in got + far:
         blocks += [swap(block[: tok // 2], 1), swap(block[tok // 2 :], 1)]
@@ -637,15 +649,32 @@
     for step in range(2 if fits else 1, planes - 1):
         sums = reduce(step, sums)
     sums, hidden, passed = fence((sums, hidden, passed))
-    total, rest = expert_results(
-        grads, inputs, hidden, passed, swap(passed, 1), last, place, lookups, top
-    )
-    total, sums = fence((total, sums))
+    first, second = passed, swap(passed, 1)
+
+    def results(some, begin, dtype):
+        return expert_results(
+            [grads[g] for g in some],
+            [inputs[g] for g in some],
+            hidden,
+            first,
+            second,
+            last,
+            place,
+            lookups,
+            top,
+            begin * tok,
+            dtype,
+        )
+
+    if groups > 1:
+        rest = results(others, 1, jnp.bfloat16)
+        rest, sums = fence((rest, sums))
     if planes > 1:
         sums = reduce(planes - 1, sums)
-    for back in others:
-        value = rest[(back - 1) * tok : back * tok]
-        total = total + over_expert(value, groups - back).astype(jnp.float32)
+    returned = [over_expert(rest[(k - 1) * tok : k * tok], groups - k) for k in others]
+    total = results([0], 0, jnp.float32)
+    for value in returned:
+        total = total + value.astype(jnp.float32)
     sums = [partials[0]] + [came_in for came_in in sums[::-1] if came_in is not None]
     table = table_total(sums, lookups * part, half)
     return total.astype(jnp.bfloat16), table.reshape(lookups, part, width // ORDERS)

time: 134 us -> 127 us (0.948)
  Pallas kernels: 33.4 us -> 25.2 us
  local copies, waits for them, and re-layouts: 5.45 us -> 10 us
  other arithmetic: 5.63 us -> 3.14 us
  starting transfers between devices: 24.5 us -> 22.8 us
    pallas_call x1, Pallas kernels: 11.1 us -> 6.22 us  [hidden_layers(): pl.pallas_call(functools.partial(hidden_kernel, where, last, groups, dp /...]
    unnamed x60 -> x32, local copies, waits for them, and re-layouts: 3.54 us -> 8.1 us
    ppermute x4, waiting for transfers between devices: 11.9 us -> 15.2 us  [over_expert(): lax.ppermute(value, 'expert', [(i, (i + step) % size) for i in range(size)])]
    convert_element_type x3, other arithmetic: 2.57 us -> 0.67 us  [plus(): (share.astype(jnp.float32) + came_in.astype(jnp.float32)).astype(jnp.bflo...]
    pallas_call x1 -> x2, Pallas kernels: 10.9 us -> 9 us  [expert_results(): pl.pallas_call(functools.partial(result_kernel, last, begin, groups, dp /...]
    ppermute x4, waiting for transfers between devices: 9.53 us -> 7.81 us  [over_even(): return lax.ppermute(value, 'dp', pairs)]
    pallas_call x1, Pallas kernels: 7.77 us -> 6.32 us  [table_sums(): pl.pallas_call(functools.partial(table_kernel, lookups, part, planes, tup...]
  transfers between devices with their start and end apart: 29 -> 29, of which waited for: 18 -> 17; matrix products, arithmetic and copies ran while one was open for 6% -> 4% of each run, Pallas kernels for 14% -> 14%
where the time goes in v3:
time: 127 us; the launch traced here: 125 us
  waiting for transfers between devices  63.2 us (50%)
  Pallas kernels  25.2 us (20%)
  starting transfers between devices  22.8 us (18%)
  local copies, waits for them, and re-layouts  10 us (8%)
  other arithmetic  3.14 us (2%)
    ppermute x21, waiting for transfers between devices, swap(): return lax.ppermute(value, 'dp', [(i, i ^ bit) for i in range(size)])  40.1 us
    ppermute x4, waiting for transfers between devices, over_expert(): lax.ppermute(value, 'expert', [(i, (i + step) % size) for i in range(size)])  15.2 us
    ppermute x4, starting transfers between devices, over_even(): return lax.ppermute(value, 'dp', pairs)  12.2 us
    pallas_call x2, Pallas kernels, expert_results(): pl.pallas_call(functools.partial(result_kernel, last, begin, groups, dp /...  9 us
    unnamed x32, local copies, waits for them, and re-layouts  8.1 us
    ppermute x4, waiting for transfers between devices, over_even(): return lax.ppermute(value, 'dp', pairs)  7.81 us
    ppermute x21, starting transfers between devices, swap(): return lax.ppermute(value, 'dp', [(i, i ^ bit) for i in range(size)])  6.53 us
    pallas_call x1, Pallas kernels, table_sums(): pl.pallas_call(functools.partial(table_kernel, lookups, part, planes, tup...  6.32 us
  transfers between devices with their start and end apart: 29, of which 17 were waited for; matrix products, arithmetic and copies ran while one was open for 4% of the time, Pallas kernels for 14%

profile of v3, /device:TPU:10, one launch (start us, length us, event | category | flops | bytes accessed | tf_op | source)
XLA Modules:
  0.0 125.3 jit_solution(11162251019512320042)
XLA Ops:
  0.6 2.4 %shard_map.104 = (bf16[2,10,32,512]{3,2,1,0:T(8,128)(2,1)}, bf16[128,2688]{1,0:T(8,128)(2,1)}) custom-call(bf16[2,160,512]{2,1,0:T(8,128)(2,1)} %up_ref.1, bf16[2,32,2560]{2,1,0:T(8,128)(2,1)} %down_ref.1, bf16[128,2560]{1,0:T(8,128)(2,1)} %grad_ref.1, s32[2,128]{1,0:T(2,128)} %bitcast.16, f32[2,128]{1,0:T(2,128)} %bitcast.17, f32[4,128]{1,0:T(4,128)} %bitcast.13, ...), custom_call_target="tpu_custom_call" | custom-call | tf_op jit(solution)/shard_map/pallas_call | solution.py:95
  3.1 0.5 collective-permute-start
  3.6 1.5 %collective-permute-start.1 = (bf16[128,2688]{1,0:T(8,128)(2,1)}, bf16[128,2688]{1,0:T(8,128)(2,1)S(1)}, u32[]{:S(2)}, u32[]{:S(2)}) collective-permute-start(bf16[128,2688]{1,0:T(8,128)(2,1)} %get-tuple-element.41.refs_0_.refs_1_), channel_id=1, source_target_pairs={{0,1},{1,0},{2,3},{3,2},{4,5},{5,4},{6,7},{7,6},{8,9},{9,8},{10,11... | collective-permute-start | bytes 2064392 | tf_op jit(solution)/shard_map/ppermute | solution.py:28
  5.1 3.5 %collective-permute-start.4 = (bf16[2,10,32,512]{3,2,1,0:T(8,128)(2,1)}, bf16[2,10,32,512]{3,2,1,0:T(8,128)(2,1)S(1)}, u32[]{:S(2)}, u32[]{:S(2)}) collective-permute-start(bf16[2,10,32,512]{3,2,1,0:T(8,128)(2,1)} %get-tuple-element.56), channel_id=1, source_target_pairs={{8,16},{16,8},{10,18},{18,10},{12,20},{20,12},{14,22},{22,14},{9,1... | collective-permute-start | bytes 1966088 | tf_op jit(solution)/shard_map/ppermute | solution.py:37
  8.7 11.8 %collective-permute-done.refs_1_ = bf16[128,2688]{1,0:T(8,128)(2,1)S(1)} collective-permute-done((bf16[128,2688]{1,0:T(8,128)(2,1)}, bf16[128,2688]{1,0:T(8,128)(2,1)S(1)}, u32[]{:S(2)}, u32[]{:S(2)}) %collective-permute-start) | collective-permute-done | bytes 688160 | tf_op jit(solution)/shard_map/ppermute | solution.py:23
  20.7 0.9 copy-done.6
  21.6 1.5 %collective-permute-start.8 = (bf16[128,2688]{1,0:T(8,128)(2,1)S(1)}, bf16[128,2688]{1,0:T(8,128)(2,1)S(1)}, u32[]{:S(2)}, u32[]{:S(2)}) collective-permute-start(bf16[128,2688]{1,0:T(8,128)(2,1)S(1)} %collective-permute-done.refs_1_), channel_id=1, source_target_pairs={{0,1},{1,0},{2,3},{3,2},{4,5},{5,4},{6,7},{7,6},{8,9},{9,8},{10,11... | collective-permute-start | bytes 2064392 | tf_op jit(solution)/shard_map/ppermute | solution.py:28
  23.1 1.3 %collective-permute-done.4 = bf16[2,10,32,512]{3,2,1,0:T(8,128)(2,1)S(1)} collective-permute-done((bf16[2,10,32,512]{3,2,1,0:T(8,128)(2,1)}, bf16[2,10,32,512]{3,2,1,0:T(8,128)(2,1)S(1)}, u32[]{:S(2)}, u32[]{:S(2)}) %collective-permute-start.4) | collective-permute-done | bytes 655392 | tf_op jit(solution)/shard_map/ppermute | solution.py:37
  24.4 1.4 %collective-permute-done.6 = bf16[2,10,32,512]{3,2,1,0:T(8,128)(2,1)S(1)} collective-permute-done((bf16[2,10,32,512]{3,2,1,0:T(8,128)(2,1)}, bf16[2,10,32,512]{3,2,1,0:T(8,128)(2,1)S(1)}, u32[]{:S(2)}, u32[]{:S(2)}) %collective-permute-start.6) | collective-permute-done | bytes 655392 | tf_op jit(solution)/shard_map/ppermute | solution.py:23
  25.8 2.4 %collective-permute-start.7 = (bf16[2,10,32,512]{3,2,1,0:T(8,128)(2,1)S(1)}, bf16[2,10,32,512]{3,2,1,0:T(8,128)(2,1)S(1)}, u32[]{:S(2)}, u32[]{:S(2)}) collective-permute-start(bf16[2,10,32,512]{3,2,1,0:T(8,128)(2,1)S(1)} %collective-permute-done.6), channel_id=1, source_target_pairs={{8,16},{16,8},{10,18},{18,10},{12,20},{20,12},{14,22},{22,14},{9,1... | collective-permute-start | bytes 1966088 | tf_op jit(solution)/shard_map/ppermute | solution.py:37
  28.2 1.2 pad_maximum_fusion.refs_5_
  29.5 1.6 %collective-permute-start.13 = (bf16[2,2,10,32,512]{4,3,2,1,0:T(8,128)(2,1)S(1)}, bf16[2,2,10,32,512]{4,3,2,1,0:T(8,128)(2,1)}, u32[]{:S(2)}, u32[]{:S(2)}) collective-permute-start(bf16[2,2,10,32,512]{4,3,2,1,0:T(8,128)(2,1)S(1)} %pad_maximum_fusion.refs_5_), channel_id=1, source_target_pairs={{0,4},{2,6},{4,0},{6,2},{8,12},{10,14},{12,8},{14,10},{16,20},{18,... | collective-permute-start | bytes 3932168 | tf_op jit(solution)/shard_map/ppermute | solution.py:23
  31.1 6.6 %collective-permute-done.8.refs_5_ = bf16[128,2688]{1,0:T(8,128)(2,1)S(1)} collective-permute-done((bf16[128,2688]{1,0:T(8,128)(2,1)S(1)}, bf16[128,2688]{1,0:T(8,128)(2,1)S(1)}, u32[]{:S(2)}, u32[]{:S(2)}) %collective-permute-start.8) | collective-permute-done | bytes 688160 | tf_op jit(solution)/shard_map/ppermute | solution.py:28
  37.7 0.9 fusion
  38.6 1.0 fusion.1
  39.6 1.1 collective-permute-done.5
  40.7 2.9 %collective-permute-done.7 = bf16[2,10,32,512]{3,2,1,0:T(8,128)(2,1)S(1)} collective-permute-done((bf16[2,10,32,512]{3,2,1,0:T(8,128)(2,1)S(1)}, bf16[2,10,32,512]{3,2,1,0:T(8,128)(2,1)S(1)}, u32[]{:S(2)}, u32[]{:S(2)}) %collective-permute-start.7) | collective-permute-done | bytes 655392 | tf_op jit(solution)/shard_map/ppermute | solution.py:37
  43.7 0.9 copy-done.10
  44.6 0.9 copy-done.8
  45.5 0.5 collective-permute-start.19
  46.0 0.5 collective-permute-start.18
  46.5 0.9 collective-permute-done.9.refs_6_
  47.4 1.1 copy-done.3
  48.5 1.1 copy-done.5
  49.6 1.1 copy-done.7
  50.7 1.1 copy-done.9
  51.8 6.3 %shard_map.105 = (f32[2,10,32,512]{3,2,1,0:T(8,128)S(1)}, bf16[2,10,32,512]{3,2,1,0:T(8,128)(2,1)S(1)}, bf16[2,10,32,512]{3,2,1,0:T(8,128)(2,1)S(1)}, bf16[2,10,32,512]{3,2,1,0:T(8,128)(2,1)S(1)}) custom-call(s32[2]{0:T(128)S(1)} %pad_add_fusion.place_ref.refs_0_, bf16[128,2688]{1,0:T(8,128)(2,1)S(1)} %copy-done, bf16[128,2688]{1,0:T(8,128)(2,1)S(1)} %copy-done.5, ...), custom_call_target="tpu_custom_call" | custom-call | flops 2684354560 | bytes 8126464 | tf_op jit(solution)/shard_map/pallas_call | solution.py:193
  58.3 0.9 copy-done.13
  59.5 1.3 %collective-permute-done.13.refs_6_ = bf16[2,2,10,32,512]{4,3,2,1,0:T(8,128)(2,1)} collective-permute-done((bf16[2,2,10,32,512]{4,3,2,1,0:T(8,128)(2,1)S(1)}, bf16[2,2,10,32,512]{4,3,2,1,0:T(8,128)(2,1)}, u32[]{:S(2)}, u32[]{:S(2)}) %collective-permute-start.13) | collective-permute-done | bytes 1310752 | tf_op jit(solution)/shard_map/ppermute | solution.py:23
  60.8 1.5 %collective-permute-start.17 = (bf16[2,10,32,512]{3,2,1,0:T(8,128)(2,1)S(1)}, bf16[2,10,32,512]{3,2,1,0:T(8,128)(2,1)S(1)}, u32[]{:S(2)}, u32[]{:S(2)}) collective-permute-start(bf16[2,10,32,512]{3,2,1,0:T(8,128)(2,1)S(1)} %select_select_fusion.1.refs_7_), channel_id=1, source_target_pairs={{0,4},{2,6},{4,0},{6,2},{8,12},{10,14},{12,8},{14,10},{16,20},{18,... | collective-permute-start | bytes 1966088 | tf_op jit(solution)/shard_map/ppermute | solution.py:23
  62.3 12.8 %collective-permute-done.15 = bf16[2,10,32,512]{3,2,1,0:T(8,128)(2,1)S(1)} collective-permute-done((bf16[2,10,32,512]{3,2,1,0:T(8,128)(2,1)S(1)}, bf16[2,10,32,512]{3,2,1,0:T(8,128)(2,1)S(1)}, u32[]{:S(2)}, u32[]{:S(2)}) %collective-permute-start.15) | collective-permute-done | bytes 655392 | tf_op jit(solution)/shard_map/ppermute | solution.py:23
  75.2 2.0 %collective-permute-done.17.refs_8_ = bf16[2,10,32,512]{3,2,1,0:T(8,128)(2,1)S(1)} collective-permute-done((bf16[2,10,32,512]{3,2,1,0:T(8,128)(2,1)S(1)}, bf16[2,10,32,512]{3,2,1,0:T(8,128)(2,1)S(1)}, u32[]{:S(2)}, u32[]{:S(2)}) %collective-permute-start.17) | collective-permute-done | bytes 655392 | tf_op jit(solution)/shard_map/ppermute | solution.py:23
  77.2 0.5 collective-permute-start.23
  78.0 3.4 %collective-permute-start.16 = (bf16[2,10,32,512]{3,2,1,0:T(8,128)(2,1)S(1)}, bf16[2,10,32,512]{3,2,1,0:T(8,128)(2,1)S(1)}, u32[]{:S(2)}, u32[]{:S(2)}) collective-permute-start(bf16[2,10,32,512]{3,2,1,0:T(8,128)(2,1)S(1)} %add_convert_fusion.3), channel_id=1, source_target_pairs={{8,16},{16,8},{10,18},{18,10},{12,20},{20,12},{14,22},{22,14},{9,1... | collective-permute-start | bytes 1966088 | tf_op jit(solution)/shard_map/ppermute | solution.py:37
  81.5 1.6 %collective-permute-start.24 = (bf16[2,10,32,512]{3,2,1,0:T(8,128)(2,1)S(1)}, bf16[2,10,32,512]{3,2,1,0:T(8,128)(2,1)S(1)}, u32[]{:S(2)}, u32[]{:S(2)}) collective-permute-start(bf16[2,10,32,512]{3,2,1,0:T(8,128)(2,1)S(1)} %select_select_fusion.refs_11_), channel_id=1, source_target_pairs={{0,4},{2,6},{4,0},{6,2},{8,12},{10,14},{12,8},{14,10},{16,20},{18,... | collective-permute-start | bytes 1966088 | tf_op jit(solution)/shard_map/ppermute | solution.py:23
  83.1 6.2 %shard_map.106 = (bf16[2,512,2560]{2,1,0:T(8,128)(2,1)S(1)}, f32[256,1024]{1,0:T(8,128)S(1)}, f32[256,1024]{1,0:T(8,128)S(1)}) custom-call(s32[2]{0:T(128)S(1)} %pad_add_fusion.place_ref.refs_0_, bf16[128,2688]{1,0:T(8,128)(2,1)S(1)} %copy-done, bf16[128,2688]{1,0:T(8,128)(2,1)S(1)} %collective-permute-done.1.refs_4_.refs_2_.refs_1_, ...), custom_call_target="tpu_custom_call" | custom-call | flops 2684354560 | bytes 20971520 | tf_op jit(solution)/shard_map/pallas_call | solution.py:449
  89.3 5.4 %collective-permute-done.14 = bf16[2,10,32,512]{3,2,1,0:T(8,128)(2,1)S(1)} collective-permute-done((bf16[2,10,32,512]{3,2,1,0:T(8,128)(2,1)S(1)}, bf16[2,10,32,512]{3,2,1,0:T(8,128)(2,1)S(1)}, u32[]{:S(2)}, u32[]{:S(2)}) %collective-permute-start.14) | collective-permute-done | bytes 655392 | tf_op jit(solution)/shard_map/ppermute | solution.py:23
  94.7 1.9 %collective-permute-done.16 = bf16[2,10,32,512]{3,2,1,0:T(8,128)(2,1)S(1)} collective-permute-done((bf16[2,10,32,512]{3,2,1,0:T(8,128)(2,1)S(1)}, bf16[2,10,32,512]{3,2,1,0:T(8,128)(2,1)S(1)}, u32[]{:S(2)}, u32[]{:S(2)}) %collective-permute-start.16) | collective-permute-done | bytes 655392 | tf_op jit(solution)/shard_map/ppermute | solution.py:37
  96.6 1.3 %collective-permute-done.24.refs_4_ = bf16[2,10,32,512]{3,2,1,0:T(8,128)(2,1)S(1)} collective-permute-done((bf16[2,10,32,512]{3,2,1,0:T(8,128)(2,1)S(1)}, bf16[2,10,32,512]{3,2,1,0:T(8,128)(2,1)S(1)}, u32[]{:S(2)}, u32[]{:S(2)}) %collective-permute-start.24) | collective-permute-done | bytes 655392 | tf_op jit(solution)/shard_map/ppermute | solution.py:23
  97.9 2.1 %collective-permute-done.25.refs_5_ = bf16[2,10,32,512]{3,2,1,0:T(8,128)(2,1)S(1)} collective-permute-done((bf16[2,10,32,512]{3,2,1,0:T(8,128)(2,1)S(1)}, bf16[2,10,32,512]{3,2,1,0:T(8,128)(2,1)S(1)}, u32[]{:S(2)}, u32[]{:S(2)}) %collective-permute-start.25) | collective-permute-done | bytes 655392 | tf_op jit(solution)/shard_map/ppermute | solution.py:23
  100.0 4.5 %shard_map.108 = bf16[128,2560]{1,0:T(8,128)(2,1)S(1)} custom-call(s32[2]{0:T(128)S(1)} %pad_add_fusion.place_ref.refs_0_, bf16[128,2688]{1,0:T(8,128)(2,1)S(1)} %collective-permute-done.1.refs_4_.refs_2_.refs_1_, bf16[128,2560]{1,0:T(8,128)(2,1)S(1)} %collective-permute-done.18.refs_4_.refs_2_, bf16[2,512,2560]{2,1,0:T(8,128)(2,1)S(1)} %get-tuple-element.68.refs_3_, ...), custom_call_target="tpu_custom_call" | custom-call | flops 671088640 | bytes 9175040 | tf_op jit(solution)/shard_map/pallas_call | solution.py:491
  104.5 0.6 collective-permute-start.26
  105.6 2.9 %collective-permute-start.27 = (bf16[2,10,32,512]{3,2,1,0:T(8,128)(2,1)S(1)}, bf16[2,10,32,512]{3,2,1,0:T(8,128)(2,1)S(1)}, u32[]{:S(2)}, u32[]{:S(2)}) collective-permute-start(bf16[2,10,32,512]{3,2,1,0:T(8,128)(2,1)S(1)} %add_convert_fusion.1), channel_id=1, source_target_pairs={{8,16},{16,8},{10,18},{18,10},{12,20},{20,12},{14,22},{22,14},{9,1... | collective-permute-start | bytes 1966088 | tf_op jit(solution)/shard_map/ppermute | solution.py:37
  108.5 4.5 %shard_map.107 = f32[128,2560]{1,0:T(8,128)S(1)} custom-call(s32[2]{0:T(128)S(1)} %pad_add_fusion.place_ref.refs_0_, bf16[128,2688]{1,0:T(8,128)(2,1)S(1)} %copy-done, bf16[128,2560]{1,0:T(8,128)(2,1)S(1)} %copy-done.1, bf16[2,512,2560]{2,1,0:T(8,128)(2,1)S(1)} %get-tuple-element.68.refs_3_, bf16[2,10,32,512]{3,2,1,0:T(8,128)(2,1)S(1)} %collective-permute-done.24.refs_4_, ...), custom_call_target="tpu_custom_call" | custom-call | flops 671088640 | bytes 9175040 | tf_op jit(solution)/shard_map/pallas_call | solution.py:491
  113.0 8.4 %collective-permute-done.26 = bf16[128,2560]{1,0:T(8,128)(2,1)S(1)} collective-permute-done((bf16[128,2560]{1,0:T(8,128)(2,1)S(1)}, bf16[128,2560]{1,0:T(8,128)(2,1)S(1)}, u32[]{:S(2)}, u32[]{:S(2)}) %collective-permute-start.26) | collective-permute-done | bytes 655392 | tf_op jit(solution)/shard_map/ppermute | solution.py:28
  121.4 1.0 add_convert_fusion.2
  122.3 1.7 %collective-permute-done.27.refs_1_ = bf16[2,10,32,512]{3,2,1,0:T(8,128)(2,1)S(1)} collective-permute-done((bf16[2,10,32,512]{3,2,1,0:T(8,128)(2,1)S(1)}, bf16[2,10,32,512]{3,2,1,0:T(8,128)(2,1)S(1)}, u32[]{:S(2)}, u32[]{:S(2)}) %collective-permute-start.27) | collective-permute-done | bytes 655392 | tf_op jit(solution)/shard_map/ppermute | solution.py:37
  124.0 1.3 %shard_map.109 = f32[256,1280]{1,0:T(8,128)} custom-call(f32[2,10,32,512]{3,2,1,0:T(8,128)S(1)} %get-tuple-element.75.refs_0_, bf16[2,10,32,512]{3,2,1,0:T(8,128)(2,1)S(1)} %collective-permute-done.27.refs_1_, bf16[2,10,32,512]{3,2,1,0:T(8,128)(2,1)S(1)} %collective-permute-done.28.refs_2_), custom_call_target="tpu_custom_call" | custom-call | tf_op jit(solution)/shard_map/pallas_call | solution.py:233
  (59 shorter events, 1.9 us)
Async XLA Ops:
  3.1 17.4 %collective-permute-start = (bf16[128,2688]{1,0:T(8,128)(2,1)}, bf16[128,2688]{1,0:T(8,128)(2,1)S(1)}, u32[]{:S(2)}, u32[]{:S(2)}) collective-permute-start(bf16[128,2688]{1,0:T(8,128)(2,1)} %get-tuple-element.41.refs_0_.refs_1_), channel_id=1, source_target_pairs={{0,4},{2,6},{4,0},{6,2},{8,12},{10,14},{12,8},{14,10},{16,20},{18,... | collective-permute-start | bytes 2064392 | tf_op jit(solution)/shard_map/ppermute | solution.py:23
  3.6 17.1 %collective-permute-start.1 = (bf16[128,2688]{1,0:T(8,128)(2,1)}, bf16[128,2688]{1,0:T(8,128)(2,1)S(1)}, u32[]{:S(2)}, u32[]{:S(2)}) collective-permute-start(bf16[128,2688]{1,0:T(8,128)(2,1)} %get-tuple-element.41.refs_0_.refs_1_), channel_id=1, source_target_pairs={{0,1},{1,0},{2,3},{3,2},{4,5},{5,4},{6,7},{7,6},{8,9},{9,8},{10,11... | collective-permute-start | bytes 2064392 | tf_op jit(solution)/shard_map/ppermute | solution.py:28
  5.1 15.6 %collective-permute-start.2 = (bf16[128,2688]{1,0:T(8,128)(2,1)}, bf16[128,2688]{1,0:T(8,128)(2,1)S(1)}, u32[]{:S(2)}, u32[]{:S(2)}) collective-permute-start(bf16[128,2688]{1,0:T(8,128)(2,1)} %get-tuple-element.41.refs_0_.refs_1_), channel_id=1, source_target_pairs={{0,2},{2,0},{4,6},{6,4},{8,10},{10,8},{12,14},{14,12},{16,18},{18,... | collective-permute-start | bytes 2064392 | tf_op jit(solution)/shard_map/ppermute | solution.py:23
  5.1 19.2 %collective-permute-start.4 = (bf16[2,10,32,512]{3,2,1,0:T(8,128)(2,1)}, bf16[2,10,32,512]{3,2,1,0:T(8,128)(2,1)S(1)}, u32[]{:S(2)}, u32[]{:S(2)}) collective-permute-start(bf16[2,10,32,512]{3,2,1,0:T(8,128)(2,1)} %get-tuple-element.56), channel_id=1, source_target_pairs={{8,16},{16,8},{10,18},{18,10},{12,20},{20,12},{14,22},{22,14},{9,1... | collective-permute-start | bytes 1966088 | tf_op jit(solution)/shard_map/ppermute | solution.py:37
  8.6 17.1 %collective-permute-start.6 = (bf16[2,10,32,512]{3,2,1,0:T(8,128)(2,1)}, bf16[2,10,32,512]{3,2,1,0:T(8,128)(2,1)S(1)}, u32[]{:S(2)}, u32[]{:S(2)}) collective-permute-start(bf16[2,10,32,512]{3,2,1,0:T(8,128)(2,1)} %get-tuple-element.56), channel_id=1, source_target_pairs={{0,8},{2,10},{4,12},{6,14},{8,0},{10,2},{12,4},{14,6},{16,24},{18,... | collective-permute-start | bytes 1966088 | tf_op jit(solution)/shard_map/ppermute | solution.py:23
  20.5 9.0 %copy-start.4 = (bf16[128,2688]{1,0:T(8,128)(2,1)}, bf16[128,2688]{1,0:T(8,128)(2,1)S(1)}, u32[]{:S(2)}) copy-start(bf16[128,2688]{1,0:T(8,128)(2,1)S(1)} %collective-permute-done.refs_1_) | copy-start | bytes 2064388
  20.7 0.9 copy-start.6
  21.6 16.1 %collective-permute-start.8 = (bf16[128,2688]{1,0:T(8,128)(2,1)S(1)}, bf16[128,2688]{1,0:T(8,128)(2,1)S(1)}, u32[]{:S(2)}, u32[]{:S(2)}) collective-permute-start(bf16[128,2688]{1,0:T(8,128)(2,1)S(1)} %collective-permute-done.refs_1_), channel_id=1, source_target_pairs={{0,1},{1,0},{2,3},{3,2},{4,5},{5,4},{6,7},{7,6},{8,9},{9,8},{10,11... | collective-permute-start | bytes 2064392 | tf_op jit(solution)/shard_map/ppermute | solution.py:28
  24.4 5.1 %copy-start.12 = (bf16[2,10,32,512]{3,2,1,0:T(8,128)(2,1)}, bf16[2,10,32,512]{3,2,1,0:T(8,128)(2,1)S(1)}, u32[]{:S(2)}) copy-start(bf16[2,10,32,512]{3,2,1,0:T(8,128)(2,1)S(1)} %collective-permute-done.4) | copy-start | bytes 1966084
  24.4 16.4 %collective-permute-start.5 = (bf16[2,10,32,512]{3,2,1,0:T(8,128)(2,1)S(1)}, bf16[2,10,32,512]{3,2,1,0:T(8,128)(2,1)S(1)}, u32[]{:S(2)}, u32[]{:S(2)}) collective-permute-start(bf16[2,10,32,512]{3,2,1,0:T(8,128)(2,1)S(1)} %collective-permute-done.4), channel_id=1, source_target_pairs={{0,8},{2,10},{4,12},{6,14},{8,0},{10,2},{12,4},{14,6},{16,24},{18,... | collective-permute-start | bytes 1966088 | tf_op jit(solution)/shard_map/ppermute | solution.py:23
  25.8 17.9 %collective-permute-start.7 = (bf16[2,10,32,512]{3,2,1,0:T(8,128)(2,1)S(1)}, bf16[2,10,32,512]{3,2,1,0:T(8,128)(2,1)S(1)}, u32[]{:S(2)}, u32[]{:S(2)}) collective-permute-start(bf16[2,10,32,512]{3,2,1,0:T(8,128)(2,1)S(1)} %collective-permute-done.6), channel_id=1, source_target_pairs={{8,16},{16,8},{10,18},{18,10},{12,20},{20,12},{14,22},{22,14},{9,1... | collective-permute-start | bytes 1966088 | tf_op jit(solution)/shard_map/ppermute | solution.py:37
  28.2 15.5 %collective-permute-start.3 = (bf16[128,2688]{1,0:T(8,128)(2,1)S(1)}, bf16[128,2688]{1,0:T(8,128)(2,1)S(1)}, u32[]{:S(2)}, u32[]{:S(2)}) collective-permute-start(bf16[128,2688]{1,0:T(8,128)(2,1)S(1)} %collective-permute-done.refs_1_), channel_id=1, source_target_pairs={{0,2},{2,0},{4,6},{6,4},{8,10},{10,8},{12,14},{14,12},{16,18},{18,... | collective-permute-start | bytes 2064392 | tf_op jit(solution)/shard_map/ppermute | solution.py:23
  29.5 16.5 %copy-start.1 = (bf16[128,2560]{1,0:T(8,128)(2,1)S(1)}, bf16[128,2560]{1,0:T(8,128)(2,1)}, u32[]{:S(2)}) copy-start(bf16[128,2560]{1,0:T(8,128)(2,1)} %refs_2_.1) | copy-start | bytes 1966084
  29.5 17.9 %copy-start = (bf16[128,2688]{1,0:T(8,128)(2,1)S(1)}, bf16[128,2688]{1,0:T(8,128)(2,1)}, u32[]{:S(2)}) copy-start(bf16[128,2688]{1,0:T(8,128)(2,1)} %get-tuple-element.41.refs_0_.refs_1_) | copy-start | bytes 2064388
  29.5 31.3 %collective-permute-start.13 = (bf16[2,2,10,32,512]{4,3,2,1,0:T(8,128)(2,1)S(1)}, bf16[2,2,10,32,512]{4,3,2,1,0:T(8,128)(2,1)}, u32[]{:S(2)}, u32[]{:S(2)}) collective-permute-start(bf16[2,2,10,32,512]{4,3,2,1,0:T(8,128)(2,1)S(1)} %pad_maximum_fusion.refs_5_), channel_id=1, source_target_pairs={{0,4},{2,6},{4,0},{6,2},{8,12},{10,14},{12,8},{14,10},{16,20},{18,... | collective-permute-start | bytes 3932168 | tf_op jit(solution)/shard_map/ppermute | solution.py:23
  37.7 1.9 %copy-start.2 = (bf16[128,2688]{1,0:T(8,128)(2,1)}, bf16[128,2688]{1,0:T(8,128)(2,1)S(1)}, u32[]{:S(2)}) copy-start(bf16[128,2688]{1,0:T(8,128)(2,1)S(1)} %collective-permute-done.8.refs_5_) | copy-start | bytes 2064388
  38.6 6.9 %collective-permute-start.11 = (bf16[64,2688]{1,0:T(8,128)(2,1)}, bf16[64,2688]{1,0:T(8,128)(2,1)}, u32[]{:S(2)}, u32[]{:S(2)}) collective-permute-start(bf16[64,2688]{1,0:T(8,128)(2,1)} %get-tuple-element.81), channel_id=1, source_target_pairs={{0,2},{2,0},{4,6},{6,4},{8,10},{10,8},{12,14},{14,12},{16,18},{18,... | collective-permute-start | bytes 1032200 | tf_op jit(solution)/shard_map/ppermute | solution.py:23
  40.7 4.7 %copy-start.14 = (bf16[2,10,32,512]{3,2,1,0:T(8,128)(2,1)}, bf16[2,10,32,512]{3,2,1,0:T(8,128)(2,1)S(1)}, u32[]{:S(2)}) copy-start(bf16[2,10,32,512]{3,2,1,0:T(8,128)(2,1)S(1)} %collective-permute-done.5) | copy-start | bytes 1966084
  40.7 5.3 %collective-permute-start.12 = (bf16[64,2688]{1,0:T(8,128)(2,1)}, bf16[64,2688]{1,0:T(8,128)(2,1)}, u32[]{:S(2)}, u32[]{:S(2)}) collective-permute-start(bf16[64,2688]{1,0:T(8,128)(2,1)} %get-tuple-element.80), channel_id=1, source_target_pairs={{0,2},{2,0},{4,6},{6,4},{8,10},{10,8},{12,14},{14,12},{16,18},{18,... | collective-permute-start | bytes 1032200 | tf_op jit(solution)/shard_map/ppermute | solution.py:23
  43.7 0.9 copy-start.10
  43.7 2.8 %collective-permute-start.10 = (bf16[64,2688]{1,0:T(8,128)(2,1)}, bf16[64,2688]{1,0:T(8,128)(2,1)}, u32[]{:S(2)}, u32[]{:S(2)}) collective-permute-start(bf16[64,2688]{1,0:T(8,128)(2,1)} %get-tuple-element.82), channel_id=1, source_target_pairs={{0,2},{2,0},{4,6},{6,4},{8,10},{10,8},{12,14},{14,12},{16,18},{18,... | collective-permute-start | bytes 1032200 | tf_op jit(solution)/shard_map/ppermute | solution.py:23
  44.6 0.9 copy-start.8
  45.4 2.0 %collective-permute-start.9 = (bf16[64,2688]{1,0:T(8,128)(2,1)}, bf16[64,2688]{1,0:T(8,128)(2,1)}, u32[]{:S(2)}, u32[]{:S(2)}) collective-permute-start(bf16[64,2688]{1,0:T(8,128)(2,1)} %get-tuple-element.83), channel_id=1, source_target_pairs={{0,2},{2,0},{4,6},{6,4},{8,10},{10,8},{12,14},{14,12},{16,18},{18,... | collective-permute-start | bytes 1032200 | tf_op jit(solution)/shard_map/ppermute | solution.py:23
  45.5 32.4 %collective-permute-start.19 = (bf16[2,2,10,32,512]{4,3,2,1,0:T(8,128)(2,1)S(1)}, bf16[2,2,10,32,512]{4,3,2,1,0:T(8,128)(2,1)S(1)}, u32[]{:S(2)}, u32[]{:S(2)}) collective-permute-start(bf16[2,2,10,32,512]{4,3,2,1,0:T(8,128)(2,1)S(1)} %pad_maximum_fusion.refs_5_), channel_id=1, source_target_pairs={{0,2},{2,0},{4,6},{6,4},{8,10},{10,8},{12,14},{14,12},{16,18},{18,... | collective-permute-start | bytes 3932168 | tf_op jit(solution)/shard_map/ppermute | solution.py:23
  46.0 29.2 %collective-permute-start.18 = (bf16[128,2560]{1,0:T(8,128)(2,1)S(1)}, bf16[128,2560]{1,0:T(8,128)(2,1)S(1)}, u32[]{:S(2)}, u32[]{:S(2)}) collective-permute-start(bf16[128,2560]{1,0:T(8,128)(2,1)S(1)} %copy-done.1), channel_id=1, source_target_pairs={{0,1},{1,0},{2,3},{3,2},{4,5},{5,4},{6,7},{7,6},{8,9},{9,8},{10,11... | collective-permute-start | bytes 1966088 | tf_op jit(solution)/shard_map/ppermute | solution.py:28
  47.4 1.1 copy-start.3
  48.5 1.1 copy-start.5
  49.6 1.1 copy-start.7
  50.7 1.1 copy-start.9
  51.8 6.4 %copy-start.11 = (bf16[2,10,32,512]{3,2,1,0:T(8,128)(2,1)S(1)}, bf16[2,10,32,512]{3,2,1,0:T(8,128)(2,1)}, u32[]{:S(2)}) copy-start(bf16[2,10,32,512]{3,2,1,0:T(8,128)(2,1)} %copy-done.10) | copy-start | bytes 1966084
  58.1 1.1 copy-start.13
  58.2 1.3 %copy-start.15 = (bf16[2,10,32,512]{3,2,1,0:T(8,128)(2,1)S(1)}, bf16[2,10,32,512]{3,2,1,0:T(8,128)(2,1)}, u32[]{:S(2)}) copy-start(bf16[2,10,32,512]{3,2,1,0:T(8,128)(2,1)} %copy-done.14) | copy-start | bytes 1966084
  58.3 16.8 %collective-permute-start.15 = (bf16[2,10,32,512]{3,2,1,0:T(8,128)(2,1)S(1)}, bf16[2,10,32,512]{3,2,1,0:T(8,128)(2,1)S(1)}, u32[]{:S(2)}, u32[]{:S(2)}) collective-permute-start(bf16[2,10,32,512]{3,2,1,0:T(8,128)(2,1)S(1)} %broadcast_select_fusion), channel_id=1, source_target_pairs={{0,8},{2,10},{4,12},{6,14},{8,0},{10,2},{12,4},{14,6},{16,24},{18,... | collective-permute-start | bytes 1966088 | tf_op jit(solution)/shard_map/ppermute | solution.py:23
  60.8 16.4 %collective-permute-start.17 = (bf16[2,10,32,512]{3,2,1,0:T(8,128)(2,1)S(1)}, bf16[2,10,32,512]{3,2,1,0:T(8,128)(2,1)S(1)}, u32[]{:S(2)}, u32[]{:S(2)}) collective-permute-start(bf16[2,10,32,512]{3,2,1,0:T(8,128)(2,1)S(1)} %select_select_fusion.1.refs_7_), channel_id=1, source_target_pairs={{0,4},{2,6},{4,0},{6,2},{8,12},{10,14},{12,8},{14,10},{16,20},{18,... | collective-permute-start | bytes 1966088 | tf_op jit(solution)/shard_map/ppermute | solution.py:23
  62.3 15.7 %collective-permute-start.21 = (bf16[2,10,32,512]{3,2,1,0:T(8,128)(2,1)S(1)}, bf16[2,10,32,512]{3,2,1,0:T(8,128)(2,1)S(1)}, u32[]{:S(2)}, u32[]{:S(2)}) collective-permute-start(bf16[2,10,32,512]{3,2,1,0:T(8,128)(2,1)S(1)} %select_select_fusion.1.refs_7_), channel_id=1, source_target_pairs={{0,2},{2,0},{4,6},{6,4},{8,10},{10,8},{12,14},{14,12},{16,18},{18,... | collective-permute-start | bytes 1966088 | tf_op jit(solution)/shard_map/ppermute | solution.py:23
  75.1 8.0 %collective-permute-start.20 = (bf16[2,2,10,32,512]{4,3,2,1,0:T(8,128)(2,1)}, bf16[2,2,10,32,512]{4,3,2,1,0:T(8,128)(2,1)S(1)}, u32[]{:S(2)}, u32[]{:S(2)}) collective-permute-start(bf16[2,2,10,32,512]{4,3,2,1,0:T(8,128)(2,1)} %collective-permute-done.13.refs_6_), channel_id=1, source_target_pairs={{0,2},{2,0},{4,6},{6,4},{8,10},{10,8},{12,14},{14,12},{16,18},{18,... | collective-permute-start | bytes 3932168 | tf_op jit(solution)/shard_map/ppermute | solution.py:23
  77.2 4.3 %collective-permute-start.22 = (bf16[2,10,32,512]{3,2,1,0:T(8,128)(2,1)S(1)}, bf16[2,10,32,512]{3,2,1,0:T(8,128)(2,1)S(1)}, u32[]{:S(2)}, u32[]{:S(2)}) collective-permute-start(bf16[2,10,32,512]{3,2,1,0:T(8,128)(2,1)S(1)} %collective-permute-done.17.refs_8_), channel_id=1, source_target_pairs={{0,2},{2,0},{4,6},{6,4},{8,10},{10,8},{12,14},{14,12},{16,18},{18,... | collective-permute-start | bytes 1966088 | tf_op jit(solution)/shard_map/ppermute | solution.py:23
  77.2 5.8 %collective-permute-start.23 = (bf16[2,10,32,512]{3,2,1,0:T(8,128)(2,1)S(1)}, bf16[2,10,32,512]{3,2,1,0:T(8,128)(2,1)S(1)}, u32[]{:S(2)}, u32[]{:S(2)}) collective-permute-start(bf16[2,10,32,512]{3,2,1,0:T(8,128)(2,1)S(1)} %select_select_fusion.refs_11_), channel_id=1, source_target_pairs={{0,2},{2,0},{4,6},{6,4},{8,10},{10,8},{12,14},{14,12},{16,18},{18,... | collective-permute-start | bytes 1966088 | tf_op jit(solution)/shard_map/ppermute | solution.py:23
  77.9 16.7 %collective-permute-start.14 = (bf16[2,10,32,512]{3,2,1,0:T(8,128)(2,1)S(1)}, bf16[2,10,32,512]{3,2,1,0:T(8,128)(2,1)S(1)}, u32[]{:S(2)}, u32[]{:S(2)}) collective-permute-start(bf16[2,10,32,512]{3,2,1,0:T(8,128)(2,1)S(1)} %get-tuple-element.57), channel_id=1, source_target_pairs={{0,8},{2,10},{4,12},{6,14},{8,0},{10,2},{12,4},{14,6},{16,24},{18,... | collective-permute-start | bytes 1966088 | tf_op jit(solution)/shard_map/ppermute | solution.py:23
  78.0 18.5 %collective-permute-start.16 = (bf16[2,10,32,512]{3,2,1,0:T(8,128)(2,1)S(1)}, bf16[2,10,32,512]{3,2,1,0:T(8,128)(2,1)S(1)}, u32[]{:S(2)}, u32[]{:S(2)}) collective-permute-start(bf16[2,10,32,512]{3,2,1,0:T(8,128)(2,1)S(1)} %add_convert_fusion.3), channel_id=1, source_target_pairs={{8,16},{16,8},{10,18},{18,10},{12,20},{20,12},{14,22},{22,14},{9,1... | collective-permute-start | bytes 1966088 | tf_op jit(solution)/shard_map/ppermute | solution.py:37
  81.5 16.4 %collective-permute-start.24 = (bf16[2,10,32,512]{3,2,1,0:T(8,128)(2,1)S(1)}, bf16[2,10,32,512]{3,2,1,0:T(8,128)(2,1)S(1)}, u32[]{:S(2)}, u32[]{:S(2)}) collective-permute-start(bf16[2,10,32,512]{3,2,1,0:T(8,128)(2,1)S(1)} %select_select_fusion.refs_11_), channel_id=1, source_target_pairs={{0,4},{2,6},{4,0},{6,2},{8,12},{10,14},{12,8},{14,10},{16,20},{18,... | collective-permute-start | bytes 1966088 | tf_op jit(solution)/shard_map/ppermute | solution.py:23
  97.9 2.1 %collective-permute-start.25 = (bf16[2,10,32,512]{3,2,1,0:T(8,128)(2,1)S(1)}, bf16[2,10,32,512]{3,2,1,0:T(8,128)(2,1)S(1)}, u32[]{:S(2)}, u32[]{:S(2)}) collective-permute-start(bf16[2,10,32,512]{3,2,1,0:T(8,128)(2,1)S(1)} %collective-permute-done.24.refs_4_), channel_id=1, source_target_pairs={{0,2},{2,0},{4,6},{6,4},{8,10},{10,8},{12,14},{14,12},{16,18},{18,... | collective-permute-start | bytes 1966088 | tf_op jit(solution)/shard_map/ppermute | solution.py:23
  104.5 16.8 %collective-permute-start.26 = (bf16[128,2560]{1,0:T(8,128)(2,1)S(1)}, bf16[128,2560]{1,0:T(8,128)(2,1)S(1)}, u32[]{:S(2)}, u32[]{:S(2)}) collective-permute-start(bf16[128,2560]{1,0:T(8,128)(2,1)S(1)} %shard_map.108), channel_id=1, source_target_pairs={{0,1},{1,0},{2,3},{3,2},{4,5},{5,4},{6,7},{7,6},{8,9},{9,8},{10,11... | collective-permute-start | bytes 1966088 | tf_op jit(solution)/shard_map/ppermute | solution.py:28
  105.3 17.0 %collective-permute-start.28 = (bf16[2,10,32,512]{3,2,1,0:T(8,128)(2,1)S(1)}, bf16[2,10,32,512]{3,2,1,0:T(8,128)(2,1)S(1)}, u32[]{:S(2)}, u32[]{:S(2)}) collective-permute-start(bf16[2,10,32,512]{3,2,1,0:T(8,128)(2,1)S(1)} %add_convert_fusion), channel_id=1, source_target_pairs={{0,8},{2,10},{4,12},{6,14},{8,0},{10,2},{12,4},{14,6},{16,24},{18,... | collective-permute-start | bytes 1966088 | tf_op jit(solution)/shard_map/ppermute | solution.py:23
  105.6 18.4 %collective-permute-start.27 = (bf16[2,10,32,512]{3,2,1,0:T(8,128)(2,1)S(1)}, bf16[2,10,32,512]{3,2,1,0:T(8,128)(2,1)S(1)}, u32[]{:S(2)}, u32[]{:S(2)}) collective-permute-start(bf16[2,10,32,512]{3,2,1,0:T(8,128)(2,1)S(1)} %add_convert_fusion.1), channel_id=1, source_target_pairs={{8,16},{16,8},{10,18},{18,10},{12,20},{20,12},{14,22},{22,14},{9,1... | collective-permute-start | bytes 1966088 | tf_op jit(solution)/shard_map/ppermute | solution.py:37

commit v4 on v3

--- a/solution.py
+++ b/solution.py
@@ -209,7 +209,7 @@
         ),
         cost_estimate=pl.CostEstimate(
             flops=2 * len(offsets) * rows * count * half,
-            bytes_accessed=2 * count * total + 2 * len(offsets) * rows * half,
+            bytes_accessed=1 << 12,
             transcendentals=0,
         ),
     )(place, *blocks)

time: 127 us -> 127 us (level)
  no operation moved by 1% of the time
where the time goes in v4:
time: 127 us; the launch traced here: 125 us
  waiting for transfers between devices  63.2 us (50%)
  Pallas kernels  25.2 us (20%)
  starting transfers between devices  22.8 us (18%)
  local copies, waits for them, and re-layouts  10 us (8%)
  other arithmetic  3.14 us (2%)
    ppermute x21, waiting for transfers between devices, swap(): return lax.ppermute(value, 'dp', [(i, i ^ bit) for i in range(size)])  40.1 us
    ppermute x4, waiting for transfers between devices, over_expert(): lax.ppermute(value, 'expert', [(i, (i + step) % size) for i in range(size)])  15.2 us
    ppermute x4, starting transfers between devices, over_even(): return lax.ppermute(value, 'dp', pairs)  12.2 us
    pallas_call x2, Pallas kernels, expert_results(): pl.pallas_call(functools.partial(result_kernel, last, begin, groups, dp /...  9 us
    unnamed x32, local copies, waits for them, and re-layouts  8.1 us
    ppermute x4, waiting for transfers between devices, over_even(): return lax.ppermute(value, 'dp', pairs)  7.81 us
    ppermute x21, starting transfers between devices, swap(): return lax.ppermute(value, 'dp', [(i, i ^ bit) for i in range(size)])  6.53 us
    pallas_call x1, Pallas kernels, table_sums(): pl.pallas_call(functools.partial(table_kernel, lookups, part, planes, tup...  6.32 us
  transfers between devices with their start and end apart: 29, of which 17 were waited for; matrix products, arithmetic and copies ran while one was open for 4% of the time, Pallas kernels for 14%

profile of v4, /device:TPU:10, one launch (start us, length us, event | category | flops | bytes accessed | tf_op | source)
XLA Modules:
  0.0 125.3 jit_solution(11162251019512320042)
XLA Ops:
  0.6 2.4 %shard_map.104 = (bf16[2,10,32,512]{3,2,1,0:T(8,128)(2,1)}, bf16[128,2688]{1,0:T(8,128)(2,1)}) custom-call(bf16[2,160,512]{2,1,0:T(8,128)(2,1)} %up_ref.1, bf16[2,32,2560]{2,1,0:T(8,128)(2,1)} %down_ref.1, bf16[128,2560]{1,0:T(8,128)(2,1)} %grad_ref.1, s32[2,128]{1,0:T(2,128)} %bitcast.16, f32[2,128]{1,0:T(2,128)} %bitcast.17, f32[4,128]{1,0:T(4,128)} %bitcast.13, ...), custom_call_target="tpu_custom_call" | custom-call | tf_op jit(solution)/shard_map/pallas_call | solution.py:95
  3.1 0.5 collective-permute-start
  3.6 1.5 %collective-permute-start.1 = (bf16[128,2688]{1,0:T(8,128)(2,1)}, bf16[128,2688]{1,0:T(8,128)(2,1)S(1)}, u32[]{:S(2)}, u32[]{:S(2)}) collective-permute-start(bf16[128,2688]{1,0:T(8,128)(2,1)} %get-tuple-element.41.refs_0_.refs_1_), channel_id=1, source_target_pairs={{0,1},{1,0},{2,3},{3,2},{4,5},{5,4},{6,7},{7,6},{8,9},{9,8},{10,11... | collective-permute-start | bytes 2064392 | tf_op jit(solution)/shard_map/ppermute | solution.py:28
  5.1 3.5 %collective-permute-start.4 = (bf16[2,10,32,512]{3,2,1,0:T(8,128)(2,1)}, bf16[2,10,32,512]{3,2,1,0:T(8,128)(2,1)S(1)}, u32[]{:S(2)}, u32[]{:S(2)}) collective-permute-start(bf16[2,10,32,512]{3,2,1,0:T(8,128)(2,1)} %get-tuple-element.56), channel_id=1, source_target_pairs={{8,16},{16,8},{10,18},{18,10},{12,20},{20,12},{14,22},{22,14},{9,1... | collective-permute-start | bytes 1966088 | tf_op jit(solution)/shard_map/ppermute | solution.py:37
  8.7 11.8 %collective-permute-done.refs_1_ = bf16[128,2688]{1,0:T(8,128)(2,1)S(1)} collective-permute-done((bf16[128,2688]{1,0:T(8,128)(2,1)}, bf16[128,2688]{1,0:T(8,128)(2,1)S(1)}, u32[]{:S(2)}, u32[]{:S(2)}) %collective-permute-start) | collective-permute-done | bytes 688160 | tf_op jit(solution)/shard_map/ppermute | solution.py:23
  20.7 0.9 copy-done.6
  21.6 1.5 %collective-permute-start.8 = (bf16[128,2688]{1,0:T(8,128)(2,1)S(1)}, bf16[128,2688]{1,0:T(8,128)(2,1)S(1)}, u32[]{:S(2)}, u32[]{:S(2)}) collective-permute-start(bf16[128,2688]{1,0:T(8,128)(2,1)S(1)} %collective-permute-done.refs_1_), channel_id=1, source_target_pairs={{0,1},{1,0},{2,3},{3,2},{4,5},{5,4},{6,7},{7,6},{8,9},{9,8},{10,11... | collective-permute-start | bytes 2064392 | tf_op jit(solution)/shard_map/ppermute | solution.py:28
  23.1 1.3 %collective-permute-done.4 = bf16[2,10,32,512]{3,2,1,0:T(8,128)(2,1)S(1)} collective-permute-done((bf16[2,10,32,512]{3,2,1,0:T(8,128)(2,1)}, bf16[2,10,32,512]{3,2,1,0:T(8,128)(2,1)S(1)}, u32[]{:S(2)}, u32[]{:S(2)}) %collective-permute-start.4) | collective-permute-done | bytes 655392 | tf_op jit(solution)/shard_map/ppermute | solution.py:37
  24.4 1.4 %collective-permute-done.6 = bf16[2,10,32,512]{3,2,1,0:T(8,128)(2,1)S(1)} collective-permute-done((bf16[2,10,32,512]{3,2,1,0:T(8,128)(2,1)}, bf16[2,10,32,512]{3,2,1,0:T(8,128)(2,1)S(1)}, u32[]{:S(2)}, u32[]{:S(2)}) %collective-permute-start.6) | collective-permute-done | bytes 655392 | tf_op jit(solution)/shard_map/ppermute | solution.py:23
  25.8 2.4 %collective-permute-start.7 = (bf16[2,10,32,512]{3,2,1,0:T(8,128)(2,1)S(1)}, bf16[2,10,32,512]{3,2,1,0:T(8,128)(2,1)S(1)}, u32[]{:S(2)}, u32[]{:S(2)}) collective-permute-start(bf16[2,10,32,512]{3,2,1,0:T(8,128)(2,1)S(1)} %collective-permute-done.6), channel_id=1, source_target_pairs={{8,16},{16,8},{10,18},{18,10},{12,20},{20,12},{14,22},{22,14},{9,1... | collective-permute-start | bytes 1966088 | tf_op jit(solution)/shard_map/ppermute | solution.py:37
  28.2 1.2 pad_maximum_fusion.refs_5_
  29.5 1.6 %collective-permute-start.13 = (bf16[2,2,10,32,512]{4,3,2,1,0:T(8,128)(2,1)S(1)}, bf16[2,2,10,32,512]{4,3,2,1,0:T(8,128)(2,1)}, u32[]{:S(2)}, u32[]{:S(2)}) collective-permute-start(bf16[2,2,10,32,512]{4,3,2,1,0:T(8,128)(2,1)S(1)} %pad_maximum_fusion.refs_5_), channel_id=1, source_target_pairs={{0,4},{2,6},{4,0},{6,2},{8,12},{10,14},{12,8},{14,10},{16,20},{18,... | collective-permute-start | bytes 3932168 | tf_op jit(solution)/shard_map/ppermute | solution.py:23
  31.1 6.6 %collective-permute-done.8.refs_5_ = bf16[128,2688]{1,0:T(8,128)(2,1)S(1)} collective-permute-done((bf16[128,2688]{1,0:T(8,128)(2,1)S(1)}, bf16[128,2688]{1,0:T(8,128)(2,1)S(1)}, u32[]{:S(2)}, u32[]{:S(2)}) %collective-permute-start.8) | collective-permute-done | bytes 688160 | tf_op jit(solution)/shard_map/ppermute | solution.py:28
  37.7 0.9 fusion
  38.6 1.0 fusion.1
  39.6 1.1 collective-permute-done.5
  40.7 2.9 %collective-permute-done.7 = bf16[2,10,32,512]{3,2,1,0:T(8,128)(2,1)S(1)} collective-permute-done((bf16[2,10,32,512]{3,2,1,0:T(8,128)(2,1)S(1)}, bf16[2,10,32,512]{3,2,1,0:T(8,128)(2,1)S(1)}, u32[]{:S(2)}, u32[]{:S(2)}) %collective-permute-start.7) | collective-permute-done | bytes 655392 | tf_op jit(solution)/shard_map/ppermute | solution.py:37
  43.7 0.9 copy-done.10
  44.6 0.9 copy-done.8
  45.5 0.5 collective-permute-start.19
  46.0 0.5 collective-permute-start.18
  46.5 0.9 collective-permute-done.9.refs_6_
  47.4 1.1 copy-done.3
  48.5 1.1 copy-done.5
  49.6 1.1 copy-done.7
  50.7 1.1 copy-done.9
  51.8 6.3 %shard_map.105 = (f32[2,10,32,512]{3,2,1,0:T(8,128)S(1)}, bf16[2,10,32,512]{3,2,1,0:T(8,128)(2,1)S(1)}, bf16[2,10,32,512]{3,2,1,0:T(8,128)(2,1)S(1)}, bf16[2,10,32,512]{3,2,1,0:T(8,128)(2,1)S(1)}) custom-call(s32[2]{0:T(128)S(1)} %pad_add_fusion.place_ref.refs_0_, bf16[128,2688]{1,0:T(8,128)(2,1)S(1)} %copy-done, bf16[128,2688]{1,0:T(8,128)(2,1)S(1)} %copy-done.5, ...), custom_call_target="tpu_custom_call" | custom-call | flops 2684354560 | bytes 4096 | tf_op jit(solution)/shard_map/pallas_call | solution.py:193
  58.3 0.9 copy-done.13
  59.5 1.3 %collective-permute-done.13.refs_6_ = bf16[2,2,10,32,512]{4,3,2,1,0:T(8,128)(2,1)} collective-permute-done((bf16[2,2,10,32,512]{4,3,2,1,0:T(8,128)(2,1)S(1)}, bf16[2,2,10,32,512]{4,3,2,1,0:T(8,128)(2,1)}, u32[]{:S(2)}, u32[]{:S(2)}) %collective-permute-start.13) | collective-permute-done | bytes 1310752 | tf_op jit(solution)/shard_map/ppermute | solution.py:23
  60.8 1.5 %collective-permute-start.17 = (bf16[2,10,32,512]{3,2,1,0:T(8,128)(2,1)S(1)}, bf16[2,10,32,512]{3,2,1,0:T(8,128)(2,1)S(1)}, u32[]{:S(2)}, u32[]{:S(2)}) collective-permute-start(bf16[2,10,32,512]{3,2,1,0:T(8,128)(2,1)S(1)} %select_select_fusion.1.refs_7_), channel_id=1, source_target_pairs={{0,4},{2,6},{4,0},{6,2},{8,12},{10,14},{12,8},{14,10},{16,20},{18,... | collective-permute-start | bytes 1966088 | tf_op jit(solution)/shard_map/ppermute | solution.py:23
  62.3 12.8 %collective-permute-done.15 = bf16[2,10,32,512]{3,2,1,0:T(8,128)(2,1)S(1)} collective-permute-done((bf16[2,10,32,512]{3,2,1,0:T(8,128)(2,1)S(1)}, bf16[2,10,32,512]{3,2,1,0:T(8,128)(2,1)S(1)}, u32[]{:S(2)}, u32[]{:S(2)}) %collective-permute-start.15) | collective-permute-done | bytes 655392 | tf_op jit(solution)/shard_map/ppermute | solution.py:23
  75.2 2.0 %collective-permute-done.17.refs_8_ = bf16[2,10,32,512]{3,2,1,0:T(8,128)(2,1)S(1)} collective-permute-done((bf16[2,10,32,512]{3,2,1,0:T(8,128)(2,1)S(1)}, bf16[2,10,32,512]{3,2,1,0:T(8,128)(2,1)S(1)}, u32[]{:S(2)}, u32[]{:S(2)}) %collective-permute-start.17) | collective-permute-done | bytes 655392 | tf_op jit(solution)/shard_map/ppermute | solution.py:23
  77.2 0.5 collective-permute-start.23
  78.0 3.4 %collective-permute-start.16 = (bf16[2,10,32,512]{3,2,1,0:T(8,128)(2,1)S(1)}, bf16[2,10,32,512]{3,2,1,0:T(8,128)(2,1)S(1)}, u32[]{:S(2)}, u32[]{:S(2)}) collective-permute-start(bf16[2,10,32,512]{3,2,1,0:T(8,128)(2,1)S(1)} %add_convert_fusion.3), channel_id=1, source_target_pairs={{8,16},{16,8},{10,18},{18,10},{12,20},{20,12},{14,22},{22,14},{9,1... | collective-permute-start | bytes 1966088 | tf_op jit(solution)/shard_map/ppermute | solution.py:37
  81.5 1.6 %collective-permute-start.24 = (bf16[2,10,32,512]{3,2,1,0:T(8,128)(2,1)S(1)}, bf16[2,10,32,512]{3,2,1,0:T(8,128)(2,1)S(1)}, u32[]{:S(2)}, u32[]{:S(2)}) collective-permute-start(bf16[2,10,32,512]{3,2,1,0:T(8,128)(2,1)S(1)} %select_select_fusion.refs_11_), channel_id=1, source_target_pairs={{0,4},{2,6},{4,0},{6,2},{8,12},{10,14},{12,8},{14,10},{16,20},{18,... | collective-permute-start | bytes 1966088 | tf_op jit(solution)/shard_map/ppermute | solution.py:23
  83.1 6.2 %shard_map.106 = (bf16[2,512,2560]{2,1,0:T(8,128)(2,1)S(1)}, f32[256,1024]{1,0:T(8,128)S(1)}, f32[256,1024]{1,0:T(8,128)S(1)}) custom-call(s32[2]{0:T(128)S(1)} %pad_add_fusion.place_ref.refs_0_, bf16[128,2688]{1,0:T(8,128)(2,1)S(1)} %copy-done, bf16[128,2688]{1,0:T(8,128)(2,1)S(1)} %collective-permute-done.1.refs_4_.refs_2_.refs_1_, ...), custom_call_target="tpu_custom_call" | custom-call | flops 2684354560 | bytes 20971520 | tf_op jit(solution)/shard_map/pallas_call | solution.py:449
  89.3 5.4 %collective-permute-done.14 = bf16[2,10,32,512]{3,2,1,0:T(8,128)(2,1)S(1)} collective-permute-done((bf16[2,10,32,512]{3,2,1,0:T(8,128)(2,1)S(1)}, bf16[2,10,32,512]{3,2,1,0:T(8,128)(2,1)S(1)}, u32[]{:S(2)}, u32[]{:S(2)}) %collective-permute-start.14) | collective-permute-done | bytes 655392 | tf_op jit(solution)/shard_map/ppermute | solution.py:23
  94.7 1.9 %collective-permute-done.16 = bf16[2,10,32,512]{3,2,1,0:T(8,128)(2,1)S(1)} collective-permute-done((bf16[2,10,32,512]{3,2,1,0:T(8,128)(2,1)S(1)}, bf16[2,10,32,512]{3,2,1,0:T(8,128)(2,1)S(1)}, u32[]{:S(2)}, u32[]{:S(2)}) %collective-permute-start.16) | collective-permute-done | bytes 655392 | tf_op jit(solution)/shard_map/ppermute | solution.py:37
  96.6 1.3 %collective-permute-done.24.refs_4_ = bf16[2,10,32,512]{3,2,1,0:T(8,128)(2,1)S(1)} collective-permute-done((bf16[2,10,32,512]{3,2,1,0:T(8,128)(2,1)S(1)}, bf16[2,10,32,512]{3,2,1,0:T(8,128)(2,1)S(1)}, u32[]{:S(2)}, u32[]{:S(2)}) %collective-permute-start.24) | collective-permute-done | bytes 655392 | tf_op jit(solution)/shard_map/ppermute | solution.py:23
  97.9 2.1 %collective-permute-done.25.refs_5_ = bf16[2,10,32,512]{3,2,1,0:T(8,128)(2,1)S(1)} collective-permute-done((bf16[2,10,32,512]{3,2,1,0:T(8,128)(2,1)S(1)}, bf16[2,10,32,512]{3,2,1,0:T(8,128)(2,1)S(1)}, u32[]{:S(2)}, u32[]{:S(2)}) %collective-permute-start.25) | collective-permute-done | bytes 655392 | tf_op jit(solution)/shard_map/ppermute | solution.py:23
  100.0 4.5 %shard_map.108 = bf16[128,2560]{1,0:T(8,128)(2,1)S(1)} custom-call(s32[2]{0:T(128)S(1)} %pad_add_fusion.place_ref.refs_0_, bf16[128,2688]{1,0:T(8,128)(2,1)S(1)} %collective-permute-done.1.refs_4_.refs_2_.refs_1_, bf16[128,2560]{1,0:T(8,128)(2,1)S(1)} %collective-permute-done.18.refs_4_.refs_2_, bf16[2,512,2560]{2,1,0:T(8,128)(2,1)S(1)} %get-tuple-element.68.refs_3_, ...), custom_call_target="tpu_custom_call" | custom-call | flops 671088640 | bytes 9175040 | tf_op jit(solution)/shard_map/pallas_call | solution.py:491
  104.5 0.6 collective-permute-start.26
  105.6 2.9 %collective-permute-start.27 = (bf16[2,10,32,512]{3,2,1,0:T(8,128)(2,1)S(1)}, bf16[2,10,32,512]{3,2,1,0:T(8,128)(2,1)S(1)}, u32[]{:S(2)}, u32[]{:S(2)}) collective-permute-start(bf16[2,10,32,512]{3,2,1,0:T(8,128)(2,1)S(1)} %add_convert_fusion.1), channel_id=1, source_target_pairs={{8,16},{16,8},{10,18},{18,10},{12,20},{20,12},{14,22},{22,14},{9,1... | collective-permute-start | bytes 1966088 | tf_op jit(solution)/shard_map/ppermute | solution.py:37
  108.5 4.5 %shard_map.107 = f32[128,2560]{1,0:T(8,128)S(1)} custom-call(s32[2]{0:T(128)S(1)} %pad_add_fusion.place_ref.refs_0_, bf16[128,2688]{1,0:T(8,128)(2,1)S(1)} %copy-done, bf16[128,2560]{1,0:T(8,128)(2,1)S(1)} %copy-done.1, bf16[2,512,2560]{2,1,0:T(8,128)(2,1)S(1)} %get-tuple-element.68.refs_3_, bf16[2,10,32,512]{3,2,1,0:T(8,128)(2,1)S(1)} %collective-permute-done.24.refs_4_, ...), custom_call_target="tpu_custom_call" | custom-call | flops 671088640 | bytes 9175040 | tf_op jit(solution)/shard_map/pallas_call | solution.py:491
  113.0 8.4 %collective-permute-done.26 = bf16[128,2560]{1,0:T(8,128)(2,1)S(1)} collective-permute-done((bf16[128,2560]{1,0:T(8,128)(2,1)S(1)}, bf16[128,2560]{1,0:T(8,128)(2,1)S(1)}, u32[]{:S(2)}, u32[]{:S(2)}) %collective-permute-start.26) | collective-permute-done | bytes 655392 | tf_op jit(solution)/shard_map/ppermute | solution.py:28
  121.4 1.0 add_convert_fusion.2
  122.3 1.7 %collective-permute-done.27.refs_1_ = bf16[2,10,32,512]{3,2,1,0:T(8,128)(2,1)S(1)} collective-permute-done((bf16[2,10,32,512]{3,2,1,0:T(8,128)(2,1)S(1)}, bf16[2,10,32,512]{3,2,1,0:T(8,128)(2,1)S(1)}, u32[]{:S(2)}, u32[]{:S(2)}) %collective-permute-start.27) | collective-permute-done | bytes 655392 | tf_op jit(solution)/shard_map/ppermute | solution.py:37
  124.0 1.3 %shard_map.109 = f32[256,1280]{1,0:T(8,128)} custom-call(f32[2,10,32,512]{3,2,1,0:T(8,128)S(1)} %get-tuple-element.75.refs_0_, bf16[2,10,32,512]{3,2,1,0:T(8,128)(2,1)S(1)} %collective-permute-done.27.refs_1_, bf16[2,10,32,512]{3,2,1,0:T(8,128)(2,1)S(1)} %collective-permute-done.28.refs_2_), custom_call_target="tpu_custom_call" | custom-call | tf_op jit(solution)/shard_map/pallas_call | solution.py:233
  (59 shorter events, 1.9 us)
Async XLA Ops:
  3.1 17.4 %collective-permute-start = (bf16[128,2688]{1,0:T(8,128)(2,1)}, bf16[128,2688]{1,0:T(8,128)(2,1)S(1)}, u32[]{:S(2)}, u32[]{:S(2)}) collective-permute-start(bf16[128,2688]{1,0:T(8,128)(2,1)} %get-tuple-element.41.refs_0_.refs_1_), channel_id=1, source_target_pairs={{0,4},{2,6},{4,0},{6,2},{8,12},{10,14},{12,8},{14,10},{16,20},{18,... | collective-permute-start | bytes 2064392 | tf_op jit(solution)/shard_map/ppermute | solution.py:23
  3.6 17.1 %collective-permute-start.1 = (bf16[128,2688]{1,0:T(8,128)(2,1)}, bf16[128,2688]{1,0:T(8,128)(2,1)S(1)}, u32[]{:S(2)}, u32[]{:S(2)}) collective-permute-start(bf16[128,2688]{1,0:T(8,128)(2,1)} %get-tuple-element.41.refs_0_.refs_1_), channel_id=1, source_target_pairs={{0,1},{1,0},{2,3},{3,2},{4,5},{5,4},{6,7},{7,6},{8,9},{9,8},{10,11... | collective-permute-start | bytes 2064392 | tf_op jit(solution)/shard_map/ppermute | solution.py:28
  5.1 15.6 %collective-permute-start.2 = (bf16[128,2688]{1,0:T(8,128)(2,1)}, bf16[128,2688]{1,0:T(8,128)(2,1)S(1)}, u32[]{:S(2)}, u32[]{:S(2)}) collective-permute-start(bf16[128,2688]{1,0:T(8,128)(2,1)} %get-tuple-element.41.refs_0_.refs_1_), channel_id=1, source_target_pairs={{0,2},{2,0},{4,6},{6,4},{8,10},{10,8},{12,14},{14,12},{16,18},{18,... | collective-permute-start | bytes 2064392 | tf_op jit(solution)/shard_map/ppermute | solution.py:23
  5.1 19.2 %collective-permute-start.4 = (bf16[2,10,32,512]{3,2,1,0:T(8,128)(2,1)}, bf16[2,10,32,512]{3,2,1,0:T(8,128)(2,1)S(1)}, u32[]{:S(2)}, u32[]{:S(2)}) collective-permute-start(bf16[2,10,32,512]{3,2,1,0:T(8,128)(2,1)} %get-tuple-element.56), channel_id=1, source_target_pairs={{8,16},{16,8},{10,18},{18,10},{12,20},{20,12},{14,22},{22,14},{9,1... | collective-permute-start | bytes 1966088 | tf_op jit(solution)/shard_map/ppermute | solution.py:37
  8.6 17.1 %collective-permute-start.6 = (bf16[2,10,32,512]{3,2,1,0:T(8,128)(2,1)}, bf16[2,10,32,512]{3,2,1,0:T(8,128)(2,1)S(1)}, u32[]{:S(2)}, u32[]{:S(2)}) collective-permute-start(bf16[2,10,32,512]{3,2,1,0:T(8,128)(2,1)} %get-tuple-element.56), channel_id=1, source_target_pairs={{0,8},{2,10},{4,12},{6,14},{8,0},{10,2},{12,4},{14,6},{16,24},{18,... | collective-permute-start | bytes 1966088 | tf_op jit(solution)/shard_map/ppermute | solution.py:23
  20.5 9.0 %copy-start.4 = (bf16[128,2688]{1,0:T(8,128)(2,1)}, bf16[128,2688]{1,0:T(8,128)(2,1)S(1)}, u32[]{:S(2)}) copy-start(bf16[128,2688]{1,0:T(8,128)(2,1)S(1)} %collective-permute-done.refs_1_) | copy-start | bytes 2064388
  20.7 0.9 copy-start.6
  21.6 16.1 %collective-permute-start.8 = (bf16[128,2688]{1,0:T(8,128)(2,1)S(1)}, bf16[128,2688]{1,0:T(8,128)(2,1)S(1)}, u32[]{:S(2)}, u32[]{:S(2)}) collective-permute-start(bf16[128,2688]{1,0:T(8,128)(2,1)S(1)} %collective-permute-done.refs_1_), channel_id=1, source_target_pairs={{0,1},{1,0},{2,3},{3,2},{4,5},{5,4},{6,7},{7,6},{8,9},{9,8},{10,11... | collective-permute-start | bytes 2064392 | tf_op jit(solution)/shard_map/ppermute | solution.py:28
  24.4 5.1 %copy-start.12 = (bf16[2,10,32,512]{3,2,1,0:T(8,128)(2,1)}, bf16[2,10,32,512]{3,2,1,0:T(8,128)(2,1)S(1)}, u32[]{:S(2)}) copy-start(bf16[2,10,32,512]{3,2,1,0:T(8,128)(2,1)S(1)} %collective-permute-done.4) | copy-start | bytes 1966084
  24.4 16.4 %collective-permute-start.5 = (bf16[2,10,32,512]{3,2,1,0:T(8,128)(2,1)S(1)}, bf16[2,10,32,512]{3,2,1,0:T(8,128)(2,1)S(1)}, u32[]{:S(2)}, u32[]{:S(2)}) collective-permute-start(bf16[2,10,32,512]{3,2,1,0:T(8,128)(2,1)S(1)} %collective-permute-done.4), channel_id=1, source_target_pairs={{0,8},{2,10},{4,12},{6,14},{8,0},{10,2},{12,4},{14,6},{16,24},{18,... | collective-permute-start | bytes 1966088 | tf_op jit(solution)/shard_map/ppermute | solution.py:23
  25.8 17.9 %collective-permute-start.7 = (bf16[2,10,32,512]{3,2,1,0:T(8,128)(2,1)S(1)}, bf16[2,10,32,512]{3,2,1,0:T(8,128)(2,1)S(1)}, u32[]{:S(2)}, u32[]{:S(2)}) collective-permute-start(bf16[2,10,32,512]{3,2,1,0:T(8,128)(2,1)S(1)} %collective-permute-done.6), channel_id=1, source_target_pairs={{8,16},{16,8},{10,18},{18,10},{12,20},{20,12},{14,22},{22,14},{9,1... | collective-permute-start | bytes 1966088 | tf_op jit(solution)/shard_map/ppermute | solution.py:37
  28.2 15.5 %collective-permute-start.3 = (bf16[128,2688]{1,0:T(8,128)(2,1)S(1)}, bf16[128,2688]{1,0:T(8,128)(2,1)S(1)}, u32[]{:S(2)}, u32[]{:S(2)}) collective-permute-start(bf16[128,2688]{1,0:T(8,128)(2,1)S(1)} %collective-permute-done.refs_1_), channel_id=1, source_target_pairs={{0,2},{2,0},{4,6},{6,4},{8,10},{10,8},{12,14},{14,12},{16,18},{18,... | collective-permute-start | bytes 2064392 | tf_op jit(solution)/shard_map/ppermute | solution.py:23
  29.5 16.5 %copy-start.1 = (bf16[128,2560]{1,0:T(8,128)(2,1)S(1)}, bf16[128,2560]{1,0:T(8,128)(2,1)}, u32[]{:S(2)}) copy-start(bf16[128,2560]{1,0:T(8,128)(2,1)} %refs_2_.1) | copy-start | bytes 1966084
  29.5 17.9 %copy-start = (bf16[128,2688]{1,0:T(8,128)(2,1)S(1)}, bf16[128,2688]{1,0:T(8,128)(2,1)}, u32[]{:S(2)}) copy-start(bf16[128,2688]{1,0:T(8,128)(2,1)} %get-tuple-element.41.refs_0_.refs_1_) | copy-start | bytes 2064388
  29.5 31.3 %collective-permute-start.13 = (bf16[2,2,10,32,512]{4,3,2,1,0:T(8,128)(2,1)S(1)}, bf16[2,2,10,32,512]{4,3,2,1,0:T(8,128)(2,1)}, u32[]{:S(2)}, u32[]{:S(2)}) collective-permute-start(bf16[2,2,10,32,512]{4,3,2,1,0:T(8,128)(2,1)S(1)} %pad_maximum_fusion.refs_5_), channel_id=1, source_target_pairs={{0,4},{2,6},{4,0},{6,2},{8,12},{10,14},{12,8},{14,10},{16,20},{18,... | collective-permute-start | bytes 3932168 | tf_op jit(solution)/shard_map/ppermute | solution.py:23
  37.7 1.9 %copy-start.2 = (bf16[128,2688]{1,0:T(8,128)(2,1)}, bf16[128,2688]{1,0:T(8,128)(2,1)S(1)}, u32[]{:S(2)}) copy-start(bf16[128,2688]{1,0:T(8,128)(2,1)S(1)} %collective-permute-done.8.refs_5_) | copy-start | bytes 2064388
  38.6 6.9 %collective-permute-start.11 = (bf16[64,2688]{1,0:T(8,128)(2,1)}, bf16[64,2688]{1,0:T(8,128)(2,1)}, u32[]{:S(2)}, u32[]{:S(2)}) collective-permute-start(bf16[64,2688]{1,0:T(8,128)(2,1)} %get-tuple-element.81), channel_id=1, source_target_pairs={{0,2},{2,0},{4,6},{6,4},{8,10},{10,8},{12,14},{14,12},{16,18},{18,... | collective-permute-start | bytes 1032200 | tf_op jit(solution)/shard_map/ppermute | solution.py:23
  40.7 4.7 %copy-start.14 = (bf16[2,10,32,512]{3,2,1,0:T(8,128)(2,1)}, bf16[2,10,32,512]{3,2,1,0:T(8,128)(2,1)S(1)}, u32[]{:S(2)}) copy-start(bf16[2,10,32,512]{3,2,1,0:T(8,128)(2,1)S(1)} %collective-permute-done.5) | copy-start | bytes 1966084
  40.7 5.3 %collective-permute-start.12 = (bf16[64,2688]{1,0:T(8,128)(2,1)}, bf16[64,2688]{1,0:T(8,128)(2,1)}, u32[]{:S(2)}, u32[]{:S(2)}) collective-permute-start(bf16[64,2688]{1,0:T(8,128)(2,1)} %get-tuple-element.80), channel_id=1, source_target_pairs={{0,2},{2,0},{4,6},{6,4},{8,10},{10,8},{12,14},{14,12},{16,18},{18,... | collective-permute-start | bytes 1032200 | tf_op jit(solution)/shard_map/ppermute | solution.py:23
  43.7 0.9 copy-start.10
  43.7 2.8 %collective-permute-start.10 = (bf16[64,2688]{1,0:T(8,128)(2,1)}, bf16[64,2688]{1,0:T(8,128)(2,1)}, u32[]{:S(2)}, u32[]{:S(2)}) collective-permute-start(bf16[64,2688]{1,0:T(8,128)(2,1)} %get-tuple-element.82), channel_id=1, source_target_pairs={{0,2},{2,0},{4,6},{6,4},{8,10},{10,8},{12,14},{14,12},{16,18},{18,... | collective-permute-start | bytes 1032200 | tf_op jit(solution)/shard_map/ppermute | solution.py:23
  44.6 0.9 copy-start.8
  45.4 2.0 %collective-permute-start.9 = (bf16[64,2688]{1,0:T(8,128)(2,1)}, bf16[64,2688]{1,0:T(8,128)(2,1)}, u32[]{:S(2)}, u32[]{:S(2)}) collective-permute-start(bf16[64,2688]{1,0:T(8,128)(2,1)} %get-tuple-element.83), channel_id=1, source_target_pairs={{0,2},{2,0},{4,6},{6,4},{8,10},{10,8},{12,14},{14,12},{16,18},{18,... | collective-permute-start | bytes 1032200 | tf_op jit(solution)/shard_map/ppermute | solution.py:23
  45.5 32.4 %collective-permute-start.19 = (bf16[2,2,10,32,512]{4,3,2,1,0:T(8,128)(2,1)S(1)}, bf16[2,2,10,32,512]{4,3,2,1,0:T(8,128)(2,1)S(1)}, u32[]{:S(2)}, u32[]{:S(2)}) collective-permute-start(bf16[2,2,10,32,512]{4,3,2,1,0:T(8,128)(2,1)S(1)} %pad_maximum_fusion.refs_5_), channel_id=1, source_target_pairs={{0,2},{2,0},{4,6},{6,4},{8,10},{10,8},{12,14},{14,12},{16,18},{18,... | collective-permute-start | bytes 3932168 | tf_op jit(solution)/shard_map/ppermute | solution.py:23
  46.0 29.2 %collective-permute-start.18 = (bf16[128,2560]{1,0:T(8,128)(2,1)S(1)}, bf16[128,2560]{1,0:T(8,128)(2,1)S(1)}, u32[]{:S(2)}, u32[]{:S(2)}) collective-permute-start(bf16[128,2560]{1,0:T(8,128)(2,1)S(1)} %copy-done.1), channel_id=1, source_target_pairs={{0,1},{1,0},{2,3},{3,2},{4,5},{5,4},{6,7},{7,6},{8,9},{9,8},{10,11... | collective-permute-start | bytes 1966088 | tf_op jit(solution)/shard_map/ppermute | solution.py:28
  47.4 1.1 copy-start.3
  48.5 1.1 copy-start.5
  49.6 1.1 copy-start.7
  50.7 1.1 copy-start.9
  51.8 6.4 %copy-start.11 = (bf16[2,10,32,512]{3,2,1,0:T(8,128)(2,1)S(1)}, bf16[2,10,32,512]{3,2,1,0:T(8,128)(2,1)}, u32[]{:S(2)}) copy-start(bf16[2,10,32,512]{3,2,1,0:T(8,128)(2,1)} %copy-done.10) | copy-start | bytes 1966084
  58.1 1.1 copy-start.13
  58.2 1.3 %copy-start.15 = (bf16[2,10,32,512]{3,2,1,0:T(8,128)(2,1)S(1)}, bf16[2,10,32,512]{3,2,1,0:T(8,128)(2,1)}, u32[]{:S(2)}) copy-start(bf16[2,10,32,512]{3,2,1,0:T(8,128)(2,1)} %copy-done.14) | copy-start | bytes 1966084
  58.3 16.8 %collective-permute-start.15 = (bf16[2,10,32,512]{3,2,1,0:T(8,128)(2,1)S(1)}, bf16[2,10,32,512]{3,2,1,0:T(8,128)(2,1)S(1)}, u32[]{:S(2)}, u32[]{:S(2)}) collective-permute-start(bf16[2,10,32,512]{3,2,1,0:T(8,128)(2,1)S(1)} %broadcast_select_fusion), channel_id=1, source_target_pairs={{0,8},{2,10},{4,12},{6,14},{8,0},{10,2},{12,4},{14,6},{16,24},{18,... | collective-permute-start | bytes 1966088 | tf_op jit(solution)/shard_map/ppermute | solution.py:23
  60.8 16.4 %collective-permute-start.17 = (bf16[2,10,32,512]{3,2,1,0:T(8,128)(2,1)S(1)}, bf16[2,10,32,512]{3,2,1,0:T(8,128)(2,1)S(1)}, u32[]{:S(2)}, u32[]{:S(2)}) collective-permute-start(bf16[2,10,32,512]{3,2,1,0:T(8,128)(2,1)S(1)} %select_select_fusion.1.refs_7_), channel_id=1, source_target_pairs={{0,4},{2,6},{4,0},{6,2},{8,12},{10,14},{12,8},{14,10},{16,20},{18,... | collective-permute-start | bytes 1966088 | tf_op jit(solution)/shard_map/ppermute | solution.py:23
  62.3 15.7 %collective-permute-start.21 = (bf16[2,10,32,512]{3,2,1,0:T(8,128)(2,1)S(1)}, bf16[2,10,32,512]{3,2,1,0:T(8,128)(2,1)S(1)}, u32[]{:S(2)}, u32[]{:S(2)}) collective-permute-start(bf16[2,10,32,512]{3,2,1,0:T(8,128)(2,1)S(1)} %select_select_fusion.1.refs_7_), channel_id=1, source_target_pairs={{0,2},{2,0},{4,6},{6,4},{8,10},{10,8},{12,14},{14,12},{16,18},{18,... | collective-permute-start | bytes 1966088 | tf_op jit(solution)/shard_map/ppermute | solution.py:23
  75.1 8.0 %collective-permute-start.20 = (bf16[2,2,10,32,512]{4,3,2,1,0:T(8,128)(2,1)}, bf16[2,2,10,32,512]{4,3,2,1,0:T(8,128)(2,1)S(1)}, u32[]{:S(2)}, u32[]{:S(2)}) collective-permute-start(bf16[2,2,10,32,512]{4,3,2,1,0:T(8,128)(2,1)} %collective-permute-done.13.refs_6_), channel_id=1, source_target_pairs={{0,2},{2,0},{4,6},{6,4},{8,10},{10,8},{12,14},{14,12},{16,18},{18,... | collective-permute-start | bytes 3932168 | tf_op jit(solution)/shard_map/ppermute | solution.py:23
  77.2 4.3 %collective-permute-start.22 = (bf16[2,10,32,512]{3,2,1,0:T(8,128)(2,1)S(1)}, bf16[2,10,32,512]{3,2,1,0:T(8,128)(2,1)S(1)}, u32[]{:S(2)}, u32[]{:S(2)}) collective-permute-start(bf16[2,10,32,512]{3,2,1,0:T(8,128)(2,1)S(1)} %collective-permute-done.17.refs_8_), channel_id=1, source_target_pairs={{0,2},{2,0},{4,6},{6,4},{8,10},{10,8},{12,14},{14,12},{16,18},{18,... | collective-permute-start | bytes 1966088 | tf_op jit(solution)/shard_map/ppermute | solution.py:23
  77.2 5.8 %collective-permute-start.23 = (bf16[2,10,32,512]{3,2,1,0:T(8,128)(2,1)S(1)}, bf16[2,10,32,512]{3,2,1,0:T(8,128)(2,1)S(1)}, u32[]{:S(2)}, u32[]{:S(2)}) collective-permute-start(bf16[2,10,32,512]{3,2,1,0:T(8,128)(2,1)S(1)} %select_select_fusion.refs_11_), channel_id=1, source_target_pairs={{0,2},{2,0},{4,6},{6,4},{8,10},{10,8},{12,14},{14,12},{16,18},{18,... | collective-permute-start | bytes 1966088 | tf_op jit(solution)/shard_map/ppermute | solution.py:23
  77.9 16.7 %collective-permute-start.14 = (bf16[2,10,32,512]{3,2,1,0:T(8,128)(2,1)S(1)}, bf16[2,10,32,512]{3,2,1,0:T(8,128)(2,1)S(1)}, u32[]{:S(2)}, u32[]{:S(2)}) collective-permute-start(bf16[2,10,32,512]{3,2,1,0:T(8,128)(2,1)S(1)} %get-tuple-element.57), channel_id=1, source_target_pairs={{0,8},{2,10},{4,12},{6,14},{8,0},{10,2},{12,4},{14,6},{16,24},{18,... | collective-permute-start | bytes 1966088 | tf_op jit(solution)/shard_map/ppermute | solution.py:23
  78.0 18.5 %collective-permute-start.16 = (bf16[2,10,32,512]{3,2,1,0:T(8,128)(2,1)S(1)}, bf16[2,10,32,512]{3,2,1,0:T(8,128)(2,1)S(1)}, u32[]{:S(2)}, u32[]{:S(2)}) collective-permute-start(bf16[2,10,32,512]{3,2,1,0:T(8,128)(2,1)S(1)} %add_convert_fusion.3), channel_id=1, source_target_pairs={{8,16},{16,8},{10,18},{18,10},{12,20},{20,12},{14,22},{22,14},{9,1... | collective-permute-start | bytes 1966088 | tf_op jit(solution)/shard_map/ppermute | solution.py:37
  81.5 16.4 %collective-permute-start.24 = (bf16[2,10,32,512]{3,2,1,0:T(8,128)(2,1)S(1)}, bf16[2,10,32,512]{3,2,1,0:T(8,128)(2,1)S(1)}, u32[]{:S(2)}, u32[]{:S(2)}) collective-permute-start(bf16[2,10,32,512]{3,2,1,0:T(8,128)(2,1)S(1)} %select_select_fusion.refs_11_), channel_id=1, source_target_pairs={{0,4},{2,6},{4,0},{6,2},{8,12},{10,14},{12,8},{14,10},{16,20},{18,... | collective-permute-start | bytes 1966088 | tf_op jit(solution)/shard_map/ppermute | solution.py:23
  97.9 2.1 %collective-permute-start.25 = (bf16[2,10,32,512]{3,2,1,0:T(8,128)(2,1)S(1)}, bf16[2,10,32,512]{3,2,1,0:T(8,128)(2,1)S(1)}, u32[]{:S(2)}, u32[]{:S(2)}) collective-permute-start(bf16[2,10,32,512]{3,2,1,0:T(8,128)(2,1)S(1)} %collective-permute-done.24.refs_4_), channel_id=1, source_target_pairs={{0,2},{2,0},{4,6},{6,4},{8,10},{10,8},{12,14},{14,12},{16,18},{18,... | collective-permute-start | bytes 1966088 | tf_op jit(solution)/shard_map/ppermute | solution.py:23
  104.5 16.8 %collective-permute-start.26 = (bf16[128,2560]{1,0:T(8,128)(2,1)S(1)}, bf16[128,2560]{1,0:T(8,128)(2,1)S(1)}, u32[]{:S(2)}, u32[]{:S(2)}) collective-permute-start(bf16[128,2560]{1,0:T(8,128)(2,1)S(1)} %shard_map.108), channel_id=1, source_target_pairs={{0,1},{1,0},{2,3},{3,2},{4,5},{5,4},{6,7},{7,6},{8,9},{9,8},{10,11... | collective-permute-start | bytes 1966088 | tf_op jit(solution)/shard_map/ppermute | solution.py:28
  105.3 17.0 %collective-permute-start.28 = (bf16[2,10,32,512]{3,2,1,0:T(8,128)(2,1)S(1)}, bf16[2,10,32,512]{3,2,1,0:T(8,128)(2,1)S(1)}, u32[]{:S(2)}, u32[]{:S(2)}) collective-permute-start(bf16[2,10,32,512]{3,2,1,0:T(8,128)(2,1)S(1)} %add_convert_fusion), channel_id=1, source_target_pairs={{0,8},{2,10},{4,12},{6,14},{8,0},{10,2},{12,4},{14,6},{16,24},{18,... | collective-permute-start | bytes 1966088 | tf_op jit(solution)/shard_map/ppermute | solution.py:23
  105.6 18.4 %collective-permute-start.27 = (bf16[2,10,32,512]{3,2,1,0:T(8,128)(2,1)S(1)}, bf16[2,10,32,512]{3,2,1,0:T(8,128)(2,1)S(1)}, u32[]{:S(2)}, u32[]{:S(2)}) collective-permute-start(bf16[2,10,32,512]{3,2,1,0:T(8,128)(2,1)S(1)} %add_convert_fusion.1), channel_id=1, source_target_pairs={{8,16},{16,8},{10,18},{18,10},{12,20},{20,12},{14,22},{22,14},{9,1... | collective-permute-start | bytes 1966088 | tf_op jit(solution)/shard_map/ppermute | solution.py:37

commit v5 on v4

--- a/solution.py
+++ b/solution.py
@@ -135,24 +135,29 @@
 
 def table_kernel(lookups, part, planes, offsets, place_ref, *refs):
     count = len(offsets)
-    blocks = unstacked(refs[: -count - 2])
-    outs, tokens, sem = refs[-count - 2 : -2], refs[-2], refs[-1]
-    width = tokens.shape[1] - LANES
+    blocks = unstacked(refs[: -count - 3])
+    outs, tokens, routing, sem = refs[-count - 3 : -3], refs[-3], refs[-2], refs[-1]
+    width = tokens.shape[1]
     half = width // ORDERS
     heads = lookups // ORDERS
-    copies, at = [], 0
+    firsts, copies, at = [], [], 0
     for b, block in enumerate(blocks):
+        span = pl.ds(at, block.shape[0])
+        firsts.append(
+            pltpu.make_async_copy(
+                block.at[:, pl.ds(width, LANES)], routing.at[span], sem.at[0, b]
+            )
+        )
         copies.append(
-            pltpu.make_async_copy(block, tokens.at[pl.ds(at, block.shape[0])], sem.at[b])
+            pltpu.make_async_copy(block.at[:, pl.ds(0, width)], tokens.at[span], sem.at[1, b])
         )
         at += block.shape[0]
-    for copy in copies:
+    for copy in firsts + copies:
         copy.start()
-    for copy in copies:
+    for copy in firsts:
         copy.wait()
     metas = [
-        tokens[pl.ds(first, LANES), pl.ds(width, LANES)].astype(jnp.float32).T
-        for first in range(0, at, LANES)
+        routing[pl.ds(first, LANES), :].astype(jnp.float32).T for first in range(0, at, LANES)
     ]
     meta = jnp.concatenate([m[: 3 * lookups] for m in metas], axis=1)
     key = meta[:lookups] * SHARD + meta[lookups : 2 * lookups]
@@ -161,8 +166,8 @@
     plane = me // 4
     row = lax.broadcasted_iota(jnp.int32, (part, at), 0)
     size = heads * part
+    hits = []
     for o in range(ORDERS):
-        hits = []
         for offset in offsets:
             to = lax.rem(jnp.where(plane % 2 == 0, plane + offset, plane + planes - offset), planes)
             to = to * 4 + me % 4
@@ -170,8 +175,12 @@
             for j in range(o * heads, (o + 1) * heads):
                 hit = jnp.where(rows == key[j : j + 1], gate[j : j + 1], 0.0)
                 hits.append(hit.astype(jnp.bfloat16))
+    for copy in copies:
+        copy.wait()
+    for o in range(ORDERS):
+        mine = hits[o * heads * count : (o + 1) * heads * count]
         sums = jnp.dot(
-            jnp.concatenate(hits, axis=0),
+            jnp.concatenate(mine, axis=0),
             tokens[:, pl.ds(o * half, half)],
             preferred_element_type=jnp.float32,
         )
@@ -199,8 +208,9 @@
         in_specs=[pl.BlockSpec(memory_space=pltpu.SMEM)]
         + [pl.BlockSpec(memory_space=pl.ANY)] * len(blocks),
         scratch_shapes=[
-            pltpu.VMEM((count, total), jnp.bfloat16),
-            pltpu.SemaphoreType.DMA((len(blocks),)),
+            pltpu.VMEM((count, total - LANES), jnp.bfloat16),
+            pltpu.VMEM((count, LANES), jnp.bfloat16),
+            pltpu.SemaphoreType.DMA((2, len(blocks))),
         ],
         compiler_params=pltpu.CompilerParams(
             vmem_limit_bytes=room(

time: 127 us -> 127 us (level)
  waiting for transfers between devices: 63.2 us -> 64.5 us
  transfers between devices with their start and end apart: 29 -> 29, of which waited for: 17 -> 17; matrix products, arithmetic and copies ran while one was open for 4% -> 4% of each run, Pallas kernels for 14% -> 13%
where the time goes in v5:
time: 127 us; the launch traced here: 125 us
  waiting for transfers between devices  64.5 us (51%)
  Pallas kernels  24.1 us (19%)
  starting transfers between devices  22.8 us (18%)
  local copies, waits for them, and re-layouts  10 us (8%)
  other arithmetic  3.14 us (2%)
    ppermute x21, waiting for transfers between devices, swap(): return lax.ppermute(value, 'dp', [(i, i ^ bit) for i in range(size)])  41.2 us
    ppermute x4, waiting for transfers between devices, over_expert(): lax.ppermute(value, 'expert', [(i, (i + step) % size) for i in range(size)])  15.4 us
    ppermute x4, starting transfers between devices, over_even(): return lax.ppermute(value, 'dp', pairs)  12.2 us
    pallas_call x2, Pallas kernels, expert_results(): pl.pallas_call(functools.partial(result_kernel, last, begin, groups, dp /...  9 us
    unnamed x32, local copies, waits for them, and re-layouts  8.1 us
    ppermute x4, waiting for transfers between devices, over_even(): return lax.ppermute(value, 'dp', pairs)  7.82 us
    ppermute x21, starting transfers between devices, swap(): return lax.ppermute(value, 'dp', [(i, i ^ bit) for i in range(size)])  6.53 us
    pallas_call x1, Pallas kernels, hidden_layers(): pl.pallas_call(functools.partial(hidden_kernel, where, last, groups, dp /...  6.22 us
  transfers between devices with their start and end apart: 29, of which 17 were waited for; matrix products, arithmetic and copies ran while one was open for 4% of the time, Pallas kernels for 13%

profile of v5, /device:TPU:10, one launch (start us, length us, event | category | flops | bytes accessed | tf_op | source)
XLA Modules:
  0.0 125.5 jit_solution(16511686857112280889)
XLA Ops:
  0.6 2.4 %shard_map.104 = (bf16[2,10,32,512]{3,2,1,0:T(8,128)(2,1)}, bf16[128,2688]{1,0:T(8,128)(2,1)}) custom-call(bf16[2,160,512]{2,1,0:T(8,128)(2,1)} %up_ref.1, bf16[2,32,2560]{2,1,0:T(8,128)(2,1)} %down_ref.1, bf16[128,2560]{1,0:T(8,128)(2,1)} %grad_ref.1, s32[2,128]{1,0:T(2,128)} %bitcast.16, f32[2,128]{1,0:T(2,128)} %bitcast.17, f32[4,128]{1,0:T(4,128)} %bitcast.13, ...), custom_call_target="tpu_custom_call" | custom-call | tf_op jit(solution)/shard_map/pallas_call | solution.py:95
  3.1 0.5 collective-permute-start
  3.6 1.5 %collective-permute-start.1 = (bf16[128,2688]{1,0:T(8,128)(2,1)}, bf16[128,2688]{1,0:T(8,128)(2,1)S(1)}, u32[]{:S(2)}, u32[]{:S(2)}) collective-permute-start(bf16[128,2688]{1,0:T(8,128)(2,1)} %get-tuple-element.41.refs_0_.refs_1_), channel_id=1, source_target_pairs={{0,1},{1,0},{2,3},{3,2},{4,5},{5,4},{6,7},{7,6},{8,9},{9,8},{10,11... | collective-permute-start | bytes 2064392 | tf_op jit(solution)/shard_map/ppermute | solution.py:28
  5.1 3.5 %collective-permute-start.4 = (bf16[2,10,32,512]{3,2,1,0:T(8,128)(2,1)}, bf16[2,10,32,512]{3,2,1,0:T(8,128)(2,1)S(1)}, u32[]{:S(2)}, u32[]{:S(2)}) collective-permute-start(bf16[2,10,32,512]{3,2,1,0:T(8,128)(2,1)} %get-tuple-element.56), channel_id=1, source_target_pairs={{8,16},{16,8},{10,18},{18,10},{12,20},{20,12},{14,22},{22,14},{9,1... | collective-permute-start | bytes 1966088 | tf_op jit(solution)/shard_map/ppermute | solution.py:37
  8.7 11.8 %collective-permute-done.refs_1_ = bf16[128,2688]{1,0:T(8,128)(2,1)S(1)} collective-permute-done((bf16[128,2688]{1,0:T(8,128)(2,1)}, bf16[128,2688]{1,0:T(8,128)(2,1)S(1)}, u32[]{:S(2)}, u32[]{:S(2)}) %collective-permute-start) | collective-permute-done | bytes 688160 | tf_op jit(solution)/shard_map/ppermute | solution.py:23
  20.7 0.9 copy-done.6
  21.6 1.5 %collective-permute-start.8 = (bf16[128,2688]{1,0:T(8,128)(2,1)S(1)}, bf16[128,2688]{1,0:T(8,128)(2,1)S(1)}, u32[]{:S(2)}, u32[]{:S(2)}) collective-permute-start(bf16[128,2688]{1,0:T(8,128)(2,1)S(1)} %collective-permute-done.refs_1_), channel_id=1, source_target_pairs={{0,1},{1,0},{2,3},{3,2},{4,5},{5,4},{6,7},{7,6},{8,9},{9,8},{10,11... | collective-permute-start | bytes 2064392 | tf_op jit(solution)/shard_map/ppermute | solution.py:28
  23.1 1.3 %collective-permute-done.4 = bf16[2,10,32,512]{3,2,1,0:T(8,128)(2,1)S(1)} collective-permute-done((bf16[2,10,32,512]{3,2,1,0:T(8,128)(2,1)}, bf16[2,10,32,512]{3,2,1,0:T(8,128)(2,1)S(1)}, u32[]{:S(2)}, u32[]{:S(2)}) %collective-permute-start.4) | collective-permute-done | bytes 655392 | tf_op jit(solution)/shard_map/ppermute | solution.py:37
  24.4 1.4 %collective-permute-done.6 = bf16[2,10,32,512]{3,2,1,0:T(8,128)(2,1)S(1)} collective-permute-done((bf16[2,10,32,512]{3,2,1,0:T(8,128)(2,1)}, bf16[2,10,32,512]{3,2,1,0:T(8,128)(2,1)S(1)}, u32[]{:S(2)}, u32[]{:S(2)}) %collective-permute-start.6) | collective-permute-done | bytes 655392 | tf_op jit(solution)/shard_map/ppermute | solution.py:23
  25.8 2.4 %collective-permute-start.7 = (bf16[2,10,32,512]{3,2,1,0:T(8,128)(2,1)S(1)}, bf16[2,10,32,512]{3,2,1,0:T(8,128)(2,1)S(1)}, u32[]{:S(2)}, u32[]{:S(2)}) collective-permute-start(bf16[2,10,32,512]{3,2,1,0:T(8,128)(2,1)S(1)} %collective-permute-done.6), channel_id=1, source_target_pairs={{8,16},{16,8},{10,18},{18,10},{12,20},{20,12},{14,22},{22,14},{9,1... | collective-permute-start | bytes 1966088 | tf_op jit(solution)/shard_map/ppermute | solution.py:37
  28.2 1.2 pad_maximum_fusion.refs_5_
  29.5 1.6 %collective-permute-start.13 = (bf16[2,2,10,32,512]{4,3,2,1,0:T(8,128)(2,1)S(1)}, bf16[2,2,10,32,512]{4,3,2,1,0:T(8,128)(2,1)}, u32[]{:S(2)}, u32[]{:S(2)}) collective-permute-start(bf16[2,2,10,32,512]{4,3,2,1,0:T(8,128)(2,1)S(1)} %pad_maximum_fusion.refs_5_), channel_id=1, source_target_pairs={{0,4},{2,6},{4,0},{6,2},{8,12},{10,14},{12,8},{14,10},{16,20},{18,... | collective-permute-start | bytes 3932168 | tf_op jit(solution)/shard_map/ppermute | solution.py:23
  31.1 6.6 %collective-permute-done.8.refs_5_ = bf16[128,2688]{1,0:T(8,128)(2,1)S(1)} collective-permute-done((bf16[128,2688]{1,0:T(8,128)(2,1)S(1)}, bf16[128,2688]{1,0:T(8,128)(2,1)S(1)}, u32[]{:S(2)}, u32[]{:S(2)}) %collective-permute-start.8) | collective-permute-done | bytes 688160 | tf_op jit(solution)/shard_map/ppermute | solution.py:28
  37.7 0.9 fusion
  38.6 1.0 fusion.1
  39.6 1.1 collective-permute-done.5
  40.7 2.9 %collective-permute-done.7 = bf16[2,10,32,512]{3,2,1,0:T(8,128)(2,1)S(1)} collective-permute-done((bf16[2,10,32,512]{3,2,1,0:T(8,128)(2,1)S(1)}, bf16[2,10,32,512]{3,2,1,0:T(8,128)(2,1)S(1)}, u32[]{:S(2)}, u32[]{:S(2)}) %collective-permute-start.7) | collective-permute-done | bytes 655392 | tf_op jit(solution)/shard_map/ppermute | solution.py:37
  43.7 0.9 copy-done.10
  44.6 0.9 copy-done.8
  45.5 0.5 collective-permute-start.19
  46.0 0.5 collective-permute-start.18
  46.5 0.9 collective-permute-done.9.refs_6_
  47.4 1.1 copy-done.3
  48.5 1.1 copy-done.5
  49.6 1.1 copy-done.7
  50.7 1.1 copy-done.9
  51.8 5.2 %shard_map.105 = (f32[2,10,32,512]{3,2,1,0:T(8,128)S(1)}, bf16[2,10,32,512]{3,2,1,0:T(8,128)(2,1)S(1)}, bf16[2,10,32,512]{3,2,1,0:T(8,128)(2,1)S(1)}, bf16[2,10,32,512]{3,2,1,0:T(8,128)(2,1)S(1)}) custom-call(s32[2]{0:T(128)S(1)} %pad_add_fusion.place_ref.refs_0_, bf16[128,2688]{1,0:T(8,128)(2,1)S(1)} %copy-done, bf16[128,2688]{1,0:T(8,128)(2,1)S(1)} %copy-done.5, ...), custom_call_target="tpu_custom_call" | custom-call | flops 2684354560 | bytes 4096 | tf_op jit(solution)/shard_map/pallas_call | solution.py:202
  57.2 0.9 copy-done.13
  58.4 2.5 %collective-permute-done.13.refs_6_ = bf16[2,2,10,32,512]{4,3,2,1,0:T(8,128)(2,1)} collective-permute-done((bf16[2,2,10,32,512]{4,3,2,1,0:T(8,128)(2,1)S(1)}, bf16[2,2,10,32,512]{4,3,2,1,0:T(8,128)(2,1)}, u32[]{:S(2)}, u32[]{:S(2)}) %collective-permute-start.13) | collective-permute-done | bytes 1310752 | tf_op jit(solution)/shard_map/ppermute | solution.py:23
  60.8 1.5 %collective-permute-start.17 = (bf16[2,10,32,512]{3,2,1,0:T(8,128)(2,1)S(1)}, bf16[2,10,32,512]{3,2,1,0:T(8,128)(2,1)S(1)}, u32[]{:S(2)}, u32[]{:S(2)}) collective-permute-start(bf16[2,10,32,512]{3,2,1,0:T(8,128)(2,1)S(1)} %select_select_fusion.1.refs_7_), channel_id=1, source_target_pairs={{0,4},{2,6},{4,0},{6,2},{8,12},{10,14},{12,8},{14,10},{16,20},{18,... | collective-permute-start | bytes 1966088 | tf_op jit(solution)/shard_map/ppermute | solution.py:23
  62.3 11.6 %collective-permute-done.15 = bf16[2,10,32,512]{3,2,1,0:T(8,128)(2,1)S(1)} collective-permute-done((bf16[2,10,32,512]{3,2,1,0:T(8,128)(2,1)S(1)}, bf16[2,10,32,512]{3,2,1,0:T(8,128)(2,1)S(1)}, u32[]{:S(2)}, u32[]{:S(2)}) %collective-permute-start.15) | collective-permute-done | bytes 655392 | tf_op jit(solution)/shard_map/ppermute | solution.py:23
  74.1 3.1 %collective-permute-done.17.refs_8_ = bf16[2,10,32,512]{3,2,1,0:T(8,128)(2,1)S(1)} collective-permute-done((bf16[2,10,32,512]{3,2,1,0:T(8,128)(2,1)S(1)}, bf16[2,10,32,512]{3,2,1,0:T(8,128)(2,1)S(1)}, u32[]{:S(2)}, u32[]{:S(2)}) %collective-permute-start.17) | collective-permute-done | bytes 655392 | tf_op jit(solution)/shard_map/ppermute | solution.py:23
  77.2 0.5 collective-permute-start.23
  78.0 3.6 %collective-permute-start.16 = (bf16[2,10,32,512]{3,2,1,0:T(8,128)(2,1)S(1)}, bf16[2,10,32,512]{3,2,1,0:T(8,128)(2,1)S(1)}, u32[]{:S(2)}, u32[]{:S(2)}) collective-permute-start(bf16[2,10,32,512]{3,2,1,0:T(8,128)(2,1)S(1)} %add_convert_fusion.3), channel_id=1, source_target_pairs={{8,16},{16,8},{10,18},{18,10},{12,20},{20,12},{14,22},{22,14},{9,1... | collective-permute-start | bytes 1966088 | tf_op jit(solution)/shard_map/ppermute | solution.py:37
  81.7 1.6 %collective-permute-start.24 = (bf16[2,10,32,512]{3,2,1,0:T(8,128)(2,1)S(1)}, bf16[2,10,32,512]{3,2,1,0:T(8,128)(2,1)S(1)}, u32[]{:S(2)}, u32[]{:S(2)}) collective-permute-start(bf16[2,10,32,512]{3,2,1,0:T(8,128)(2,1)S(1)} %select_select_fusion.refs_11_), channel_id=1, source_target_pairs={{0,4},{2,6},{4,0},{6,2},{8,12},{10,14},{12,8},{14,10},{16,20},{18,... | collective-permute-start | bytes 1966088 | tf_op jit(solution)/shard_map/ppermute | solution.py:23
  83.2 6.2 %shard_map.106 = (bf16[2,512,2560]{2,1,0:T(8,128)(2,1)S(1)}, f32[256,1024]{1,0:T(8,128)S(1)}, f32[256,1024]{1,0:T(8,128)S(1)}) custom-call(s32[2]{0:T(128)S(1)} %pad_add_fusion.place_ref.refs_0_, bf16[128,2688]{1,0:T(8,128)(2,1)S(1)} %copy-done, bf16[128,2688]{1,0:T(8,128)(2,1)S(1)} %collective-permute-done.1.refs_4_.refs_2_.refs_1_, ...), custom_call_target="tpu_custom_call" | custom-call | flops 2684354560 | bytes 20971520 | tf_op jit(solution)/shard_map/pallas_call | solution.py:459
  89.5 5.2 %collective-permute-done.14 = bf16[2,10,32,512]{3,2,1,0:T(8,128)(2,1)S(1)} collective-permute-done((bf16[2,10,32,512]{3,2,1,0:T(8,128)(2,1)S(1)}, bf16[2,10,32,512]{3,2,1,0:T(8,128)(2,1)S(1)}, u32[]{:S(2)}, u32[]{:S(2)}) %collective-permute-start.14) | collective-permute-done | bytes 655392 | tf_op jit(solution)/shard_map/ppermute | solution.py:23
  94.7 1.9 %collective-permute-done.16 = bf16[2,10,32,512]{3,2,1,0:T(8,128)(2,1)S(1)} collective-permute-done((bf16[2,10,32,512]{3,2,1,0:T(8,128)(2,1)S(1)}, bf16[2,10,32,512]{3,2,1,0:T(8,128)(2,1)S(1)}, u32[]{:S(2)}, u32[]{:S(2)}) %collective-permute-start.16) | collective-permute-done | bytes 655392 | tf_op jit(solution)/shard_map/ppermute | solution.py:37
  96.6 1.5 %collective-permute-done.24.refs_4_ = bf16[2,10,32,512]{3,2,1,0:T(8,128)(2,1)S(1)} collective-permute-done((bf16[2,10,32,512]{3,2,1,0:T(8,128)(2,1)S(1)}, bf16[2,10,32,512]{3,2,1,0:T(8,128)(2,1)S(1)}, u32[]{:S(2)}, u32[]{:S(2)}) %collective-permute-start.24) | collective-permute-done | bytes 655392 | tf_op jit(solution)/shard_map/ppermute | solution.py:23
  98.1 2.1 %collective-permute-done.25.refs_5_ = bf16[2,10,32,512]{3,2,1,0:T(8,128)(2,1)S(1)} collective-permute-done((bf16[2,10,32,512]{3,2,1,0:T(8,128)(2,1)S(1)}, bf16[2,10,32,512]{3,2,1,0:T(8,128)(2,1)S(1)}, u32[]{:S(2)}, u32[]{:S(2)}) %collective-permute-start.25) | collective-permute-done | bytes 655392 | tf_op jit(solution)/shard_map/ppermute | solution.py:23
  100.2 4.5 %shard_map.108 = bf16[128,2560]{1,0:T(8,128)(2,1)S(1)} custom-call(s32[2]{0:T(128)S(1)} %pad_add_fusion.place_ref.refs_0_, bf16[128,2688]{1,0:T(8,128)(2,1)S(1)} %collective-permute-done.1.refs_4_.refs_2_.refs_1_, bf16[128,2560]{1,0:T(8,128)(2,1)S(1)} %collective-permute-done.18.refs_4_.refs_2_, bf16[2,512,2560]{2,1,0:T(8,128)(2,1)S(1)} %get-tuple-element.68.refs_3_, ...), custom_call_target="tpu_custom_call" | custom-call | flops 671088640 | bytes 9175040 | tf_op jit(solution)/shard_map/pallas_call | solution.py:501
  104.7 0.6 collective-permute-start.26
  105.8 2.7 %collective-permute-start.27 = (bf16[2,10,32,512]{3,2,1,0:T(8,128)(2,1)S(1)}, bf16[2,10,32,512]{3,2,1,0:T(8,128)(2,1)S(1)}, u32[]{:S(2)}, u32[]{:S(2)}) collective-permute-start(bf16[2,10,32,512]{3,2,1,0:T(8,128)(2,1)S(1)} %add_convert_fusion.1), channel_id=1, source_target_pairs={{8,16},{16,8},{10,18},{18,10},{12,20},{20,12},{14,22},{22,14},{9,1... | collective-permute-start | bytes 1966088 | tf_op jit(solution)/shard_map/ppermute | solution.py:37
  108.5 4.5 %shard_map.107 = f32[128,2560]{1,0:T(8,128)S(1)} custom-call(s32[2]{0:T(128)S(1)} %pad_add_fusion.place_ref.refs_0_, bf16[128,2688]{1,0:T(8,128)(2,1)S(1)} %copy-done, bf16[128,2560]{1,0:T(8,128)(2,1)S(1)} %copy-done.1, bf16[2,512,2560]{2,1,0:T(8,128)(2,1)S(1)} %get-tuple-element.68.refs_3_, bf16[2,10,32,512]{3,2,1,0:T(8,128)(2,1)S(1)} %collective-permute-done.24.refs_4_, ...), custom_call_target="tpu_custom_call" | custom-call | flops 671088640 | bytes 9175040 | tf_op jit(solution)/shard_map/pallas_call | solution.py:501
  113.0 8.5 %collective-permute-done.26 = bf16[128,2560]{1,0:T(8,128)(2,1)S(1)} collective-permute-done((bf16[128,2560]{1,0:T(8,128)(2,1)S(1)}, bf16[128,2560]{1,0:T(8,128)(2,1)S(1)}, u32[]{:S(2)}, u32[]{:S(2)}) %collective-permute-start.26) | collective-permute-done | bytes 655392 | tf_op jit(solution)/shard_map/ppermute | solution.py:28
  121.5 1.0 add_convert_fusion.2
  122.5 1.7 %collective-permute-done.27.refs_1_ = bf16[2,10,32,512]{3,2,1,0:T(8,128)(2,1)S(1)} collective-permute-done((bf16[2,10,32,512]{3,2,1,0:T(8,128)(2,1)S(1)}, bf16[2,10,32,512]{3,2,1,0:T(8,128)(2,1)S(1)}, u32[]{:S(2)}, u32[]{:S(2)}) %collective-permute-start.27) | collective-permute-done | bytes 655392 | tf_op jit(solution)/shard_map/ppermute | solution.py:37
  124.2 1.3 %shard_map.109 = f32[256,1280]{1,0:T(8,128)} custom-call(f32[2,10,32,512]{3,2,1,0:T(8,128)S(1)} %get-tuple-element.75.refs_0_, bf16[2,10,32,512]{3,2,1,0:T(8,128)(2,1)S(1)} %collective-permute-done.27.refs_1_, bf16[2,10,32,512]{3,2,1,0:T(8,128)(2,1)S(1)} %collective-permute-done.28.refs_2_), custom_call_target="tpu_custom_call" | custom-call | tf_op jit(solution)/shard_map/pallas_call | solution.py:243
  (59 shorter events, 1.9 us)
Async XLA Ops:
  3.1 17.4 %collective-permute-start = (bf16[128,2688]{1,0:T(8,128)(2,1)}, bf16[128,2688]{1,0:T(8,128)(2,1)S(1)}, u32[]{:S(2)}, u32[]{:S(2)}) collective-permute-start(bf16[128,2688]{1,0:T(8,128)(2,1)} %get-tuple-element.41.refs_0_.refs_1_), channel_id=1, source_target_pairs={{0,4},{2,6},{4,0},{6,2},{8,12},{10,14},{12,8},{14,10},{16,20},{18,... | collective-permute-start | bytes 2064392 | tf_op jit(solution)/shard_map/ppermute | solution.py:23
  3.6 17.1 %collective-permute-start.1 = (bf16[128,2688]{1,0:T(8,128)(2,1)}, bf16[128,2688]{1,0:T(8,128)(2,1)S(1)}, u32[]{:S(2)}, u32[]{:S(2)}) collective-permute-start(bf16[128,2688]{1,0:T(8,128)(2,1)} %get-tuple-element.41.refs_0_.refs_1_), channel_id=1, source_target_pairs={{0,1},{1,0},{2,3},{3,2},{4,5},{5,4},{6,7},{7,6},{8,9},{9,8},{10,11... | collective-permute-start | bytes 2064392 | tf_op jit(solution)/shard_map/ppermute | solution.py:28
  5.1 15.6 %collective-permute-start.2 = (bf16[128,2688]{1,0:T(8,128)(2,1)}, bf16[128,2688]{1,0:T(8,128)(2,1)S(1)}, u32[]{:S(2)}, u32[]{:S(2)}) collective-permute-start(bf16[128,2688]{1,0:T(8,128)(2,1)} %get-tuple-element.41.refs_0_.refs_1_), channel_id=1, source_target_pairs={{0,2},{2,0},{4,6},{6,4},{8,10},{10,8},{12,14},{14,12},{16,18},{18,... | collective-permute-start | bytes 2064392 | tf_op jit(solution)/shard_map/ppermute | solution.py:23
  5.1 19.2 %collective-permute-start.4 = (bf16[2,10,32,512]{3,2,1,0:T(8,128)(2,1)}, bf16[2,10,32,512]{3,2,1,0:T(8,128)(2,1)S(1)}, u32[]{:S(2)}, u32[]{:S(2)}) collective-permute-start(bf16[2,10,32,512]{3,2,1,0:T(8,128)(2,1)} %get-tuple-element.56), channel_id=1, source_target_pairs={{8,16},{16,8},{10,18},{18,10},{12,20},{20,12},{14,22},{22,14},{9,1... | collective-permute-start | bytes 1966088 | tf_op jit(solution)/shard_map/ppermute | solution.py:37
  8.6 17.1 %collective-permute-start.6 = (bf16[2,10,32,512]{3,2,1,0:T(8,128)(2,1)}, bf16[2,10,32,512]{3,2,1,0:T(8,128)(2,1)S(1)}, u32[]{:S(2)}, u32[]{:S(2)}) collective-permute-start(bf16[2,10,32,512]{3,2,1,0:T(8,128)(2,1)} %get-tuple-element.56), channel_id=1, source_target_pairs={{0,8},{2,10},{4,12},{6,14},{8,0},{10,2},{12,4},{14,6},{16,24},{18,... | collective-permute-start | bytes 1966088 | tf_op jit(solution)/shard_map/ppermute | solution.py:23
  20.5 9.0 %copy-start.4 = (bf16[128,2688]{1,0:T(8,128)(2,1)}, bf16[128,2688]{1,0:T(8,128)(2,1)S(1)}, u32[]{:S(2)}) copy-start(bf16[128,2688]{1,0:T(8,128)(2,1)S(1)} %collective-permute-done.refs_1_) | copy-start | bytes 2064388
  20.7 0.9 copy-start.6
  21.6 16.1 %collective-permute-start.8 = (bf16[128,2688]{1,0:T(8,128)(2,1)S(1)}, bf16[128,2688]{1,0:T(8,128)(2,1)S(1)}, u32[]{:S(2)}, u32[]{:S(2)}) collective-permute-start(bf16[128,2688]{1,0:T(8,128)(2,1)S(1)} %collective-permute-done.refs_1_), channel_id=1, source_target_pairs={{0,1},{1,0},{2,3},{3,2},{4,5},{5,4},{6,7},{7,6},{8,9},{9,8},{10,11... | collective-permute-start | bytes 2064392 | tf_op jit(solution)/shard_map/ppermute | solution.py:28
  24.4 5.1 %copy-start.12 = (bf16[2,10,32,512]{3,2,1,0:T(8,128)(2,1)}, bf16[2,10,32,512]{3,2,1,0:T(8,128)(2,1)S(1)}, u32[]{:S(2)}) copy-start(bf16[2,10,32,512]{3,2,1,0:T(8,128)(2,1)S(1)} %collective-permute-done.4) | copy-start | bytes 1966084
  24.4 16.4 %collective-permute-start.5 = (bf16[2,10,32,512]{3,2,1,0:T(8,128)(2,1)S(1)}, bf16[2,10,32,512]{3,2,1,0:T(8,128)(2,1)S(1)}, u32[]{:S(2)}, u32[]{:S(2)}) collective-permute-start(bf16[2,10,32,512]{3,2,1,0:T(8,128)(2,1)S(1)} %collective-permute-done.4), channel_id=1, source_target_pairs={{0,8},{2,10},{4,12},{6,14},{8,0},{10,2},{12,4},{14,6},{16,24},{18,... | collective-permute-start | bytes 1966088 | tf_op jit(solution)/shard_map/ppermute | solution.py:23
  25.8 17.9 %collective-permute-start.7 = (bf16[2,10,32,512]{3,2,1,0:T(8,128)(2,1)S(1)}, bf16[2,10,32,512]{3,2,1,0:T(8,128)(2,1)S(1)}, u32[]{:S(2)}, u32[]{:S(2)}) collective-permute-start(bf16[2,10,32,512]{3,2,1,0:T(8,128)(2,1)S(1)} %collective-permute-done.6), channel_id=1, source_target_pairs={{8,16},{16,8},{10,18},{18,10},{12,20},{20,12},{14,22},{22,14},{9,1... | collective-permute-start | bytes 1966088 | tf_op jit(solution)/shard_map/ppermute | solution.py:37
  28.2 15.5 %collective-permute-start.3 = (bf16[128,2688]{1,0:T(8,128)(2,1)S(1)}, bf16[128,2688]{1,0:T(8,128)(2,1)S(1)}, u32[]{:S(2)}, u32[]{:S(2)}) collective-permute-start(bf16[128,2688]{1,0:T(8,128)(2,1)S(1)} %collective-permute-done.refs_1_), channel_id=1, source_target_pairs={{0,2},{2,0},{4,6},{6,4},{8,10},{10,8},{12,14},{14,12},{16,18},{18,... | collective-permute-start | bytes 2064392 | tf_op jit(solution)/shard_map/ppermute | solution.py:23
  29.5 16.5 %copy-start.1 = (bf16[128,2560]{1,0:T(8,128)(2,1)S(1)}, bf16[128,2560]{1,0:T(8,128)(2,1)}, u32[]{:S(2)}) copy-start(bf16[128,2560]{1,0:T(8,128)(2,1)} %refs_2_.1) | copy-start | bytes 1966084
  29.5 17.9 %copy-start = (bf16[128,2688]{1,0:T(8,128)(2,1)S(1)}, bf16[128,2688]{1,0:T(8,128)(2,1)}, u32[]{:S(2)}) copy-start(bf16[128,2688]{1,0:T(8,128)(2,1)} %get-tuple-element.41.refs_0_.refs_1_) | copy-start | bytes 2064388
  29.5 31.3 %collective-permute-start.13 = (bf16[2,2,10,32,512]{4,3,2,1,0:T(8,128)(2,1)S(1)}, bf16[2,2,10,32,512]{4,3,2,1,0:T(8,128)(2,1)}, u32[]{:S(2)}, u32[]{:S(2)}) collective-permute-start(bf16[2,2,10,32,512]{4,3,2,1,0:T(8,128)(2,1)S(1)} %pad_maximum_fusion.refs_5_), channel_id=1, source_target_pairs={{0,4},{2,6},{4,0},{6,2},{8,12},{10,14},{12,8},{14,10},{16,20},{18,... | collective-permute-start | bytes 3932168 | tf_op jit(solution)/shard_map/ppermute | solution.py:23
  37.7 1.9 %copy-start.2 = (bf16[128,2688]{1,0:T(8,128)(2,1)}, bf16[128,2688]{1,0:T(8,128)(2,1)S(1)}, u32[]{:S(2)}) copy-start(bf16[128,2688]{1,0:T(8,128)(2,1)S(1)} %collective-permute-done.8.refs_5_) | copy-start | bytes 2064388
  38.6 6.9 %collective-permute-start.11 = (bf16[64,2688]{1,0:T(8,128)(2,1)}, bf16[64,2688]{1,0:T(8,128)(2,1)}, u32[]{:S(2)}, u32[]{:S(2)}) collective-permute-start(bf16[64,2688]{1,0:T(8,128)(2,1)} %get-tuple-element.81), channel_id=1, source_target_pairs={{0,2},{2,0},{4,6},{6,4},{8,10},{10,8},{12,14},{14,12},{16,18},{18,... | collective-permute-start | bytes 1032200 | tf_op jit(solution)/shard_map/ppermute | solution.py:23
  40.7 4.7 %copy-start.14 = (bf16[2,10,32,512]{3,2,1,0:T(8,128)(2,1)}, bf16[2,10,32,512]{3,2,1,0:T(8,128)(2,1)S(1)}, u32[]{:S(2)}) copy-start(bf16[2,10,32,512]{3,2,1,0:T(8,128)(2,1)S(1)} %collective-permute-done.5) | copy-start | bytes 1966084
  40.7 5.3 %collective-permute-start.12 = (bf16[64,2688]{1,0:T(8,128)(2,1)}, bf16[64,2688]{1,0:T(8,128)(2,1)}, u32[]{:S(2)}, u32[]{:S(2)}) collective-permute-start(bf16[64,2688]{1,0:T(8,128)(2,1)} %get-tuple-element.80), channel_id=1, source_target_pairs={{0,2},{2,0},{4,6},{6,4},{8,10},{10,8},{12,14},{14,12},{16,18},{18,... | collective-permute-start | bytes 1032200 | tf_op jit(solution)/shard_map/ppermute | solution.py:23
  43.7 0.9 copy-start.10
  43.7 2.8 %collective-permute-start.10 = (bf16[64,2688]{1,0:T(8,128)(2,1)}, bf16[64,2688]{1,0:T(8,128)(2,1)}, u32[]{:S(2)}, u32[]{:S(2)}) collective-permute-start(bf16[64,2688]{1,0:T(8,128)(2,1)} %get-tuple-element.82), channel_id=1, source_target_pairs={{0,2},{2,0},{4,6},{6,4},{8,10},{10,8},{12,14},{14,12},{16,18},{18,... | collective-permute-start | bytes 1032200 | tf_op jit(solution)/shard_map/ppermute | solution.py:23
  44.6 0.9 copy-start.8
  45.4 2.0 %collective-permute-start.9 = (bf16[64,2688]{1,0:T(8,128)(2,1)}, bf16[64,2688]{1,0:T(8,128)(2,1)}, u32[]{:S(2)}, u32[]{:S(2)}) collective-permute-start(bf16[64,2688]{1,0:T(8,128)(2,1)} %get-tuple-element.83), channel_id=1, source_target_pairs={{0,2},{2,0},{4,6},{6,4},{8,10},{10,8},{12,14},{14,12},{16,18},{18,... | collective-permute-start | bytes 1032200 | tf_op jit(solution)/shard_map/ppermute | solution.py:23
  45.5 32.4 %collective-permute-start.19 = (bf16[2,2,10,32,512]{4,3,2,1,0:T(8,128)(2,1)S(1)}, bf16[2,2,10,32,512]{4,3,2,1,0:T(8,128)(2,1)S(1)}, u32[]{:S(2)}, u32[]{:S(2)}) collective-permute-start(bf16[2,2,10,32,512]{4,3,2,1,0:T(8,128)(2,1)S(1)} %pad_maximum_fusion.refs_5_), channel_id=1, source_target_pairs={{0,2},{2,0},{4,6},{6,4},{8,10},{10,8},{12,14},{14,12},{16,18},{18,... | collective-permute-start | bytes 3932168 | tf_op jit(solution)/shard_map/ppermute | solution.py:23
  46.0 28.0 %collective-permute-start.18 = (bf16[128,2560]{1,0:T(8,128)(2,1)S(1)}, bf16[128,2560]{1,0:T(8,128)(2,1)S(1)}, u32[]{:S(2)}, u32[]{:S(2)}) collective-permute-start(bf16[128,2560]{1,0:T(8,128)(2,1)S(1)} %copy-done.1), channel_id=1, source_target_pairs={{0,1},{1,0},{2,3},{3,2},{4,5},{5,4},{6,7},{7,6},{8,9},{9,8},{10,11... | collective-permute-start | bytes 1966088 | tf_op jit(solution)/shard_map/ppermute | solution.py:28
  47.4 1.1 copy-start.3
  48.5 1.1 copy-start.5
  49.6 1.1 copy-start.7
  50.7 1.1 copy-start.9
  51.8 5.2 %copy-start.11 = (bf16[2,10,32,512]{3,2,1,0:T(8,128)(2,1)S(1)}, bf16[2,10,32,512]{3,2,1,0:T(8,128)(2,1)}, u32[]{:S(2)}) copy-start(bf16[2,10,32,512]{3,2,1,0:T(8,128)(2,1)} %copy-done.10) | copy-start | bytes 1966084
  57.0 1.1 copy-start.13
  57.0 1.3 %copy-start.15 = (bf16[2,10,32,512]{3,2,1,0:T(8,128)(2,1)S(1)}, bf16[2,10,32,512]{3,2,1,0:T(8,128)(2,1)}, u32[]{:S(2)}) copy-start(bf16[2,10,32,512]{3,2,1,0:T(8,128)(2,1)} %copy-done.14) | copy-start | bytes 1966084
  57.1 16.8 %collective-permute-start.15 = (bf16[2,10,32,512]{3,2,1,0:T(8,128)(2,1)S(1)}, bf16[2,10,32,512]{3,2,1,0:T(8,128)(2,1)S(1)}, u32[]{:S(2)}, u32[]{:S(2)}) collective-permute-start(bf16[2,10,32,512]{3,2,1,0:T(8,128)(2,1)S(1)} %broadcast_select_fusion), channel_id=1, source_target_pairs={{0,8},{2,10},{4,12},{6,14},{8,0},{10,2},{12,4},{14,6},{16,24},{18,... | collective-permute-start | bytes 1966088 | tf_op jit(solution)/shard_map/ppermute | solution.py:23
  60.8 16.4 %collective-permute-start.17 = (bf16[2,10,32,512]{3,2,1,0:T(8,128)(2,1)S(1)}, bf16[2,10,32,512]{3,2,1,0:T(8,128)(2,1)S(1)}, u32[]{:S(2)}, u32[]{:S(2)}) collective-permute-start(bf16[2,10,32,512]{3,2,1,0:T(8,128)(2,1)S(1)} %select_select_fusion.1.refs_7_), channel_id=1, source_target_pairs={{0,4},{2,6},{4,0},{6,2},{8,12},{10,14},{12,8},{14,10},{16,20},{18,... | collective-permute-start | bytes 1966088 | tf_op jit(solution)/shard_map/ppermute | solution.py:23
  62.3 15.7 %collective-permute-start.21 = (bf16[2,10,32,512]{3,2,1,0:T(8,128)(2,1)S(1)}, bf16[2,10,32,512]{3,2,1,0:T(8,128)(2,1)S(1)}, u32[]{:S(2)}, u32[]{:S(2)}) collective-permute-start(bf16[2,10,32,512]{3,2,1,0:T(8,128)(2,1)S(1)} %select_select_fusion.1.refs_7_), channel_id=1, source_target_pairs={{0,2},{2,0},{4,6},{6,4},{8,10},{10,8},{12,14},{14,12},{16,18},{18,... | collective-permute-start | bytes 1966088 | tf_op jit(solution)/shard_map/ppermute | solution.py:23
  74.0 9.3 %collective-permute-start.20 = (bf16[2,2,10,32,512]{4,3,2,1,0:T(8,128)(2,1)}, bf16[2,2,10,32,512]{4,3,2,1,0:T(8,128)(2,1)S(1)}, u32[]{:S(2)}, u32[]{:S(2)}) collective-permute-start(bf16[2,2,10,32,512]{4,3,2,1,0:T(8,128)(2,1)} %collective-permute-done.13.refs_6_), channel_id=1, source_target_pairs={{0,2},{2,0},{4,6},{6,4},{8,10},{10,8},{12,14},{14,12},{16,18},{18,... | collective-permute-start | bytes 3932168 | tf_op jit(solution)/shard_map/ppermute | solution.py:23
  77.2 4.5 %collective-permute-start.22 = (bf16[2,10,32,512]{3,2,1,0:T(8,128)(2,1)S(1)}, bf16[2,10,32,512]{3,2,1,0:T(8,128)(2,1)S(1)}, u32[]{:S(2)}, u32[]{:S(2)}) collective-permute-start(bf16[2,10,32,512]{3,2,1,0:T(8,128)(2,1)S(1)} %collective-permute-done.17.refs_8_), channel_id=1, source_target_pairs={{0,2},{2,0},{4,6},{6,4},{8,10},{10,8},{12,14},{14,12},{16,18},{18,... | collective-permute-start | bytes 1966088 | tf_op jit(solution)/shard_map/ppermute | solution.py:23
  77.2 6.0 %collective-permute-start.23 = (bf16[2,10,32,512]{3,2,1,0:T(8,128)(2,1)S(1)}, bf16[2,10,32,512]{3,2,1,0:T(8,128)(2,1)S(1)}, u32[]{:S(2)}, u32[]{:S(2)}) collective-permute-start(bf16[2,10,32,512]{3,2,1,0:T(8,128)(2,1)S(1)} %select_select_fusion.refs_11_), channel_id=1, source_target_pairs={{0,2},{2,0},{4,6},{6,4},{8,10},{10,8},{12,14},{14,12},{16,18},{18,... | collective-permute-start | bytes 1966088 | tf_op jit(solution)/shard_map/ppermute | solution.py:23
  77.9 16.7 %collective-permute-start.14 = (bf16[2,10,32,512]{3,2,1,0:T(8,128)(2,1)S(1)}, bf16[2,10,32,512]{3,2,1,0:T(8,128)(2,1)S(1)}, u32[]{:S(2)}, u32[]{:S(2)}) collective-permute-start(bf16[2,10,32,512]{3,2,1,0:T(8,128)(2,1)S(1)} %get-tuple-element.57), channel_id=1, source_target_pairs={{0,8},{2,10},{4,12},{6,14},{8,0},{10,2},{12,4},{14,6},{16,24},{18,... | collective-permute-start | bytes 1966088 | tf_op jit(solution)/shard_map/ppermute | solution.py:23
  78.0 18.5 %collective-permute-start.16 = (bf16[2,10,32,512]{3,2,1,0:T(8,128)(2,1)S(1)}, bf16[2,10,32,512]{3,2,1,0:T(8,128)(2,1)S(1)}, u32[]{:S(2)}, u32[]{:S(2)}) collective-permute-start(bf16[2,10,32,512]{3,2,1,0:T(8,128)(2,1)S(1)} %add_convert_fusion.3), channel_id=1, source_target_pairs={{8,16},{16,8},{10,18},{18,10},{12,20},{20,12},{14,22},{22,14},{9,1... | collective-permute-start | bytes 1966088 | tf_op jit(solution)/shard_map/ppermute | solution.py:37
  81.7 16.4 %collective-permute-start.24 = (bf16[2,10,32,512]{3,2,1,0:T(8,128)(2,1)S(1)}, bf16[2,10,32,512]{3,2,1,0:T(8,128)(2,1)S(1)}, u32[]{:S(2)}, u32[]{:S(2)}) collective-permute-start(bf16[2,10,32,512]{3,2,1,0:T(8,128)(2,1)S(1)} %select_select_fusion.refs_11_), channel_id=1, source_target_pairs={{0,4},{2,6},{4,0},{6,2},{8,12},{10,14},{12,8},{14,10},{16,20},{18,... | collective-permute-start | bytes 1966088 | tf_op jit(solution)/shard_map/ppermute | solution.py:23
  98.1 2.1 %collective-permute-start.25 = (bf16[2,10,32,512]{3,2,1,0:T(8,128)(2,1)S(1)}, bf16[2,10,32,512]{3,2,1,0:T(8,128)(2,1)S(1)}, u32[]{:S(2)}, u32[]{:S(2)}) collective-permute-start(bf16[2,10,32,512]{3,2,1,0:T(8,128)(2,1)S(1)} %collective-permute-done.24.refs_4_), channel_id=1, source_target_pairs={{0,2},{2,0},{4,6},{6,4},{8,10},{10,8},{12,14},{14,12},{16,18},{18,... | collective-permute-start | bytes 1966088 | tf_op jit(solution)/shard_map/ppermute | solution.py:23
  104.7 16.8 %collective-permute-start.26 = (bf16[128,2560]{1,0:T(8,128)(2,1)S(1)}, bf16[128,2560]{1,0:T(8,128)(2,1)S(1)}, u32[]{:S(2)}, u32[]{:S(2)}) collective-permute-start(bf16[128,2560]{1,0:T(8,128)(2,1)S(1)} %shard_map.108), channel_id=1, source_target_pairs={{0,1},{1,0},{2,3},{3,2},{4,5},{5,4},{6,7},{7,6},{8,9},{9,8},{10,11... | collective-permute-start | bytes 1966088 | tf_op jit(solution)/shard_map/ppermute | solution.py:28
  105.5 17.0 %collective-permute-start.28 = (bf16[2,10,32,512]{3,2,1,0:T(8,128)(2,1)S(1)}, bf16[2,10,32,512]{3,2,1,0:T(8,128)(2,1)S(1)}, u32[]{:S(2)}, u32[]{:S(2)}) collective-permute-start(bf16[2,10,32,512]{3,2,1,0:T(8,128)(2,1)S(1)} %add_convert_fusion), channel_id=1, source_target_pairs={{0,8},{2,10},{4,12},{6,14},{8,0},{10,2},{12,4},{14,6},{16,24},{18,... | collective-permute-start | bytes 1966088 | tf_op jit(solution)/shard_map/ppermute | solution.py:23
  105.8 18.4 %collective-permute-start.27 = (bf16[2,10,32,512]{3,2,1,0:T(8,128)(2,1)S(1)}, bf16[2,10,32,512]{3,2,1,0:T(8,128)(2,1)S(1)}, u32[]{:S(2)}, u32[]{:S(2)}) collective-permute-start(bf16[2,10,32,512]{3,2,1,0:T(8,128)(2,1)S(1)} %add_convert_fusion.1), channel_id=1, source_target_pairs={{8,16},{16,8},{10,18},{18,10},{12,20},{20,12},{14,22},{22,14},{9,1... | collective-permute-start | bytes 1966088 | tf_op jit(solution)/shard_map/ppermute | solution.py:37

commit v6 on v5

--- a/solution.py
+++ b/solution.py
@@ -341,7 +341,7 @@
 def result_kernel(last, begin, groups, planes, lookups, top, *refs):
     place_ref, tokens, refs = refs[0], refs[1 : 1 + 2 * groups], refs[1 + 2 * groups :]
     turned_ref, first_ref, second_ref, pre_ref, back_ref, out_ref, *refs = refs
-    grad, part, up, down, turned, pre_part, back_part, token_sem, piece_sem, turned_sem = refs
+    grad, part, up, down, back_part, token_sem, piece_sem = refs
     count, width = out_ref.shape
     tok = count // groups
     experts, blocks, per, rows, hid = down.shape
@@ -374,17 +374,8 @@
             )
         )
     mine = pl.ds(begin, count)
-    copies.append(pltpu.make_async_copy(pre_ref.at[mine], pre_part, piece_sem.at[0, 2]))
     copies.append(pltpu.make_async_copy(back_ref.at[mine], back_part, piece_sem.at[1, 2]))
-    turns = [
-        pltpu.make_async_copy(
-            turned_ref.at[:, :, pl.ds(b * hid, hid)],
-            turned.at[:, :, pl.ds(b * hid, hid)],
-            turned_sem.at[b],
-        )
-        for b in range(blocks)
-    ]
-    for copy in copies + turns:
+    for copy in copies:
         copy.start()
     for copy in copies:
         copy.wait()
@@ -404,7 +395,7 @@
         slopes = []
         for e in range(experts):
             units = pl.ds(e * hid, hid)
-            pre = pre_part[span, units] + jnp.dot(
+            pre = pre_ref[pl.ds(begin + start, chunk), units] + jnp.dot(
                 mine, up[e].reshape(slab, hid), preferred_element_type=jnp.float32
             )
             late = jnp.zeros((chunk, LANES), jnp.float32)
@@ -427,12 +418,10 @@
             slopes.append(slope.astype(jnp.bfloat16))
         for b in range(blocks):
             cols = pl.ds(b * hid, hid)
-            if start == 0:
-                turns[b].wait()
             total = jnp.zeros((chunk, hid), jnp.float32)
             for e in range(experts):
                 total += jnp.dot(
-                    slopes[e], turned[e, :, cols], preferred_element_type=jnp.float32
+                    slopes[e], turned_ref[e, :, cols], preferred_element_type=jnp.float32
                 )
             out_ref[span, cols] = total.astype(out_ref.dtype)
         late = jnp.zeros((chunk, slab), jnp.float32)
@@ -501,19 +490,18 @@
     return pl.pallas_call(
         functools.partial(result_kernel, last, begin, groups, dp // 4, lookups, top),
         out_shape=jax.ShapeDtypeStruct((groups * tok, width), dtype),
-        in_specs=[pl.BlockSpec(memory_space=pltpu.SMEM)] + [any_space] * (2 * groups + 5),
+        in_specs=[pl.BlockSpec(memory_space=pltpu.SMEM)]
+        + [any_space] * (2 * groups)
+        + [vmem, any_space, any_space, vmem, any_space],
         out_specs=vmem,
         scratch_shapes=[
             pltpu.VMEM((groups * tok, width + LANES), jnp.bfloat16),
             pltpu.VMEM((groups * tok, slab), jnp.bfloat16),
             pltpu.VMEM((experts, slab // rows, rows, hid), jnp.bfloat16),
             pltpu.VMEM((experts, blocks, LANES // rows, rows, hid), jnp.bfloat16),
-            pltpu.VMEM(turned.shape, jnp.bfloat16),
-            pltpu.VMEM((groups * tok, pre.shape[1]), jnp.float32),
-            pltpu.VMEM((groups * tok, pre.shape[1]), jnp.float32),
+            pltpu.VMEM((groups * tok, back.shape[1]), jnp.float32),
             pltpu.SemaphoreType.DMA((2, groups)),
             pltpu.SemaphoreType.DMA((2, 3)),
-            pltpu.SemaphoreType.DMA((blocks,)),
         ],
         compiler_params=pltpu.CompilerParams(
             vmem_limit_bytes=room(

time: 127 us -> 125 us (0.984)
  Pallas kernels: 24.1 us -> 21.1 us
  waiting for transfers between devices: 64.5 us -> 66 us
    pallas_call x2, Pallas kernels: 9 us -> 5.94 us  [expert_results(): pl.pallas_call(functools.partial(result_kernel, last, begin, groups, dp /...]
    ppermute x4, waiting for transfers between devices: 15.4 us -> 16.9 us  [over_expert(): lax.ppermute(value, 'expert', [(i, (i + step) % size) for i in range(size)])]
  transfers between devices with their start and end apart: 29 -> 29, of which waited for: 17 -> 17; matrix products, arithmetic and copies ran while one was open for 4% -> 4% of each run, Pallas kernels for 13% -> 12%
where the time goes in v6:
time: 125 us; the launch traced here: 124 us
  waiting for transfers between devices  66 us (53%)
  starting transfers between devices  22.6 us (18%)
  Pallas kernels  21.1 us (17%)
  local copies, waits for them, and re-layouts  10 us (8%)
  other arithmetic  3.14 us (3%)
    ppermute x21, waiting for transfers between devices, swap(): return lax.ppermute(value, 'dp', [(i, i ^ bit) for i in range(size)])  41.2 us
    ppermute x4, waiting for transfers between devices, over_expert(): lax.ppermute(value, 'expert', [(i, (i + step) % size) for i in range(size)])  16.9 us
    ppermute x4, starting transfers between devices, over_even(): return lax.ppermute(value, 'dp', pairs)  12 us
    unnamed x32, local copies, waits for them, and re-layouts  8.1 us
    ppermute x4, waiting for transfers between devices, over_even(): return lax.ppermute(value, 'dp', pairs)  7.82 us
    ppermute x21, starting transfers between devices, swap(): return lax.ppermute(value, 'dp', [(i, i ^ bit) for i in range(size)])  6.53 us
    pallas_call x1, Pallas kernels, hidden_layers(): pl.pallas_call(functools.partial(hidden_kernel, where, last, groups, dp /...  6.22 us
    pallas_call x2, Pallas kernels, expert_results(): pl.pallas_call(functools.partial(result_kernel, last, begin, groups, dp /...  5.94 us
  transfers between devices with their start and end apart: 29, of which 17 were waited for; matrix products, arithmetic and copies ran while one was open for 4% of the time, Pallas kernels for 12%

profile of v6, /device:TPU:10, one launch (start us, length us, event | category | flops | bytes accessed | tf_op | source)
XLA Modules:
  0.0 123.8 jit_solution(12196400976187993847)
XLA Ops:
  0.6 2.4 %shard_map.104 = (bf16[2,10,32,512]{3,2,1,0:T(8,128)(2,1)}, bf16[128,2688]{1,0:T(8,128)(2,1)}) custom-call(bf16[2,160,512]{2,1,0:T(8,128)(2,1)} %up_ref.1, bf16[2,32,2560]{2,1,0:T(8,128)(2,1)} %down_ref.1, bf16[128,2560]{1,0:T(8,128)(2,1)} %grad_ref.1, s32[2,128]{1,0:T(2,128)} %bitcast.16, f32[2,128]{1,0:T(2,128)} %bitcast.17, f32[4,128]{1,0:T(4,128)} %bitcast.13, ...), custom_call_target="tpu_custom_call" | custom-call | tf_op jit(solution)/shard_map/pallas_call | solution.py:95
  3.1 0.5 collective-permute-start
  3.6 1.5 %collective-permute-start.1 = (bf16[128,2688]{1,0:T(8,128)(2,1)}, bf16[128,2688]{1,0:T(8,128)(2,1)S(1)}, u32[]{:S(2)}, u32[]{:S(2)}) collective-permute-start(bf16[128,2688]{1,0:T(8,128)(2,1)} %get-tuple-element.41.refs_0_.refs_1_), channel_id=1, source_target_pairs={{0,1},{1,0},{2,3},{3,2},{4,5},{5,4},{6,7},{7,6},{8,9},{9,8},{10,11... | collective-permute-start | bytes 2064392 | tf_op jit(solution)/shard_map/ppermute | solution.py:28
  5.1 3.5 %collective-permute-start.4 = (bf16[2,10,32,512]{3,2,1,0:T(8,128)(2,1)}, bf16[2,10,32,512]{3,2,1,0:T(8,128)(2,1)S(1)}, u32[]{:S(2)}, u32[]{:S(2)}) collective-permute-start(bf16[2,10,32,512]{3,2,1,0:T(8,128)(2,1)} %get-tuple-element.56), channel_id=1, source_target_pairs={{8,16},{16,8},{10,18},{18,10},{12,20},{20,12},{14,22},{22,14},{9,1... | collective-permute-start | bytes 1966088 | tf_op jit(solution)/shard_map/ppermute | solution.py:37
  8.7 11.8 %collective-permute-done.refs_1_ = bf16[128,2688]{1,0:T(8,128)(2,1)S(1)} collective-permute-done((bf16[128,2688]{1,0:T(8,128)(2,1)}, bf16[128,2688]{1,0:T(8,128)(2,1)S(1)}, u32[]{:S(2)}, u32[]{:S(2)}) %collective-permute-start) | collective-permute-done | bytes 688160 | tf_op jit(solution)/shard_map/ppermute | solution.py:23
  20.7 0.9 copy-done.6
  21.6 1.5 %collective-permute-start.8 = (bf16[128,2688]{1,0:T(8,128)(2,1)S(1)}, bf16[128,2688]{1,0:T(8,128)(2,1)S(1)}, u32[]{:S(2)}, u32[]{:S(2)}) collective-permute-start(bf16[128,2688]{1,0:T(8,128)(2,1)S(1)} %collective-permute-done.refs_1_), channel_id=1, source_target_pairs={{0,1},{1,0},{2,3},{3,2},{4,5},{5,4},{6,7},{7,6},{8,9},{9,8},{10,11... | collective-permute-start | bytes 2064392 | tf_op jit(solution)/shard_map/ppermute | solution.py:28
  23.1 1.3 %collective-permute-done.4 = bf16[2,10,32,512]{3,2,1,0:T(8,128)(2,1)S(1)} collective-permute-done((bf16[2,10,32,512]{3,2,1,0:T(8,128)(2,1)}, bf16[2,10,32,512]{3,2,1,0:T(8,128)(2,1)S(1)}, u32[]{:S(2)}, u32[]{:S(2)}) %collective-permute-start.4) | collective-permute-done | bytes 655392 | tf_op jit(solution)/shard_map/ppermute | solution.py:37
  24.4 1.4 %collective-permute-done.6 = bf16[2,10,32,512]{3,2,1,0:T(8,128)(2,1)S(1)} collective-permute-done((bf16[2,10,32,512]{3,2,1,0:T(8,128)(2,1)}, bf16[2,10,32,512]{3,2,1,0:T(8,128)(2,1)S(1)}, u32[]{:S(2)}, u32[]{:S(2)}) %collective-permute-start.6) | collective-permute-done | bytes 655392 | tf_op jit(solution)/shard_map/ppermute | solution.py:23
  25.8 2.4 %collective-permute-start.7 = (bf16[2,10,32,512]{3,2,1,0:T(8,128)(2,1)S(1)}, bf16[2,10,32,512]{3,2,1,0:T(8,128)(2,1)S(1)}, u32[]{:S(2)}, u32[]{:S(2)}) collective-permute-start(bf16[2,10,32,512]{3,2,1,0:T(8,128)(2,1)S(1)} %collective-permute-done.6), channel_id=1, source_target_pairs={{8,16},{16,8},{10,18},{18,10},{12,20},{20,12},{14,22},{22,14},{9,1... | collective-permute-start | bytes 1966088 | tf_op jit(solution)/shard_map/ppermute | solution.py:37
  28.2 1.2 pad_maximum_fusion.refs_5_
  29.5 1.6 %collective-permute-start.13 = (bf16[2,2,10,32,512]{4,3,2,1,0:T(8,128)(2,1)S(1)}, bf16[2,2,10,32,512]{4,3,2,1,0:T(8,128)(2,1)}, u32[]{:S(2)}, u32[]{:S(2)}) collective-permute-start(bf16[2,2,10,32,512]{4,3,2,1,0:T(8,128)(2,1)S(1)} %pad_maximum_fusion.refs_5_), channel_id=1, source_target_pairs={{0,4},{2,6},{4,0},{6,2},{8,12},{10,14},{12,8},{14,10},{16,20},{18,... | collective-permute-start | bytes 3932168 | tf_op jit(solution)/shard_map/ppermute | solution.py:23
  31.1 6.6 %collective-permute-done.8.refs_5_ = bf16[128,2688]{1,0:T(8,128)(2,1)S(1)} collective-permute-done((bf16[128,2688]{1,0:T(8,128)(2,1)S(1)}, bf16[128,2688]{1,0:T(8,128)(2,1)S(1)}, u32[]{:S(2)}, u32[]{:S(2)}) %collective-permute-start.8) | collective-permute-done | bytes 688160 | tf_op jit(solution)/shard_map/ppermute | solution.py:28
  37.7 0.9 fusion
  38.6 1.0 fusion.1
  39.6 1.1 collective-permute-done.5
  40.7 2.9 %collective-permute-done.7 = bf16[2,10,32,512]{3,2,1,0:T(8,128)(2,1)S(1)} collective-permute-done((bf16[2,10,32,512]{3,2,1,0:T(8,128)(2,1)S(1)}, bf16[2,10,32,512]{3,2,1,0:T(8,128)(2,1)S(1)}, u32[]{:S(2)}, u32[]{:S(2)}) %collective-permute-start.7) | collective-permute-done | bytes 655392 | tf_op jit(solution)/shard_map/ppermute | solution.py:37
  43.7 0.9 copy-done.10
  44.6 0.9 copy-done.8
  45.5 0.5 collective-permute-start.19
  46.0 0.5 collective-permute-start.18
  46.5 0.9 collective-permute-done.9.refs_6_
  47.4 1.1 copy-done.3
  48.5 1.1 copy-done.5
  49.6 1.1 copy-done.7
  50.7 1.1 copy-done.9
  51.8 5.2 %shard_map.105 = (f32[2,10,32,512]{3,2,1,0:T(8,128)S(1)}, bf16[2,10,32,512]{3,2,1,0:T(8,128)(2,1)S(1)}, bf16[2,10,32,512]{3,2,1,0:T(8,128)(2,1)S(1)}, bf16[2,10,32,512]{3,2,1,0:T(8,128)(2,1)S(1)}) custom-call(s32[2]{0:T(128)S(1)} %pad_add_fusion.place_ref.refs_0_, bf16[128,2688]{1,0:T(8,128)(2,1)S(1)} %copy-done, bf16[128,2688]{1,0:T(8,128)(2,1)S(1)} %copy-done.5, ...), custom_call_target="tpu_custom_call" | custom-call | flops 2684354560 | bytes 4096 | tf_op jit(solution)/shard_map/pallas_call | solution.py:202
  57.2 0.9 copy-done.13
  58.4 2.5 %collective-permute-done.13.refs_6_ = bf16[2,2,10,32,512]{4,3,2,1,0:T(8,128)(2,1)} collective-permute-done((bf16[2,2,10,32,512]{4,3,2,1,0:T(8,128)(2,1)S(1)}, bf16[2,2,10,32,512]{4,3,2,1,0:T(8,128)(2,1)}, u32[]{:S(2)}, u32[]{:S(2)}) %collective-permute-start.13) | collective-permute-done | bytes 1310752 | tf_op jit(solution)/shard_map/ppermute | solution.py:23
  60.8 1.5 %collective-permute-start.17 = (bf16[2,10,32,512]{3,2,1,0:T(8,128)(2,1)S(1)}, bf16[2,10,32,512]{3,2,1,0:T(8,128)(2,1)S(1)}, u32[]{:S(2)}, u32[]{:S(2)}) collective-permute-start(bf16[2,10,32,512]{3,2,1,0:T(8,128)(2,1)S(1)} %select_select_fusion.1.refs_7_), channel_id=1, source_target_pairs={{0,4},{2,6},{4,0},{6,2},{8,12},{10,14},{12,8},{14,10},{16,20},{18,... | collective-permute-start | bytes 1966088 | tf_op jit(solution)/shard_map/ppermute | solution.py:23
  62.3 11.6 %collective-permute-done.15 = bf16[2,10,32,512]{3,2,1,0:T(8,128)(2,1)S(1)} collective-permute-done((bf16[2,10,32,512]{3,2,1,0:T(8,128)(2,1)S(1)}, bf16[2,10,32,512]{3,2,1,0:T(8,128)(2,1)S(1)}, u32[]{:S(2)}, u32[]{:S(2)}) %collective-permute-start.15) | collective-permute-done | bytes 655392 | tf_op jit(solution)/shard_map/ppermute | solution.py:23
  74.1 3.1 %collective-permute-done.17.refs_8_ = bf16[2,10,32,512]{3,2,1,0:T(8,128)(2,1)S(1)} collective-permute-done((bf16[2,10,32,512]{3,2,1,0:T(8,128)(2,1)S(1)}, bf16[2,10,32,512]{3,2,1,0:T(8,128)(2,1)S(1)}, u32[]{:S(2)}, u32[]{:S(2)}) %collective-permute-start.17) | collective-permute-done | bytes 655392 | tf_op jit(solution)/shard_map/ppermute | solution.py:23
  77.2 0.5 collective-permute-start.23
  78.0 3.4 %collective-permute-start.16 = (bf16[2,10,32,512]{3,2,1,0:T(8,128)(2,1)S(1)}, bf16[2,10,32,512]{3,2,1,0:T(8,128)(2,1)S(1)}, u32[]{:S(2)}, u32[]{:S(2)}) collective-permute-start(bf16[2,10,32,512]{3,2,1,0:T(8,128)(2,1)S(1)} %add_convert_fusion.3), channel_id=1, source_target_pairs={{8,16},{16,8},{10,18},{18,10},{12,20},{20,12},{14,22},{22,14},{9,1... | collective-permute-start | bytes 1966088 | tf_op jit(solution)/shard_map/ppermute | solution.py:37
  81.5 1.6 %collective-permute-start.24 = (bf16[2,10,32,512]{3,2,1,0:T(8,128)(2,1)S(1)}, bf16[2,10,32,512]{3,2,1,0:T(8,128)(2,1)S(1)}, u32[]{:S(2)}, u32[]{:S(2)}) collective-permute-start(bf16[2,10,32,512]{3,2,1,0:T(8,128)(2,1)S(1)} %select_select_fusion.refs_11_), channel_id=1, source_target_pairs={{0,4},{2,6},{4,0},{6,2},{8,12},{10,14},{12,8},{14,10},{16,20},{18,... | collective-permute-start | bytes 1966088 | tf_op jit(solution)/shard_map/ppermute | solution.py:23
  83.1 6.2 %shard_map.106 = (bf16[2,512,2560]{2,1,0:T(8,128)(2,1)S(1)}, f32[256,1024]{1,0:T(8,128)S(1)}, f32[256,1024]{1,0:T(8,128)S(1)}) custom-call(s32[2]{0:T(128)S(1)} %pad_add_fusion.place_ref.refs_0_, bf16[128,2688]{1,0:T(8,128)(2,1)S(1)} %copy-done, bf16[128,2688]{1,0:T(8,128)(2,1)S(1)} %collective-permute-done.1.refs_4_.refs_2_.refs_1_, ...), custom_call_target="tpu_custom_call" | custom-call | flops 2684354560 | bytes 20971520 | tf_op jit(solution)/shard_map/pallas_call | solution.py:448
  89.3 5.4 %collective-permute-done.14 = bf16[2,10,32,512]{3,2,1,0:T(8,128)(2,1)S(1)} collective-permute-done((bf16[2,10,32,512]{3,2,1,0:T(8,128)(2,1)S(1)}, bf16[2,10,32,512]{3,2,1,0:T(8,128)(2,1)S(1)}, u32[]{:S(2)}, u32[]{:S(2)}) %collective-permute-start.14) | collective-permute-done | bytes 655392 | tf_op jit(solution)/shard_map/ppermute | solution.py:23
  94.7 1.9 %collective-permute-done.16 = bf16[2,10,32,512]{3,2,1,0:T(8,128)(2,1)S(1)} collective-permute-done((bf16[2,10,32,512]{3,2,1,0:T(8,128)(2,1)S(1)}, bf16[2,10,32,512]{3,2,1,0:T(8,128)(2,1)S(1)}, u32[]{:S(2)}, u32[]{:S(2)}) %collective-permute-start.16) | collective-permute-done | bytes 655392 | tf_op jit(solution)/shard_map/ppermute | solution.py:37
  96.6 1.3 %collective-permute-done.24.refs_4_ = bf16[2,10,32,512]{3,2,1,0:T(8,128)(2,1)S(1)} collective-permute-done((bf16[2,10,32,512]{3,2,1,0:T(8,128)(2,1)S(1)}, bf16[2,10,32,512]{3,2,1,0:T(8,128)(2,1)S(1)}, u32[]{:S(2)}, u32[]{:S(2)}) %collective-permute-start.24) | collective-permute-done | bytes 655392 | tf_op jit(solution)/shard_map/ppermute | solution.py:23
  97.9 2.1 %collective-permute-done.25.refs_5_ = bf16[2,10,32,512]{3,2,1,0:T(8,128)(2,1)S(1)} collective-permute-done((bf16[2,10,32,512]{3,2,1,0:T(8,128)(2,1)S(1)}, bf16[2,10,32,512]{3,2,1,0:T(8,128)(2,1)S(1)}, u32[]{:S(2)}, u32[]{:S(2)}) %collective-permute-start.25) | collective-permute-done | bytes 655392 | tf_op jit(solution)/shard_map/ppermute | solution.py:23
  100.0 3.0 %shard_map.108 = bf16[128,2560]{1,0:T(8,128)(2,1)S(1)} custom-call(s32[2]{0:T(128)S(1)} %pad_add_fusion.place_ref.refs_0_, bf16[128,2688]{1,0:T(8,128)(2,1)S(1)} %collective-permute-done.1.refs_4_.refs_2_.refs_1_, bf16[128,2560]{1,0:T(8,128)(2,1)S(1)} %collective-permute-done.18.refs_4_.refs_2_, bf16[2,512,2560]{2,1,0:T(8,128)(2,1)S(1)} %get-tuple-element.68.refs_3_, ...), custom_call_target="tpu_custom_call" | custom-call | flops 671088640 | bytes 9175040 | tf_op jit(solution)/shard_map/pallas_call | solution.py:490
  103.0 0.6 collective-permute-start.26
  104.1 2.7 %collective-permute-start.27 = (bf16[2,10,32,512]{3,2,1,0:T(8,128)(2,1)S(1)}, bf16[2,10,32,512]{3,2,1,0:T(8,128)(2,1)S(1)}, u32[]{:S(2)}, u32[]{:S(2)}) collective-permute-start(bf16[2,10,32,512]{3,2,1,0:T(8,128)(2,1)S(1)} %add_convert_fusion.1), channel_id=1, source_target_pairs={{8,16},{16,8},{10,18},{18,10},{12,20},{20,12},{14,22},{22,14},{9,1... | collective-permute-start | bytes 1966088 | tf_op jit(solution)/shard_map/ppermute | solution.py:37
  106.8 3.0 %shard_map.107 = f32[128,2560]{1,0:T(8,128)S(1)} custom-call(s32[2]{0:T(128)S(1)} %pad_add_fusion.place_ref.refs_0_, bf16[128,2688]{1,0:T(8,128)(2,1)S(1)} %copy-done, bf16[128,2560]{1,0:T(8,128)(2,1)S(1)} %copy-done.1, bf16[2,512,2560]{2,1,0:T(8,128)(2,1)S(1)} %get-tuple-element.68.refs_3_, bf16[2,10,32,512]{3,2,1,0:T(8,128)(2,1)S(1)} %collective-permute-done.24.refs_4_, ...), custom_call_target="tpu_custom_call" | custom-call | flops 671088640 | bytes 9175040 | tf_op jit(solution)/shard_map/pallas_call | solution.py:490
  109.8 10.1 %collective-permute-done.26 = bf16[128,2560]{1,0:T(8,128)(2,1)S(1)} collective-permute-done((bf16[128,2560]{1,0:T(8,128)(2,1)S(1)}, bf16[128,2560]{1,0:T(8,128)(2,1)S(1)}, u32[]{:S(2)}, u32[]{:S(2)}) %collective-permute-start.26) | collective-permute-done | bytes 655392 | tf_op jit(solution)/shard_map/ppermute | solution.py:28
  119.8 1.0 add_convert_fusion.2
  120.8 1.7 %collective-permute-done.27.refs_1_ = bf16[2,10,32,512]{3,2,1,0:T(8,128)(2,1)S(1)} collective-permute-done((bf16[2,10,32,512]{3,2,1,0:T(8,128)(2,1)S(1)}, bf16[2,10,32,512]{3,2,1,0:T(8,128)(2,1)S(1)}, u32[]{:S(2)}, u32[]{:S(2)}) %collective-permute-start.27) | collective-permute-done | bytes 655392 | tf_op jit(solution)/shard_map/ppermute | solution.py:37
  122.5 1.3 %shard_map.109 = f32[256,1280]{1,0:T(8,128)} custom-call(f32[2,10,32,512]{3,2,1,0:T(8,128)S(1)} %get-tuple-element.75.refs_0_, bf16[2,10,32,512]{3,2,1,0:T(8,128)(2,1)S(1)} %collective-permute-done.27.refs_1_, bf16[2,10,32,512]{3,2,1,0:T(8,128)(2,1)S(1)} %collective-permute-done.28.refs_2_), custom_call_target="tpu_custom_call" | custom-call | tf_op jit(solution)/shard_map/pallas_call | solution.py:243
  (59 shorter events, 1.9 us)
Async XLA Ops:
  3.1 17.4 %collective-permute-start = (bf16[128,2688]{1,0:T(8,128)(2,1)}, bf16[128,2688]{1,0:T(8,128)(2,1)S(1)}, u32[]{:S(2)}, u32[]{:S(2)}) collective-permute-start(bf16[128,2688]{1,0:T(8,128)(2,1)} %get-tuple-element.41.refs_0_.refs_1_), channel_id=1, source_target_pairs={{0,4},{2,6},{4,0},{6,2},{8,12},{10,14},{12,8},{14,10},{16,20},{18,... | collective-permute-start | bytes 2064392 | tf_op jit(solution)/shard_map/ppermute | solution.py:23
  3.6 17.1 %collective-permute-start.1 = (bf16[128,2688]{1,0:T(8,128)(2,1)}, bf16[128,2688]{1,0:T(8,128)(2,1)S(1)}, u32[]{:S(2)}, u32[]{:S(2)}) collective-permute-start(bf16[128,2688]{1,0:T(8,128)(2,1)} %get-tuple-element.41.refs_0_.refs_1_), channel_id=1, source_target_pairs={{0,1},{1,0},{2,3},{3,2},{4,5},{5,4},{6,7},{7,6},{8,9},{9,8},{10,11... | collective-permute-start | bytes 2064392 | tf_op jit(solution)/shard_map/ppermute | solution.py:28
  5.1 15.6 %collective-permute-start.2 = (bf16[128,2688]{1,0:T(8,128)(2,1)}, bf16[128,2688]{1,0:T(8,128)(2,1)S(1)}, u32[]{:S(2)}, u32[]{:S(2)}) collective-permute-start(bf16[128,2688]{1,0:T(8,128)(2,1)} %get-tuple-element.41.refs_0_.refs_1_), channel_id=1, source_target_pairs={{0,2},{2,0},{4,6},{6,4},{8,10},{10,8},{12,14},{14,12},{16,18},{18,... | collective-permute-start | bytes 2064392 | tf_op jit(solution)/shard_map/ppermute | solution.py:23
  5.1 19.2 %collective-permute-start.4 = (bf16[2,10,32,512]{3,2,1,0:T(8,128)(2,1)}, bf16[2,10,32,512]{3,2,1,0:T(8,128)(2,1)S(1)}, u32[]{:S(2)}, u32[]{:S(2)}) collective-permute-start(bf16[2,10,32,512]{3,2,1,0:T(8,128)(2,1)} %get-tuple-element.56), channel_id=1, source_target_pairs={{8,16},{16,8},{10,18},{18,10},{12,20},{20,12},{14,22},{22,14},{9,1... | collective-permute-start | bytes 1966088 | tf_op jit(solution)/shard_map/ppermute | solution.py:37
  8.6 17.1 %collective-permute-start.6 = (bf16[2,10,32,512]{3,2,1,0:T(8,128)(2,1)}, bf16[2,10,32,512]{3,2,1,0:T(8,128)(2,1)S(1)}, u32[]{:S(2)}, u32[]{:S(2)}) collective-permute-start(bf16[2,10,32,512]{3,2,1,0:T(8,128)(2,1)} %get-tuple-element.56), channel_id=1, source_target_pairs={{0,8},{2,10},{4,12},{6,14},{8,0},{10,2},{12,4},{14,6},{16,24},{18,... | collective-permute-start | bytes 1966088 | tf_op jit(solution)/shard_map/ppermute | solution.py:23
  20.5 9.0 %copy-start.4 = (bf16[128,2688]{1,0:T(8,128)(2,1)}, bf16[128,2688]{1,0:T(8,128)(2,1)S(1)}, u32[]{:S(2)}) copy-start(bf16[128,2688]{1,0:T(8,128)(2,1)S(1)} %collective-permute-done.refs_1_) | copy-start | bytes 2064388
  20.7 0.9 copy-start.6
  21.6 16.1 %collective-permute-start.8 = (bf16[128,2688]{1,0:T(8,128)(2,1)S(1)}, bf16[128,2688]{1,0:T(8,128)(2,1)S(1)}, u32[]{:S(2)}, u32[]{:S(2)}) collective-permute-start(bf16[128,2688]{1,0:T(8,128)(2,1)S(1)} %collective-permute-done.refs_1_), channel_id=1, source_target_pairs={{0,1},{1,0},{2,3},{3,2},{4,5},{5,4},{6,7},{7,6},{8,9},{9,8},{10,11... | collective-permute-start | bytes 2064392 | tf_op jit(solution)/shard_map/ppermute | solution.py:28
  24.4 5.1 %copy-start.12 = (bf16[2,10,32,512]{3,2,1,0:T(8,128)(2,1)}, bf16[2,10,32,512]{3,2,1,0:T(8,128)(2,1)S(1)}, u32[]{:S(2)}) copy-start(bf16[2,10,32,512]{3,2,1,0:T(8,128)(2,1)S(1)} %collective-permute-done.4) | copy-start | bytes 1966084
  24.4 16.4 %collective-permute-start.5 = (bf16[2,10,32,512]{3,2,1,0:T(8,128)(2,1)S(1)}, bf16[2,10,32,512]{3,2,1,0:T(8,128)(2,1)S(1)}, u32[]{:S(2)}, u32[]{:S(2)}) collective-permute-start(bf16[2,10,32,512]{3,2,1,0:T(8,128)(2,1)S(1)} %collective-permute-done.4), channel_id=1, source_target_pairs={{0,8},{2,10},{4,12},{6,14},{8,0},{10,2},{12,4},{14,6},{16,24},{18,... | collective-permute-start | bytes 1966088 | tf_op jit(solution)/shard_map/ppermute | solution.py:23
  25.8 17.9 %collective-permute-start.7 = (bf16[2,10,32,512]{3,2,1,0:T(8,128)(2,1)S(1)}, bf16[2,10,32,512]{3,2,1,0:T(8,128)(2,1)S(1)}, u32[]{:S(2)}, u32[]{:S(2)}) collective-permute-start(bf16[2,10,32,512]{3,2,1,0:T(8,128)(2,1)S(1)} %collective-permute-done.6), channel_id=1, source_target_pairs={{8,16},{16,8},{10,18},{18,10},{12,20},{20,12},{14,22},{22,14},{9,1... | collective-permute-start | bytes 1966088 | tf_op jit(solution)/shard_map/ppermute | solution.py:37
  28.2 15.5 %collective-permute-start.3 = (bf16[128,2688]{1,0:T(8,128)(2,1)S(1)}, bf16[128,2688]{1,0:T(8,128)(2,1)S(1)}, u32[]{:S(2)}, u32[]{:S(2)}) collective-permute-start(bf16[128,2688]{1,0:T(8,128)(2,1)S(1)} %collective-permute-done.refs_1_), channel_id=1, source_target_pairs={{0,2},{2,0},{4,6},{6,4},{8,10},{10,8},{12,14},{14,12},{16,18},{18,... | collective-permute-start | bytes 2064392 | tf_op jit(solution)/shard_map/ppermute | solution.py:23
  29.5 16.5 %copy-start.1 = (bf16[128,2560]{1,0:T(8,128)(2,1)S(1)}, bf16[128,2560]{1,0:T(8,128)(2,1)}, u32[]{:S(2)}) copy-start(bf16[128,2560]{1,0:T(8,128)(2,1)} %refs_2_.1) | copy-start | bytes 1966084
  29.5 17.9 %copy-start = (bf16[128,2688]{1,0:T(8,128)(2,1)S(1)}, bf16[128,2688]{1,0:T(8,128)(2,1)}, u32[]{:S(2)}) copy-start(bf16[128,2688]{1,0:T(8,128)(2,1)} %get-tuple-element.41.refs_0_.refs_1_) | copy-start | bytes 2064388
  29.5 31.3 %collective-permute-start.13 = (bf16[2,2,10,32,512]{4,3,2,1,0:T(8,128)(2,1)S(1)}, bf16[2,2,10,32,512]{4,3,2,1,0:T(8,128)(2,1)}, u32[]{:S(2)}, u32[]{:S(2)}) collective-permute-start(bf16[2,2,10,32,512]{4,3,2,1,0:T(8,128)(2,1)S(1)} %pad_maximum_fusion.refs_5_), channel_id=1, source_target_pairs={{0,4},{2,6},{4,0},{6,2},{8,12},{10,14},{12,8},{14,10},{16,20},{18,... | collective-permute-start | bytes 3932168 | tf_op jit(solution)/shard_map/ppermute | solution.py:23
  37.7 1.9 %copy-start.2 = (bf16[128,2688]{1,0:T(8,128)(2,1)}, bf16[128,2688]{1,0:T(8,128)(2,1)S(1)}, u32[]{:S(2)}) copy-start(bf16[128,2688]{1,0:T(8,128)(2,1)S(1)} %collective-permute-done.8.refs_5_) | copy-start | bytes 2064388
  38.6 6.9 %collective-permute-start.11 = (bf16[64,2688]{1,0:T(8,128)(2,1)}, bf16[64,2688]{1,0:T(8,128)(2,1)}, u32[]{:S(2)}, u32[]{:S(2)}) collective-permute-start(bf16[64,2688]{1,0:T(8,128)(2,1)} %get-tuple-element.81), channel_id=1, source_target_pairs={{0,2},{2,0},{4,6},{6,4},{8,10},{10,8},{12,14},{14,12},{16,18},{18,... | collective-permute-start | bytes 1032200 | tf_op jit(solution)/shard_map/ppermute | solution.py:23
  40.7 4.7 %copy-start.14 = (bf16[2,10,32,512]{3,2,1,0:T(8,128)(2,1)}, bf16[2,10,32,512]{3,2,1,0:T(8,128)(2,1)S(1)}, u32[]{:S(2)}) copy-start(bf16[2,10,32,512]{3,2,1,0:T(8,128)(2,1)S(1)} %collective-permute-done.5) | copy-start | bytes 1966084
  40.7 5.3 %collective-permute-start.12 = (bf16[64,2688]{1,0:T(8,128)(2,1)}, bf16[64,2688]{1,0:T(8,128)(2,1)}, u32[]{:S(2)}, u32[]{:S(2)}) collective-permute-start(bf16[64,2688]{1,0:T(8,128)(2,1)} %get-tuple-element.80), channel_id=1, source_target_pairs={{0,2},{2,0},{4,6},{6,4},{8,10},{10,8},{12,14},{14,12},{16,18},{18,... | collective-permute-start | bytes 1032200 | tf_op jit(solution)/shard_map/ppermute | solution.py:23
  43.7 0.9 copy-start.10
  43.7 2.8 %collective-permute-start.10 = (bf16[64,2688]{1,0:T(8,128)(2,1)}, bf16[64,2688]{1,0:T(8,128)(2,1)}, u32[]{:S(2)}, u32[]{:S(2)}) collective-permute-start(bf16[64,2688]{1,0:T(8,128)(2,1)} %get-tuple-element.82), channel_id=1, source_target_pairs={{0,2},{2,0},{4,6},{6,4},{8,10},{10,8},{12,14},{14,12},{16,18},{18,... | collective-permute-start | bytes 1032200 | tf_op jit(solution)/shard_map/ppermute | solution.py:23
  44.6 0.9 copy-start.8
  45.4 2.0 %collective-permute-start.9 = (bf16[64,2688]{1,0:T(8,128)(2,1)}, bf16[64,2688]{1,0:T(8,128)(2,1)}, u32[]{:S(2)}, u32[]{:S(2)}) collective-permute-start(bf16[64,2688]{1,0:T(8,128)(2,1)} %get-tuple-element.83), channel_id=1, source_target_pairs={{0,2},{2,0},{4,6},{6,4},{8,10},{10,8},{12,14},{14,12},{16,18},{18,... | collective-permute-start | bytes 1032200 | tf_op jit(solution)/shard_map/ppermute | solution.py:23
  45.5 32.4 %collective-permute-start.19 = (bf16[2,2,10,32,512]{4,3,2,1,0:T(8,128)(2,1)S(1)}, bf16[2,2,10,32,512]{4,3,2,1,0:T(8,128)(2,1)S(1)}, u32[]{:S(2)}, u32[]{:S(2)}) collective-permute-start(bf16[2,2,10,32,512]{4,3,2,1,0:T(8,128)(2,1)S(1)} %pad_maximum_fusion.refs_5_), channel_id=1, source_target_pairs={{0,2},{2,0},{4,6},{6,4},{8,10},{10,8},{12,14},{14,12},{16,18},{18,... | collective-permute-start | bytes 3932168 | tf_op jit(solution)/shard_map/ppermute | solution.py:23
  46.0 28.0 %collective-permute-start.18 = (bf16[128,2560]{1,0:T(8,128)(2,1)S(1)}, bf16[128,2560]{1,0:T(8,128)(2,1)S(1)}, u32[]{:S(2)}, u32[]{:S(2)}) collective-permute-start(bf16[128,2560]{1,0:T(8,128)(2,1)S(1)} %copy-done.1), channel_id=1, source_target_pairs={{0,1},{1,0},{2,3},{3,2},{4,5},{5,4},{6,7},{7,6},{8,9},{9,8},{10,11... | collective-permute-start | bytes 1966088 | tf_op jit(solution)/shard_map/ppermute | solution.py:28
  47.4 1.1 copy-start.3
  48.5 1.1 copy-start.5
  49.6 1.1 copy-start.7
  50.7 1.1 copy-start.9
  51.8 5.2 %copy-start.11 = (bf16[2,10,32,512]{3,2,1,0:T(8,128)(2,1)S(1)}, bf16[2,10,32,512]{3,2,1,0:T(8,128)(2,1)}, u32[]{:S(2)}) copy-start(bf16[2,10,32,512]{3,2,1,0:T(8,128)(2,1)} %copy-done.10) | copy-start | bytes 1966084
  57.0 1.1 copy-start.13
  57.0 1.3 %copy-start.15 = (bf16[2,10,32,512]{3,2,1,0:T(8,128)(2,1)S(1)}, bf16[2,10,32,512]{3,2,1,0:T(8,128)(2,1)}, u32[]{:S(2)}) copy-start(bf16[2,10,32,512]{3,2,1,0:T(8,128)(2,1)} %copy-done.14) | copy-start | bytes 1966084
  57.1 16.8 %collective-permute-start.15 = (bf16[2,10,32,512]{3,2,1,0:T(8,128)(2,1)S(1)}, bf16[2,10,32,512]{3,2,1,0:T(8,128)(2,1)S(1)}, u32[]{:S(2)}, u32[]{:S(2)}) collective-permute-start(bf16[2,10,32,512]{3,2,1,0:T(8,128)(2,1)S(1)} %broadcast_select_fusion), channel_id=1, source_target_pairs={{0,8},{2,10},{4,12},{6,14},{8,0},{10,2},{12,4},{14,6},{16,24},{18,... | collective-permute-start | bytes 1966088 | tf_op jit(solution)/shard_map/ppermute | solution.py:23
  60.8 16.4 %collective-permute-start.17 = (bf16[2,10,32,512]{3,2,1,0:T(8,128)(2,1)S(1)}, bf16[2,10,32,512]{3,2,1,0:T(8,128)(2,1)S(1)}, u32[]{:S(2)}, u32[]{:S(2)}) collective-permute-start(bf16[2,10,32,512]{3,2,1,0:T(8,128)(2,1)S(1)} %select_select_fusion.1.refs_7_), channel_id=1, source_target_pairs={{0,4},{2,6},{4,0},{6,2},{8,12},{10,14},{12,8},{14,10},{16,20},{18,... | collective-permute-start | bytes 1966088 | tf_op jit(solution)/shard_map/ppermute | solution.py:23
  62.3 15.7 %collective-permute-start.21 = (bf16[2,10,32,512]{3,2,1,0:T(8,128)(2,1)S(1)}, bf16[2,10,32,512]{3,2,1,0:T(8,128)(2,1)S(1)}, u32[]{:S(2)}, u32[]{:S(2)}) collective-permute-start(bf16[2,10,32,512]{3,2,1,0:T(8,128)(2,1)S(1)} %select_select_fusion.1.refs_7_), channel_id=1, source_target_pairs={{0,2},{2,0},{4,6},{6,4},{8,10},{10,8},{12,14},{14,12},{16,18},{18,... | collective-permute-start | bytes 1966088 | tf_op jit(solution)/shard_map/ppermute | solution.py:23
  74.0 9.1 %collective-permute-start.20 = (bf16[2,2,10,32,512]{4,3,2,1,0:T(8,128)(2,1)}, bf16[2,2,10,32,512]{4,3,2,1,0:T(8,128)(2,1)S(1)}, u32[]{:S(2)}, u32[]{:S(2)}) collective-permute-start(bf16[2,2,10,32,512]{4,3,2,1,0:T(8,128)(2,1)} %collective-permute-done.13.refs_6_), channel_id=1, source_target_pairs={{0,2},{2,0},{4,6},{6,4},{8,10},{10,8},{12,14},{14,12},{16,18},{18,... | collective-permute-start | bytes 3932168 | tf_op jit(solution)/shard_map/ppermute | solution.py:23
  77.2 4.3 %collective-permute-start.22 = (bf16[2,10,32,512]{3,2,1,0:T(8,128)(2,1)S(1)}, bf16[2,10,32,512]{3,2,1,0:T(8,128)(2,1)S(1)}, u32[]{:S(2)}, u32[]{:S(2)}) collective-permute-start(bf16[2,10,32,512]{3,2,1,0:T(8,128)(2,1)S(1)} %collective-permute-done.17.refs_8_), channel_id=1, source_target_pairs={{0,2},{2,0},{4,6},{6,4},{8,10},{10,8},{12,14},{14,12},{16,18},{18,... | collective-permute-start | bytes 1966088 | tf_op jit(solution)/shard_map/ppermute | solution.py:23
  77.2 5.8 %collective-permute-start.23 = (bf16[2,10,32,512]{3,2,1,0:T(8,128)(2,1)S(1)}, bf16[2,10,32,512]{3,2,1,0:T(8,128)(2,1)S(1)}, u32[]{:S(2)}, u32[]{:S(2)}) collective-permute-start(bf16[2,10,32,512]{3,2,1,0:T(8,128)(2,1)S(1)} %select_select_fusion.refs_11_), channel_id=1, source_target_pairs={{0,2},{2,0},{4,6},{6,4},{8,10},{10,8},{12,14},{14,12},{16,18},{18,... | collective-permute-start | bytes 1966088 | tf_op jit(solution)/shard_map/ppermute | solution.py:23
  77.9 16.7 %collective-permute-start.14 = (bf16[2,10,32,512]{3,2,1,0:T(8,128)(2,1)S(1)}, bf16[2,10,32,512]{3,2,1,0:T(8,128)(2,1)S(1)}, u32[]{:S(2)}, u32[]{:S(2)}) collective-permute-start(bf16[2,10,32,512]{3,2,1,0:T(8,128)(2,1)S(1)} %get-tuple-element.57), channel_id=1, source_target_pairs={{0,8},{2,10},{4,12},{6,14},{8,0},{10,2},{12,4},{14,6},{16,24},{18,... | collective-permute-start | bytes 1966088 | tf_op jit(solution)/shard_map/ppermute | solution.py:23
  78.0 18.5 %collective-permute-start.16 = (bf16[2,10,32,512]{3,2,1,0:T(8,128)(2,1)S(1)}, bf16[2,10,32,512]{3,2,1,0:T(8,128)(2,1)S(1)}, u32[]{:S(2)}, u32[]{:S(2)}) collective-permute-start(bf16[2,10,32,512]{3,2,1,0:T(8,128)(2,1)S(1)} %add_convert_fusion.3), channel_id=1, source_target_pairs={{8,16},{16,8},{10,18},{18,10},{12,20},{20,12},{14,22},{22,14},{9,1... | collective-permute-start | bytes 1966088 | tf_op jit(solution)/shard_map/ppermute | solution.py:37
  81.5 16.4 %collective-permute-start.24 = (bf16[2,10,32,512]{3,2,1,0:T(8,128)(2,1)S(1)}, bf16[2,10,32,512]{3,2,1,0:T(8,128)(2,1)S(1)}, u32[]{:S(2)}, u32[]{:S(2)}) collective-permute-start(bf16[2,10,32,512]{3,2,1,0:T(8,128)(2,1)S(1)} %select_select_fusion.refs_11_), channel_id=1, source_target_pairs={{0,4},{2,6},{4,0},{6,2},{8,12},{10,14},{12,8},{14,10},{16,20},{18,... | collective-permute-start | bytes 1966088 | tf_op jit(solution)/shard_map/ppermute | solution.py:23
  97.9 2.1 %collective-permute-start.25 = (bf16[2,10,32,512]{3,2,1,0:T(8,128)(2,1)S(1)}, bf16[2,10,32,512]{3,2,1,0:T(8,128)(2,1)S(1)}, u32[]{:S(2)}, u32[]{:S(2)}) collective-permute-start(bf16[2,10,32,512]{3,2,1,0:T(8,128)(2,1)S(1)} %collective-permute-done.24.refs_4_), channel_id=1, source_target_pairs={{0,2},{2,0},{4,6},{6,4},{8,10},{10,8},{12,14},{14,12},{16,18},{18,... | collective-permute-start | bytes 1966088 | tf_op jit(solution)/shard_map/ppermute | solution.py:23
  103.0 16.8 %collective-permute-start.26 = (bf16[128,2560]{1,0:T(8,128)(2,1)S(1)}, bf16[128,2560]{1,0:T(8,128)(2,1)S(1)}, u32[]{:S(2)}, u32[]{:S(2)}) collective-permute-start(bf16[128,2560]{1,0:T(8,128)(2,1)S(1)} %shard_map.108), channel_id=1, source_target_pairs={{0,1},{1,0},{2,3},{3,2},{4,5},{5,4},{6,7},{7,6},{8,9},{9,8},{10,11... | collective-permute-start | bytes 1966088 | tf_op jit(solution)/shard_map/ppermute | solution.py:28
  103.8 17.0 %collective-permute-start.28 = (bf16[2,10,32,512]{3,2,1,0:T(8,128)(2,1)S(1)}, bf16[2,10,32,512]{3,2,1,0:T(8,128)(2,1)S(1)}, u32[]{:S(2)}, u32[]{:S(2)}) collective-permute-start(bf16[2,10,32,512]{3,2,1,0:T(8,128)(2,1)S(1)} %add_convert_fusion), channel_id=1, source_target_pairs={{0,8},{2,10},{4,12},{6,14},{8,0},{10,2},{12,4},{14,6},{16,24},{18,... | collective-permute-start | bytes 1966088 | tf_op jit(solution)/shard_map/ppermute | solution.py:23
  104.1 18.4 %collective-permute-start.27 = (bf16[2,10,32,512]{3,2,1,0:T(8,128)(2,1)S(1)}, bf16[2,10,32,512]{3,2,1,0:T(8,128)(2,1)S(1)}, u32[]{:S(2)}, u32[]{:S(2)}) collective-permute-start(bf16[2,10,32,512]{3,2,1,0:T(8,128)(2,1)S(1)} %add_convert_fusion.1), channel_id=1, source_target_pairs={{8,16},{16,8},{10,18},{18,10},{12,20},{20,12},{14,22},{22,14},{9,1... | collective-permute-start | bytes 1966088 | tf_op jit(solution)/shard_map/ppermute | solution.py:37

commit v7 on v6

--- a/solution.py
+++ b/solution.py
@@ -63,14 +63,21 @@
 
 
 def prepare_kernel(up_ref, down_ref, grad_ref, *refs):
-    ids_ref, weights_ref, gate_ref, owner_ref, slot_ref, packed_ref, rows_ref, meta_ref = refs
+    ids_ref, weights_ref, gate_ref, owner_ref, slot_ref, packed_ref, rows_ref, meta_ref, sem = refs
     blocks, rows, cols = packed_ref.shape[1] // 2, packed_ref.shape[2], packed_ref.shape[3]
+    tok, width = grad_ref.shape
+    copies = [pltpu.make_async_copy(grad_ref, rows_ref.at[:, pl.ds(0, width)], sem.at[0])]
     for e in range(packed_ref.shape[0]):
         for b in range(blocks):
-            packed_ref[e, b] = up_ref[e, b * rows : (b + 1) * rows, :]
-            packed_ref[e, blocks + b] = down_ref[e, :, b * cols : (b + 1) * cols]
-    tok, width = grad_ref.shape
-    rows_ref[:, pl.ds(0, width)] = grad_ref[...]
+            for source, at in (
+                (up_ref.at[e, pl.ds(b * rows, rows)], b),
+                (down_ref.at[e, :, pl.ds(b * cols, cols)], blocks + b),
+            ):
+                copies.append(
+                    pltpu.make_async_copy(source, packed_ref.at[e, at], sem.at[len(copies)])
+                )
+    for copy in copies:
+        copy.start()
     weights = weights_ref[...]
     high = weights.astype(jnp.bfloat16).astype(jnp.float32)
     meta_ref[...] = jnp.zeros_like(meta_ref)
@@ -86,6 +93,8 @@
         meta_ref[pl.ds(at, value.shape[0]), :] = value
         at += value.shape[0]
     rows_ref[:, pl.ds(width, LANES)] = meta_ref[...].T.astype(jnp.bfloat16)
+    for copy in copies:
+        copy.wait()
 
 
 def prepare(up, down, grad_out, expert_ids, gate_weights, engram_gate, owner, slot):
@@ -98,7 +107,12 @@
             jax.ShapeDtypeStruct((experts, 2 * (width // hid), rows, hid), up.dtype),
             jax.ShapeDtypeStruct((tok, width + LANES), grad_out.dtype),
         ),
-        scratch_shapes=[pltpu.VMEM((LANES, tok), jnp.float32)],
+        in_specs=[pl.BlockSpec(memory_space=pl.ANY)] * 3
+        + [pl.BlockSpec(memory_space=pltpu.VMEM)] * 5,
+        scratch_shapes=[
+            pltpu.VMEM((LANES, tok), jnp.float32),
+            pltpu.SemaphoreType.DMA((1 + 2 * experts * (width // hid),)),
+        ],
     )(up, down, grad_out, expert_ids.T, gate_weights.T, engram_gate.T, owner.T, slot.T)
 
 

time: 125 us -> 126 us (level)
  no operation moved by 1% of the time
where the time goes in v7:
time: 126 us; the launch traced here: 125 us
  waiting for transfers between devices  66 us (52%)
  starting transfers between devices  22.7 us (18%)
  Pallas kernels  21.8 us (17%)
  local copies, waits for them, and re-layouts  10 us (8%)
  other arithmetic  3.14 us (2%)
    ppermute x21, waiting for transfers between devices, swap(): return lax.ppermute(value, 'dp', [(i, i ^ bit) for i in range(size)])  41.2 us
    ppermute x4, waiting for transfers between devices, over_expert(): lax.ppermute(value, 'expert', [(i, (i + step) % size) for i in range(size)])  16.9 us
    ppermute x4, starting transfers between devices, over_even(): return lax.ppermute(value, 'dp', pairs)  12 us
    unnamed x32, local copies, waits for them, and re-layouts  8.1 us
    ppermute x4, waiting for transfers between devices, over_even(): return lax.ppermute(value, 'dp', pairs)  7.82 us
    ppermute x21, starting transfers between devices, swap(): return lax.ppermute(value, 'dp', [(i, i ^ bit) for i in range(size)])  6.6 us
    pallas_call x1, Pallas kernels, hidden_layers(): pl.pallas_call(functools.partial(hidden_kernel, where, last, groups, dp /...  6.22 us
    pallas_call x2, Pallas kernels, expert_results(): pl.pallas_call(functools.partial(result_kernel, last, begin, groups, dp /...  5.94 us
  transfers between devices with their start and end apart: 29, of which 17 were waited for; matrix products, arithmetic and copies ran while one was open for 4% of the time, Pallas kernels for 12%

profile of v7, /device:TPU:10, one launch (start us, length us, event | category | flops | bytes accessed | tf_op | source)
XLA Modules:
  0.0 124.6 jit_solution(13813445639166182308)
XLA Ops:
  0.6 3.2 %shard_map.104 = (bf16[2,10,32,512]{3,2,1,0:T(8,128)(2,1)}, bf16[128,2688]{1,0:T(8,128)(2,1)}) custom-call(bf16[2,160,512]{2,1,0:T(8,128)(2,1)} %up_ref.1, bf16[2,32,2560]{2,1,0:T(8,128)(2,1)} %down_ref.1, bf16[128,2560]{1,0:T(8,128)(2,1)} %grad_ref.1, s32[2,128]{1,0:T(2,128)} %bitcast.16, f32[2,128]{1,0:T(2,128)} %bitcast.17, f32[4,128]{1,0:T(4,128)} %bitcast.13, ...), custom_call_target="tpu_custom_call" | custom-call | tf_op jit(solution)/shard_map/pallas_call | solution.py:104
  3.8 0.6 collective-permute-start
  4.4 1.5 %collective-permute-start.1 = (bf16[128,2688]{1,0:T(8,128)(2,1)}, bf16[128,2688]{1,0:T(8,128)(2,1)S(1)}, u32[]{:S(2)}, u32[]{:S(2)}) collective-permute-start(bf16[128,2688]{1,0:T(8,128)(2,1)} %get-tuple-element.41.refs_0_.refs_1_), channel_id=1, source_target_pairs={{0,1},{1,0},{2,3},{3,2},{4,5},{5,4},{6,7},{7,6},{8,9},{9,8},{10,11... | collective-permute-start | bytes 2064392 | tf_op jit(solution)/shard_map/ppermute | solution.py:28
  5.9 3.5 %collective-permute-start.4 = (bf16[2,10,32,512]{3,2,1,0:T(8,128)(2,1)}, bf16[2,10,32,512]{3,2,1,0:T(8,128)(2,1)S(1)}, u32[]{:S(2)}, u32[]{:S(2)}) collective-permute-start(bf16[2,10,32,512]{3,2,1,0:T(8,128)(2,1)} %get-tuple-element.56), channel_id=1, source_target_pairs={{8,16},{16,8},{10,18},{18,10},{12,20},{20,12},{14,22},{22,14},{9,1... | collective-permute-start | bytes 1966088 | tf_op jit(solution)/shard_map/ppermute | solution.py:37
  9.5 11.8 %collective-permute-done.refs_1_ = bf16[128,2688]{1,0:T(8,128)(2,1)S(1)} collective-permute-done((bf16[128,2688]{1,0:T(8,128)(2,1)}, bf16[128,2688]{1,0:T(8,128)(2,1)S(1)}, u32[]{:S(2)}, u32[]{:S(2)}) %collective-permute-start) | collective-permute-done | bytes 688160 | tf_op jit(solution)/shard_map/ppermute | solution.py:23
  21.5 0.9 copy-done.6
  22.4 1.5 %collective-permute-start.8 = (bf16[128,2688]{1,0:T(8,128)(2,1)S(1)}, bf16[128,2688]{1,0:T(8,128)(2,1)S(1)}, u32[]{:S(2)}, u32[]{:S(2)}) collective-permute-start(bf16[128,2688]{1,0:T(8,128)(2,1)S(1)} %collective-permute-done.refs_1_), channel_id=1, source_target_pairs={{0,1},{1,0},{2,3},{3,2},{4,5},{5,4},{6,7},{7,6},{8,9},{9,8},{10,11... | collective-permute-start | bytes 2064392 | tf_op jit(solution)/shard_map/ppermute | solution.py:28
  23.9 1.3 %collective-permute-done.4 = bf16[2,10,32,512]{3,2,1,0:T(8,128)(2,1)S(1)} collective-permute-done((bf16[2,10,32,512]{3,2,1,0:T(8,128)(2,1)}, bf16[2,10,32,512]{3,2,1,0:T(8,128)(2,1)S(1)}, u32[]{:S(2)}, u32[]{:S(2)}) %collective-permute-start.4) | collective-permute-done | bytes 655392 | tf_op jit(solution)/shard_map/ppermute | solution.py:37
  25.2 1.4 %collective-permute-done.6 = bf16[2,10,32,512]{3,2,1,0:T(8,128)(2,1)S(1)} collective-permute-done((bf16[2,10,32,512]{3,2,1,0:T(8,128)(2,1)}, bf16[2,10,32,512]{3,2,1,0:T(8,128)(2,1)S(1)}, u32[]{:S(2)}, u32[]{:S(2)}) %collective-permute-start.6) | collective-permute-done | bytes 655392 | tf_op jit(solution)/shard_map/ppermute | solution.py:23
  26.6 2.4 %collective-permute-start.7 = (bf16[2,10,32,512]{3,2,1,0:T(8,128)(2,1)S(1)}, bf16[2,10,32,512]{3,2,1,0:T(8,128)(2,1)S(1)}, u32[]{:S(2)}, u32[]{:S(2)}) collective-permute-start(bf16[2,10,32,512]{3,2,1,0:T(8,128)(2,1)S(1)} %collective-permute-done.6), channel_id=1, source_target_pairs={{8,16},{16,8},{10,18},{18,10},{12,20},{20,12},{14,22},{22,14},{9,1... | collective-permute-start | bytes 1966088 | tf_op jit(solution)/shard_map/ppermute | solution.py:37
  29.1 1.2 pad_maximum_fusion.refs_5_
  30.3 1.6 %collective-permute-start.13 = (bf16[2,2,10,32,512]{4,3,2,1,0:T(8,128)(2,1)S(1)}, bf16[2,2,10,32,512]{4,3,2,1,0:T(8,128)(2,1)}, u32[]{:S(2)}, u32[]{:S(2)}) collective-permute-start(bf16[2,2,10,32,512]{4,3,2,1,0:T(8,128)(2,1)S(1)} %pad_maximum_fusion.refs_5_), channel_id=1, source_target_pairs={{0,4},{2,6},{4,0},{6,2},{8,12},{10,14},{12,8},{14,10},{16,20},{18,... | collective-permute-start | bytes 3932168 | tf_op jit(solution)/shard_map/ppermute | solution.py:23
  31.9 6.6 %collective-permute-done.8.refs_5_ = bf16[128,2688]{1,0:T(8,128)(2,1)S(1)} collective-permute-done((bf16[128,2688]{1,0:T(8,128)(2,1)S(1)}, bf16[128,2688]{1,0:T(8,128)(2,1)S(1)}, u32[]{:S(2)}, u32[]{:S(2)}) %collective-permute-start.8) | collective-permute-done | bytes 688160 | tf_op jit(solution)/shard_map/ppermute | solution.py:28
  38.5 0.9 fusion
  39.4 1.0 fusion.1
  40.4 1.1 collective-permute-done.5
  41.6 2.9 %collective-permute-done.7 = bf16[2,10,32,512]{3,2,1,0:T(8,128)(2,1)S(1)} collective-permute-done((bf16[2,10,32,512]{3,2,1,0:T(8,128)(2,1)S(1)}, bf16[2,10,32,512]{3,2,1,0:T(8,128)(2,1)S(1)}, u32[]{:S(2)}, u32[]{:S(2)}) %collective-permute-start.7) | collective-permute-done | bytes 655392 | tf_op jit(solution)/shard_map/ppermute | solution.py:37
  44.5 0.9 copy-done.10
  45.4 0.9 copy-done.8
  46.3 0.5 collective-permute-start.19
  46.8 0.5 collective-permute-start.18
  47.3 0.9 collective-permute-done.9.refs_6_
  48.2 1.1 copy-done.3
  49.3 1.1 copy-done.5
  50.4 1.1 copy-done.7
  51.5 1.1 copy-done.9
  52.6 5.2 %shard_map.105 = (f32[2,10,32,512]{3,2,1,0:T(8,128)S(1)}, bf16[2,10,32,512]{3,2,1,0:T(8,128)(2,1)S(1)}, bf16[2,10,32,512]{3,2,1,0:T(8,128)(2,1)S(1)}, bf16[2,10,32,512]{3,2,1,0:T(8,128)(2,1)S(1)}) custom-call(s32[2]{0:T(128)S(1)} %pad_add_fusion.place_ref.refs_0_, bf16[128,2688]{1,0:T(8,128)(2,1)S(1)} %copy-done, bf16[128,2688]{1,0:T(8,128)(2,1)S(1)} %copy-done.5, ...), custom_call_target="tpu_custom_call" | custom-call | flops 2684354560 | bytes 4096 | tf_op jit(solution)/shard_map/pallas_call | solution.py:216
  58.0 0.9 copy-done.13
  59.2 2.5 %collective-permute-done.13.refs_6_ = bf16[2,2,10,32,512]{4,3,2,1,0:T(8,128)(2,1)} collective-permute-done((bf16[2,2,10,32,512]{4,3,2,1,0:T(8,128)(2,1)S(1)}, bf16[2,2,10,32,512]{4,3,2,1,0:T(8,128)(2,1)}, u32[]{:S(2)}, u32[]{:S(2)}) %collective-permute-start.13) | collective-permute-done | bytes 1310752 | tf_op jit(solution)/shard_map/ppermute | solution.py:23
  61.7 1.5 %collective-permute-start.17 = (bf16[2,10,32,512]{3,2,1,0:T(8,128)(2,1)S(1)}, bf16[2,10,32,512]{3,2,1,0:T(8,128)(2,1)S(1)}, u32[]{:S(2)}, u32[]{:S(2)}) collective-permute-start(bf16[2,10,32,512]{3,2,1,0:T(8,128)(2,1)S(1)} %select_select_fusion.1.refs_7_), channel_id=1, source_target_pairs={{0,4},{2,6},{4,0},{6,2},{8,12},{10,14},{12,8},{14,10},{16,20},{18,... | collective-permute-start | bytes 1966088 | tf_op jit(solution)/shard_map/ppermute | solution.py:23
  63.1 11.6 %collective-permute-done.15 = bf16[2,10,32,512]{3,2,1,0:T(8,128)(2,1)S(1)} collective-permute-done((bf16[2,10,32,512]{3,2,1,0:T(8,128)(2,1)S(1)}, bf16[2,10,32,512]{3,2,1,0:T(8,128)(2,1)S(1)}, u32[]{:S(2)}, u32[]{:S(2)}) %collective-permute-start.15) | collective-permute-done | bytes 655392 | tf_op jit(solution)/shard_map/ppermute | solution.py:23
  74.9 3.1 %collective-permute-done.17.refs_8_ = bf16[2,10,32,512]{3,2,1,0:T(8,128)(2,1)S(1)} collective-permute-done((bf16[2,10,32,512]{3,2,1,0:T(8,128)(2,1)S(1)}, bf16[2,10,32,512]{3,2,1,0:T(8,128)(2,1)S(1)}, u32[]{:S(2)}, u32[]{:S(2)}) %collective-permute-start.17) | collective-permute-done | bytes 655392 | tf_op jit(solution)/shard_map/ppermute | solution.py:23
  78.0 0.5 collective-permute-start.23
  78.8 3.4 %collective-permute-start.16 = (bf16[2,10,32,512]{3,2,1,0:T(8,128)(2,1)S(1)}, bf16[2,10,32,512]{3,2,1,0:T(8,128)(2,1)S(1)}, u32[]{:S(2)}, u32[]{:S(2)}) collective-permute-start(bf16[2,10,32,512]{3,2,1,0:T(8,128)(2,1)S(1)} %add_convert_fusion.3), channel_id=1, source_target_pairs={{8,16},{16,8},{10,18},{18,10},{12,20},{20,12},{14,22},{22,14},{9,1... | collective-permute-start | bytes 1966088 | tf_op jit(solution)/shard_map/ppermute | solution.py:37
  82.3 1.6 %collective-permute-start.24 = (bf16[2,10,32,512]{3,2,1,0:T(8,128)(2,1)S(1)}, bf16[2,10,32,512]{3,2,1,0:T(8,128)(2,1)S(1)}, u32[]{:S(2)}, u32[]{:S(2)}) collective-permute-start(bf16[2,10,32,512]{3,2,1,0:T(8,128)(2,1)S(1)} %select_select_fusion.refs_11_), channel_id=1, source_target_pairs={{0,4},{2,6},{4,0},{6,2},{8,12},{10,14},{12,8},{14,10},{16,20},{18,... | collective-permute-start | bytes 1966088 | tf_op jit(solution)/shard_map/ppermute | solution.py:23
  83.9 6.2 %shard_map.106 = (bf16[2,512,2560]{2,1,0:T(8,128)(2,1)S(1)}, f32[256,1024]{1,0:T(8,128)S(1)}, f32[256,1024]{1,0:T(8,128)S(1)}) custom-call(s32[2]{0:T(128)S(1)} %pad_add_fusion.place_ref.refs_0_, bf16[128,2688]{1,0:T(8,128)(2,1)S(1)} %copy-done, bf16[128,2688]{1,0:T(8,128)(2,1)S(1)} %collective-permute-done.1.refs_4_.refs_2_.refs_1_, ...), custom_call_target="tpu_custom_call" | custom-call | flops 2684354560 | bytes 20971520 | tf_op jit(solution)/shard_map/pallas_call | solution.py:462
  90.1 5.4 %collective-permute-done.14 = bf16[2,10,32,512]{3,2,1,0:T(8,128)(2,1)S(1)} collective-permute-done((bf16[2,10,32,512]{3,2,1,0:T(8,128)(2,1)S(1)}, bf16[2,10,32,512]{3,2,1,0:T(8,128)(2,1)S(1)}, u32[]{:S(2)}, u32[]{:S(2)}) %collective-permute-start.14) | collective-permute-done | bytes 655392 | tf_op jit(solution)/shard_map/ppermute | solution.py:23
  95.5 1.9 %collective-permute-done.16 = bf16[2,10,32,512]{3,2,1,0:T(8,128)(2,1)S(1)} collective-permute-done((bf16[2,10,32,512]{3,2,1,0:T(8,128)(2,1)S(1)}, bf16[2,10,32,512]{3,2,1,0:T(8,128)(2,1)S(1)}, u32[]{:S(2)}, u32[]{:S(2)}) %collective-permute-start.16) | collective-permute-done | bytes 655392 | tf_op jit(solution)/shard_map/ppermute | solution.py:37
  97.4 1.3 %collective-permute-done.24.refs_4_ = bf16[2,10,32,512]{3,2,1,0:T(8,128)(2,1)S(1)} collective-permute-done((bf16[2,10,32,512]{3,2,1,0:T(8,128)(2,1)S(1)}, bf16[2,10,32,512]{3,2,1,0:T(8,128)(2,1)S(1)}, u32[]{:S(2)}, u32[]{:S(2)}) %collective-permute-start.24) | collective-permute-done | bytes 655392 | tf_op jit(solution)/shard_map/ppermute | solution.py:23
  98.7 2.1 %collective-permute-done.25.refs_5_ = bf16[2,10,32,512]{3,2,1,0:T(8,128)(2,1)S(1)} collective-permute-done((bf16[2,10,32,512]{3,2,1,0:T(8,128)(2,1)S(1)}, bf16[2,10,32,512]{3,2,1,0:T(8,128)(2,1)S(1)}, u32[]{:S(2)}, u32[]{:S(2)}) %collective-permute-start.25) | collective-permute-done | bytes 655392 | tf_op jit(solution)/shard_map/ppermute | solution.py:23
  100.8 3.0 %shard_map.108 = bf16[128,2560]{1,0:T(8,128)(2,1)S(1)} custom-call(s32[2]{0:T(128)S(1)} %pad_add_fusion.place_ref.refs_0_, bf16[128,2688]{1,0:T(8,128)(2,1)S(1)} %collective-permute-done.1.refs_4_.refs_2_.refs_1_, bf16[128,2560]{1,0:T(8,128)(2,1)S(1)} %collective-permute-done.18.refs_4_.refs_2_, bf16[2,512,2560]{2,1,0:T(8,128)(2,1)S(1)} %get-tuple-element.68.refs_3_, ...), custom_call_target="tpu_custom_call" | custom-call | flops 671088640 | bytes 9175040 | tf_op jit(solution)/shard_map/pallas_call | solution.py:504
  103.8 0.6 collective-permute-start.26
  104.9 2.7 %collective-permute-start.27 = (bf16[2,10,32,512]{3,2,1,0:T(8,128)(2,1)S(1)}, bf16[2,10,32,512]{3,2,1,0:T(8,128)(2,1)S(1)}, u32[]{:S(2)}, u32[]{:S(2)}) collective-permute-start(bf16[2,10,32,512]{3,2,1,0:T(8,128)(2,1)S(1)} %add_convert_fusion.1), channel_id=1, source_target_pairs={{8,16},{16,8},{10,18},{18,10},{12,20},{20,12},{14,22},{22,14},{9,1... | collective-permute-start | bytes 1966088 | tf_op jit(solution)/shard_map/ppermute | solution.py:37
  107.6 3.0 %shard_map.107 = f32[128,2560]{1,0:T(8,128)S(1)} custom-call(s32[2]{0:T(128)S(1)} %pad_add_fusion.place_ref.refs_0_, bf16[128,2688]{1,0:T(8,128)(2,1)S(1)} %copy-done, bf16[128,2560]{1,0:T(8,128)(2,1)S(1)} %copy-done.1, bf16[2,512,2560]{2,1,0:T(8,128)(2,1)S(1)} %get-tuple-element.68.refs_3_, bf16[2,10,32,512]{3,2,1,0:T(8,128)(2,1)S(1)} %collective-permute-done.24.refs_4_, ...), custom_call_target="tpu_custom_call" | custom-call | flops 671088640 | bytes 9175040 | tf_op jit(solution)/shard_map/pallas_call | solution.py:504
  110.6 10.1 %collective-permute-done.26 = bf16[128,2560]{1,0:T(8,128)(2,1)S(1)} collective-permute-done((bf16[128,2560]{1,0:T(8,128)(2,1)S(1)}, bf16[128,2560]{1,0:T(8,128)(2,1)S(1)}, u32[]{:S(2)}, u32[]{:S(2)}) %collective-permute-start.26) | collective-permute-done | bytes 655392 | tf_op jit(solution)/shard_map/ppermute | solution.py:28
  120.6 1.0 add_convert_fusion.2
  121.6 1.7 %collective-permute-done.27.refs_1_ = bf16[2,10,32,512]{3,2,1,0:T(8,128)(2,1)S(1)} collective-permute-done((bf16[2,10,32,512]{3,2,1,0:T(8,128)(2,1)S(1)}, bf16[2,10,32,512]{3,2,1,0:T(8,128)(2,1)S(1)}, u32[]{:S(2)}, u32[]{:S(2)}) %collective-permute-start.27) | collective-permute-done | bytes 655392 | tf_op jit(solution)/shard_map/ppermute | solution.py:37
  123.3 1.3 %shard_map.109 = f32[256,1280]{1,0:T(8,128)} custom-call(f32[2,10,32,512]{3,2,1,0:T(8,128)S(1)} %get-tuple-element.75.refs_0_, bf16[2,10,32,512]{3,2,1,0:T(8,128)(2,1)S(1)} %collective-permute-done.27.refs_1_, bf16[2,10,32,512]{3,2,1,0:T(8,128)(2,1)S(1)} %collective-permute-done.28.refs_2_), custom_call_target="tpu_custom_call" | custom-call | tf_op jit(solution)/shard_map/pallas_call | solution.py:257
  (59 shorter events, 1.9 us)
Async XLA Ops:
  3.8 17.5 %collective-permute-start = (bf16[128,2688]{1,0:T(8,128)(2,1)}, bf16[128,2688]{1,0:T(8,128)(2,1)S(1)}, u32[]{:S(2)}, u32[]{:S(2)}) collective-permute-start(bf16[128,2688]{1,0:T(8,128)(2,1)} %get-tuple-element.41.refs_0_.refs_1_), channel_id=1, source_target_pairs={{0,4},{2,6},{4,0},{6,2},{8,12},{10,14},{12,8},{14,10},{16,20},{18,... | collective-permute-start | bytes 2064392 | tf_op jit(solution)/shard_map/ppermute | solution.py:23
  4.4 17.1 %collective-permute-start.1 = (bf16[128,2688]{1,0:T(8,128)(2,1)}, bf16[128,2688]{1,0:T(8,128)(2,1)S(1)}, u32[]{:S(2)}, u32[]{:S(2)}) collective-permute-start(bf16[128,2688]{1,0:T(8,128)(2,1)} %get-tuple-element.41.refs_0_.refs_1_), channel_id=1, source_target_pairs={{0,1},{1,0},{2,3},{3,2},{4,5},{5,4},{6,7},{7,6},{8,9},{9,8},{10,11... | collective-permute-start | bytes 2064392 | tf_op jit(solution)/shard_map/ppermute | solution.py:28
  5.9 15.6 %collective-permute-start.2 = (bf16[128,2688]{1,0:T(8,128)(2,1)}, bf16[128,2688]{1,0:T(8,128)(2,1)S(1)}, u32[]{:S(2)}, u32[]{:S(2)}) collective-permute-start(bf16[128,2688]{1,0:T(8,128)(2,1)} %get-tuple-element.41.refs_0_.refs_1_), channel_id=1, source_target_pairs={{0,2},{2,0},{4,6},{6,4},{8,10},{10,8},{12,14},{14,12},{16,18},{18,... | collective-permute-start | bytes 2064392 | tf_op jit(solution)/shard_map/ppermute | solution.py:23
  5.9 19.2 %collective-permute-start.4 = (bf16[2,10,32,512]{3,2,1,0:T(8,128)(2,1)}, bf16[2,10,32,512]{3,2,1,0:T(8,128)(2,1)S(1)}, u32[]{:S(2)}, u32[]{:S(2)}) collective-permute-start(bf16[2,10,32,512]{3,2,1,0:T(8,128)(2,1)} %get-tuple-element.56), channel_id=1, source_target_pairs={{8,16},{16,8},{10,18},{18,10},{12,20},{20,12},{14,22},{22,14},{9,1... | collective-permute-start | bytes 1966088 | tf_op jit(solution)/shard_map/ppermute | solution.py:37
  9.4 17.1 %collective-permute-start.6 = (bf16[2,10,32,512]{3,2,1,0:T(8,128)(2,1)}, bf16[2,10,32,512]{3,2,1,0:T(8,128)(2,1)S(1)}, u32[]{:S(2)}, u32[]{:S(2)}) collective-permute-start(bf16[2,10,32,512]{3,2,1,0:T(8,128)(2,1)} %get-tuple-element.56), channel_id=1, source_target_pairs={{0,8},{2,10},{4,12},{6,14},{8,0},{10,2},{12,4},{14,6},{16,24},{18,... | collective-permute-start | bytes 1966088 | tf_op jit(solution)/shard_map/ppermute | solution.py:23
  21.3 9.0 %copy-start.4 = (bf16[128,2688]{1,0:T(8,128)(2,1)}, bf16[128,2688]{1,0:T(8,128)(2,1)S(1)}, u32[]{:S(2)}) copy-start(bf16[128,2688]{1,0:T(8,128)(2,1)S(1)} %collective-permute-done.refs_1_) | copy-start | bytes 2064388
  21.5 0.9 copy-start.6
  22.4 16.1 %collective-permute-start.8 = (bf16[128,2688]{1,0:T(8,128)(2,1)S(1)}, bf16[128,2688]{1,0:T(8,128)(2,1)S(1)}, u32[]{:S(2)}, u32[]{:S(2)}) collective-permute-start(bf16[128,2688]{1,0:T(8,128)(2,1)S(1)} %collective-permute-done.refs_1_), channel_id=1, source_target_pairs={{0,1},{1,0},{2,3},{3,2},{4,5},{5,4},{6,7},{7,6},{8,9},{9,8},{10,11... | collective-permute-start | bytes 2064392 | tf_op jit(solution)/shard_map/ppermute | solution.py:28
  25.2 5.1 %copy-start.12 = (bf16[2,10,32,512]{3,2,1,0:T(8,128)(2,1)}, bf16[2,10,32,512]{3,2,1,0:T(8,128)(2,1)S(1)}, u32[]{:S(2)}) copy-start(bf16[2,10,32,512]{3,2,1,0:T(8,128)(2,1)S(1)} %collective-permute-done.4) | copy-start | bytes 1966084
  25.2 16.4 %collective-permute-start.5 = (bf16[2,10,32,512]{3,2,1,0:T(8,128)(2,1)S(1)}, bf16[2,10,32,512]{3,2,1,0:T(8,128)(2,1)S(1)}, u32[]{:S(2)}, u32[]{:S(2)}) collective-permute-start(bf16[2,10,32,512]{3,2,1,0:T(8,128)(2,1)S(1)} %collective-permute-done.4), channel_id=1, source_target_pairs={{0,8},{2,10},{4,12},{6,14},{8,0},{10,2},{12,4},{14,6},{16,24},{18,... | collective-permute-start | bytes 1966088 | tf_op jit(solution)/shard_map/ppermute | solution.py:23
  26.6 17.9 %collective-permute-start.7 = (bf16[2,10,32,512]{3,2,1,0:T(8,128)(2,1)S(1)}, bf16[2,10,32,512]{3,2,1,0:T(8,128)(2,1)S(1)}, u32[]{:S(2)}, u32[]{:S(2)}) collective-permute-start(bf16[2,10,32,512]{3,2,1,0:T(8,128)(2,1)S(1)} %collective-permute-done.6), channel_id=1, source_target_pairs={{8,16},{16,8},{10,18},{18,10},{12,20},{20,12},{14,22},{22,14},{9,1... | collective-permute-start | bytes 1966088 | tf_op jit(solution)/shard_map/ppermute | solution.py:37
  29.0 15.5 %collective-permute-start.3 = (bf16[128,2688]{1,0:T(8,128)(2,1)S(1)}, bf16[128,2688]{1,0:T(8,128)(2,1)S(1)}, u32[]{:S(2)}, u32[]{:S(2)}) collective-permute-start(bf16[128,2688]{1,0:T(8,128)(2,1)S(1)} %collective-permute-done.refs_1_), channel_id=1, source_target_pairs={{0,2},{2,0},{4,6},{6,4},{8,10},{10,8},{12,14},{14,12},{16,18},{18,... | collective-permute-start | bytes 2064392 | tf_op jit(solution)/shard_map/ppermute | solution.py:23
  30.3 16.5 %copy-start.1 = (bf16[128,2560]{1,0:T(8,128)(2,1)S(1)}, bf16[128,2560]{1,0:T(8,128)(2,1)}, u32[]{:S(2)}) copy-start(bf16[128,2560]{1,0:T(8,128)(2,1)} %refs_2_.1) | copy-start | bytes 1966084
  30.3 17.9 %copy-start = (bf16[128,2688]{1,0:T(8,128)(2,1)S(1)}, bf16[128,2688]{1,0:T(8,128)(2,1)}, u32[]{:S(2)}) copy-start(bf16[128,2688]{1,0:T(8,128)(2,1)} %get-tuple-element.41.refs_0_.refs_1_) | copy-start | bytes 2064388
  30.3 31.3 %collective-permute-start.13 = (bf16[2,2,10,32,512]{4,3,2,1,0:T(8,128)(2,1)S(1)}, bf16[2,2,10,32,512]{4,3,2,1,0:T(8,128)(2,1)}, u32[]{:S(2)}, u32[]{:S(2)}) collective-permute-start(bf16[2,2,10,32,512]{4,3,2,1,0:T(8,128)(2,1)S(1)} %pad_maximum_fusion.refs_5_), channel_id=1, source_target_pairs={{0,4},{2,6},{4,0},{6,2},{8,12},{10,14},{12,8},{14,10},{16,20},{18,... | collective-permute-start | bytes 3932168 | tf_op jit(solution)/shard_map/ppermute | solution.py:23
  38.5 1.9 %copy-start.2 = (bf16[128,2688]{1,0:T(8,128)(2,1)}, bf16[128,2688]{1,0:T(8,128)(2,1)S(1)}, u32[]{:S(2)}) copy-start(bf16[128,2688]{1,0:T(8,128)(2,1)S(1)} %collective-permute-done.8.refs_5_) | copy-start | bytes 2064388
  39.4 6.9 %collective-permute-start.11 = (bf16[64,2688]{1,0:T(8,128)(2,1)}, bf16[64,2688]{1,0:T(8,128)(2,1)}, u32[]{:S(2)}, u32[]{:S(2)}) collective-permute-start(bf16[64,2688]{1,0:T(8,128)(2,1)} %get-tuple-element.81), channel_id=1, source_target_pairs={{0,2},{2,0},{4,6},{6,4},{8,10},{10,8},{12,14},{14,12},{16,18},{18,... | collective-permute-start | bytes 1032200 | tf_op jit(solution)/shard_map/ppermute | solution.py:23
  41.5 4.7 %copy-start.14 = (bf16[2,10,32,512]{3,2,1,0:T(8,128)(2,1)}, bf16[2,10,32,512]{3,2,1,0:T(8,128)(2,1)S(1)}, u32[]{:S(2)}) copy-start(bf16[2,10,32,512]{3,2,1,0:T(8,128)(2,1)S(1)} %collective-permute-done.5) | copy-start | bytes 1966084
  41.5 5.3 %collective-permute-start.12 = (bf16[64,2688]{1,0:T(8,128)(2,1)}, bf16[64,2688]{1,0:T(8,128)(2,1)}, u32[]{:S(2)}, u32[]{:S(2)}) collective-permute-start(bf16[64,2688]{1,0:T(8,128)(2,1)} %get-tuple-element.80), channel_id=1, source_target_pairs={{0,2},{2,0},{4,6},{6,4},{8,10},{10,8},{12,14},{14,12},{16,18},{18,... | collective-permute-start | bytes 1032200 | tf_op jit(solution)/shard_map/ppermute | solution.py:23
  44.5 0.9 copy-start.10
  44.5 2.8 %collective-permute-start.10 = (bf16[64,2688]{1,0:T(8,128)(2,1)}, bf16[64,2688]{1,0:T(8,128)(2,1)}, u32[]{:S(2)}, u32[]{:S(2)}) collective-permute-start(bf16[64,2688]{1,0:T(8,128)(2,1)} %get-tuple-element.82), channel_id=1, source_target_pairs={{0,2},{2,0},{4,6},{6,4},{8,10},{10,8},{12,14},{14,12},{16,18},{18,... | collective-permute-start | bytes 1032200 | tf_op jit(solution)/shard_map/ppermute | solution.py:23
  45.4 0.9 copy-start.8
  46.2 2.0 %collective-permute-start.9 = (bf16[64,2688]{1,0:T(8,128)(2,1)}, bf16[64,2688]{1,0:T(8,128)(2,1)}, u32[]{:S(2)}, u32[]{:S(2)}) collective-permute-start(bf16[64,2688]{1,0:T(8,128)(2,1)} %get-tuple-element.83), channel_id=1, source_target_pairs={{0,2},{2,0},{4,6},{6,4},{8,10},{10,8},{12,14},{14,12},{16,18},{18,... | collective-permute-start | bytes 1032200 | tf_op jit(solution)/shard_map/ppermute | solution.py:23
  46.3 32.4 %collective-permute-start.19 = (bf16[2,2,10,32,512]{4,3,2,1,0:T(8,128)(2,1)S(1)}, bf16[2,2,10,32,512]{4,3,2,1,0:T(8,128)(2,1)S(1)}, u32[]{:S(2)}, u32[]{:S(2)}) collective-permute-start(bf16[2,2,10,32,512]{4,3,2,1,0:T(8,128)(2,1)S(1)} %pad_maximum_fusion.refs_5_), channel_id=1, source_target_pairs={{0,2},{2,0},{4,6},{6,4},{8,10},{10,8},{12,14},{14,12},{16,18},{18,... | collective-permute-start | bytes 3932168 | tf_op jit(solution)/shard_map/ppermute | solution.py:23
  46.8 28.0 %collective-permute-start.18 = (bf16[128,2560]{1,0:T(8,128)(2,1)S(1)}, bf16[128,2560]{1,0:T(8,128)(2,1)S(1)}, u32[]{:S(2)}, u32[]{:S(2)}) collective-permute-start(bf16[128,2560]{1,0:T(8,128)(2,1)S(1)} %copy-done.1), channel_id=1, source_target_pairs={{0,1},{1,0},{2,3},{3,2},{4,5},{5,4},{6,7},{7,6},{8,9},{9,8},{10,11... | collective-permute-start | bytes 1966088 | tf_op jit(solution)/shard_map/ppermute | solution.py:28
  48.2 1.1 copy-start.3
  49.3 1.1 copy-start.5
  50.4 1.1 copy-start.7
  51.5 1.1 copy-start.9
  52.6 5.2 %copy-start.11 = (bf16[2,10,32,512]{3,2,1,0:T(8,128)(2,1)S(1)}, bf16[2,10,32,512]{3,2,1,0:T(8,128)(2,1)}, u32[]{:S(2)}) copy-start(bf16[2,10,32,512]{3,2,1,0:T(8,128)(2,1)} %copy-done.10) | copy-start | bytes 1966084
  57.8 1.1 copy-start.13
  57.8 1.3 %copy-start.15 = (bf16[2,10,32,512]{3,2,1,0:T(8,128)(2,1)S(1)}, bf16[2,10,32,512]{3,2,1,0:T(8,128)(2,1)}, u32[]{:S(2)}) copy-start(bf16[2,10,32,512]{3,2,1,0:T(8,128)(2,1)} %copy-done.14) | copy-start | bytes 1966084
  58.0 16.8 %collective-permute-start.15 = (bf16[2,10,32,512]{3,2,1,0:T(8,128)(2,1)S(1)}, bf16[2,10,32,512]{3,2,1,0:T(8,128)(2,1)S(1)}, u32[]{:S(2)}, u32[]{:S(2)}) collective-permute-start(bf16[2,10,32,512]{3,2,1,0:T(8,128)(2,1)S(1)} %broadcast_select_fusion), channel_id=1, source_target_pairs={{0,8},{2,10},{4,12},{6,14},{8,0},{10,2},{12,4},{14,6},{16,24},{18,... | collective-permute-start | bytes 1966088 | tf_op jit(solution)/shard_map/ppermute | solution.py:23
  61.7 16.4 %collective-permute-start.17 = (bf16[2,10,32,512]{3,2,1,0:T(8,128)(2,1)S(1)}, bf16[2,10,32,512]{3,2,1,0:T(8,128)(2,1)S(1)}, u32[]{:S(2)}, u32[]{:S(2)}) collective-permute-start(bf16[2,10,32,512]{3,2,1,0:T(8,128)(2,1)S(1)} %select_select_fusion.1.refs_7_), channel_id=1, source_target_pairs={{0,4},{2,6},{4,0},{6,2},{8,12},{10,14},{12,8},{14,10},{16,20},{18,... | collective-permute-start | bytes 1966088 | tf_op jit(solution)/shard_map/ppermute | solution.py:23
  63.1 15.7 %collective-permute-start.21 = (bf16[2,10,32,512]{3,2,1,0:T(8,128)(2,1)S(1)}, bf16[2,10,32,512]{3,2,1,0:T(8,128)(2,1)S(1)}, u32[]{:S(2)}, u32[]{:S(2)}) collective-permute-start(bf16[2,10,32,512]{3,2,1,0:T(8,128)(2,1)S(1)} %select_select_fusion.1.refs_7_), channel_id=1, source_target_pairs={{0,2},{2,0},{4,6},{6,4},{8,10},{10,8},{12,14},{14,12},{16,18},{18,... | collective-permute-start | bytes 1966088 | tf_op jit(solution)/shard_map/ppermute | solution.py:23
  74.8 9.1 %collective-permute-start.20 = (bf16[2,2,10,32,512]{4,3,2,1,0:T(8,128)(2,1)}, bf16[2,2,10,32,512]{4,3,2,1,0:T(8,128)(2,1)S(1)}, u32[]{:S(2)}, u32[]{:S(2)}) collective-permute-start(bf16[2,2,10,32,512]{4,3,2,1,0:T(8,128)(2,1)} %collective-permute-done.13.refs_6_), channel_id=1, source_target_pairs={{0,2},{2,0},{4,6},{6,4},{8,10},{10,8},{12,14},{14,12},{16,18},{18,... | collective-permute-start | bytes 3932168 | tf_op jit(solution)/shard_map/ppermute | solution.py:23
  78.0 4.3 %collective-permute-start.22 = (bf16[2,10,32,512]{3,2,1,0:T(8,128)(2,1)S(1)}, bf16[2,10,32,512]{3,2,1,0:T(8,128)(2,1)S(1)}, u32[]{:S(2)}, u32[]{:S(2)}) collective-permute-start(bf16[2,10,32,512]{3,2,1,0:T(8,128)(2,1)S(1)} %collective-permute-done.17.refs_8_), channel_id=1, source_target_pairs={{0,2},{2,0},{4,6},{6,4},{8,10},{10,8},{12,14},{14,12},{16,18},{18,... | collective-permute-start | bytes 1966088 | tf_op jit(solution)/shard_map/ppermute | solution.py:23
  78.0 5.8 %collective-permute-start.23 = (bf16[2,10,32,512]{3,2,1,0:T(8,128)(2,1)S(1)}, bf16[2,10,32,512]{3,2,1,0:T(8,128)(2,1)S(1)}, u32[]{:S(2)}, u32[]{:S(2)}) collective-permute-start(bf16[2,10,32,512]{3,2,1,0:T(8,128)(2,1)S(1)} %select_select_fusion.refs_11_), channel_id=1, source_target_pairs={{0,2},{2,0},{4,6},{6,4},{8,10},{10,8},{12,14},{14,12},{16,18},{18,... | collective-permute-start | bytes 1966088 | tf_op jit(solution)/shard_map/ppermute | solution.py:23
  78.8 16.7 %collective-permute-start.14 = (bf16[2,10,32,512]{3,2,1,0:T(8,128)(2,1)S(1)}, bf16[2,10,32,512]{3,2,1,0:T(8,128)(2,1)S(1)}, u32[]{:S(2)}, u32[]{:S(2)}) collective-permute-start(bf16[2,10,32,512]{3,2,1,0:T(8,128)(2,1)S(1)} %get-tuple-element.57), channel_id=1, source_target_pairs={{0,8},{2,10},{4,12},{6,14},{8,0},{10,2},{12,4},{14,6},{16,24},{18,... | collective-permute-start | bytes 1966088 | tf_op jit(solution)/shard_map/ppermute | solution.py:23
  78.8 18.5 %collective-permute-start.16 = (bf16[2,10,32,512]{3,2,1,0:T(8,128)(2,1)S(1)}, bf16[2,10,32,512]{3,2,1,0:T(8,128)(2,1)S(1)}, u32[]{:S(2)}, u32[]{:S(2)}) collective-permute-start(bf16[2,10,32,512]{3,2,1,0:T(8,128)(2,1)S(1)} %add_convert_fusion.3), channel_id=1, source_target_pairs={{8,16},{16,8},{10,18},{18,10},{12,20},{20,12},{14,22},{22,14},{9,1... | collective-permute-start | bytes 1966088 | tf_op jit(solution)/shard_map/ppermute | solution.py:37
  82.3 16.4 %collective-permute-start.24 = (bf16[2,10,32,512]{3,2,1,0:T(8,128)(2,1)S(1)}, bf16[2,10,32,512]{3,2,1,0:T(8,128)(2,1)S(1)}, u32[]{:S(2)}, u32[]{:S(2)}) collective-permute-start(bf16[2,10,32,512]{3,2,1,0:T(8,128)(2,1)S(1)} %select_select_fusion.refs_11_), channel_id=1, source_target_pairs={{0,4},{2,6},{4,0},{6,2},{8,12},{10,14},{12,8},{14,10},{16,20},{18,... | collective-permute-start | bytes 1966088 | tf_op jit(solution)/shard_map/ppermute | solution.py:23
  98.7 2.1 %collective-permute-start.25 = (bf16[2,10,32,512]{3,2,1,0:T(8,128)(2,1)S(1)}, bf16[2,10,32,512]{3,2,1,0:T(8,128)(2,1)S(1)}, u32[]{:S(2)}, u32[]{:S(2)}) collective-permute-start(bf16[2,10,32,512]{3,2,1,0:T(8,128)(2,1)S(1)} %collective-permute-done.24.refs_4_), channel_id=1, source_target_pairs={{0,2},{2,0},{4,6},{6,4},{8,10},{10,8},{12,14},{14,12},{16,18},{18,... | collective-permute-start | bytes 1966088 | tf_op jit(solution)/shard_map/ppermute | solution.py:23
  103.8 16.8 %collective-permute-start.26 = (bf16[128,2560]{1,0:T(8,128)(2,1)S(1)}, bf16[128,2560]{1,0:T(8,128)(2,1)S(1)}, u32[]{:S(2)}, u32[]{:S(2)}) collective-permute-start(bf16[128,2560]{1,0:T(8,128)(2,1)S(1)} %shard_map.108), channel_id=1, source_target_pairs={{0,1},{1,0},{2,3},{3,2},{4,5},{5,4},{6,7},{7,6},{8,9},{9,8},{10,11... | collective-permute-start | bytes 1966088 | tf_op jit(solution)/shard_map/ppermute | solution.py:28
  104.6 17.0 %collective-permute-start.28 = (bf16[2,10,32,512]{3,2,1,0:T(8,128)(2,1)S(1)}, bf16[2,10,32,512]{3,2,1,0:T(8,128)(2,1)S(1)}, u32[]{:S(2)}, u32[]{:S(2)}) collective-permute-start(bf16[2,10,32,512]{3,2,1,0:T(8,128)(2,1)S(1)} %add_convert_fusion), channel_id=1, source_target_pairs={{0,8},{2,10},{4,12},{6,14},{8,0},{10,2},{12,4},{14,6},{16,24},{18,... | collective-permute-start | bytes 1966088 | tf_op jit(solution)/shard_map/ppermute | solution.py:23
  104.9 18.4 %collective-permute-start.27 = (bf16[2,10,32,512]{3,2,1,0:T(8,128)(2,1)S(1)}, bf16[2,10,32,512]{3,2,1,0:T(8,128)(2,1)S(1)}, u32[]{:S(2)}, u32[]{:S(2)}) collective-permute-start(bf16[2,10,32,512]{3,2,1,0:T(8,128)(2,1)S(1)} %add_convert_fusion.1), channel_id=1, source_target_pairs={{8,16},{16,8},{10,18},{18,10},{12,20},{20,12},{14,22},{22,14},{9,1... | collective-permute-start | bytes 1966088 | tf_op jit(solution)/shard_map/ppermute | solution.py:37
